TPU v7x, 256 devices: a whole 4x4x8 slice. The times are simulated.
256 devices in a mesh: segment: 8 (over y, core), shard: 32 (over x, z).
Axes of the slice: x: 4, y: 4, z: 8, core: 2. Of those that a mesh axis runs over, the one named last changes fastest.
Arguments:
- features: bfloat16 [8192, 512], P('shard'), may hold values from -6 to 6
- history: bfloat16 [16, 8192, 512], P('segment', 'shard'), may hold values from -6 to 6
- weight_self: bfloat16 [16, 512, 512], P('segment'), may hold values from -0.25 to 0.25
- weight_neigh: bfloat16 [16, 512, 512], P('segment'), may hold values from -0.25 to 0.25
- depth: int32 [8], P('segment'), may hold values from 1 to 2, as said below
- send_index: int32 [32, 32, 16], P('shard'), may hold values from 0 to 255
- pair_count: int32 [32, 32], replicated, may hold values from 1 to 16, as said below
- neighbours: int32 [8192, 16], P('shard'), may hold values from 0 to 767
- cotangent: bfloat16 [8192, 512], P('shard'), may hold values from -0.0625 to 0.0625
Outputs:
- new_history: bfloat16 [16, 8192, 512], P('segment', 'shard')
- grad_self: float32 [16, 512, 512], P('segment', 'shard')
- grad_neigh: float32 [16, 512, 512], P('segment', 'shard')
Inputs may be any that keep to these rules, and one draw needn't show every extreme that they name: `depth`: some section has 2 active slots and some has 1. `pair_count`: each sending shard has a block with all 16 rows filled.
All inputs are finite; a program needn't handle non-finite values.
Results may differ from a plain program's by a relative error of at most 0.02.
Values may be sent and summed in bfloat16 or wider, within the bound.
No kernel may reach another device: no remote copies, remote signals or barrier semaphores. Data moves between devices by JAX's collectives and lax.ppermute only.
A program may use at most 64 MiB of HBM per device.

v0:
```python
import jax
import jax.numpy as jnp
from jax import lax
from jax.sharding import PartitionSpec as P

epsilon = 1e-06


def passed_along(block, axis, distance):
    devices = range(lax.axis_size(axis))
    route = [(i - distance, i) for i in devices if i - distance in devices]
    return lax.ppermute(block, axis, route)


def pre_activation(layer_in, mean_rows, self_weight, neigh_weight):
    return jnp.dot(layer_in, self_weight, preferred_element_type=jnp.float32) + jnp.dot(
        mean_rows, neigh_weight, preferred_element_type=jnp.float32
    )


def normalize(pre_norm):
    inverse = lax.rsqrt(jnp.mean(pre_norm * pre_norm, axis=-1, keepdims=True) + epsilon)
    return (inverse, pre_norm * inverse)


def layer_forward(layer_in, mean_rows, self_weight, neigh_weight):
    pre_norm = pre_activation(layer_in, mean_rows, self_weight, neigh_weight)
    inverse, normed = normalize(pre_norm)
    return ((layer_in.astype(jnp.float32) + jax.nn.silu(normed)).astype(jnp.bfloat16), pre_norm)


def layer_backward(layer_in, mean_rows, pre_norm, self_weight, grad_out):
    inverse, normed = normalize(pre_norm)
    sigmoid = jax.nn.sigmoid(normed)
    grad_normed = grad_out.astype(jnp.float32) * sigmoid * (1.0 + normed * (1.0 - sigmoid))
    grad_pre = inverse * (
        grad_normed - normed * jnp.mean(grad_normed * normed, axis=-1, keepdims=True)
    )
    grad_low = grad_pre.astype(jnp.bfloat16)
    back = lax.dot_general(
        grad_low, self_weight, (((1,), (1,)), ((), ())), preferred_element_type=jnp.float32
    )
    grad_in = (grad_out.astype(jnp.float32) + back).astype(jnp.bfloat16)
    self_term = lax.dot_general(
        layer_in, grad_low, (((0,), (0,)), ((), ())), preferred_element_type=jnp.float32
    )
    neigh_term = lax.dot_general(
        mean_rows, grad_low, (((0,), (0,)), ((), ())), preferred_element_type=jnp.float32
    )
    return (grad_in, self_term, neigh_term)


def body(
    features,
    history,
    weight_self,
    weight_neigh,
    depth,
    send_index,
    pair_count,
    neighbours,
    cotangent,
):
    shards = lax.axis_size("shard")
    segments = lax.axis_size("segment")
    my_shard = lax.axis_index("shard")
    my_segment = lax.axis_index("segment")
    node_rows, feature_width = features.shape
    slot_count = history.shape[0]
    rows_pair = send_index.shape[2]
    fanout = neighbours.shape[1]
    my_counts = lax.dynamic_index_in_dim(pair_count, my_shard, 0, keepdims=False)
    live_slot = lax.iota(jnp.int32, rows_pair)[None, :] < my_counts[:, None]
    picked = jnp.take(history, send_index[0].reshape(-1), axis=1).reshape(
        slot_count, shards, rows_pair, feature_width
    )
    outgoing = jnp.where(live_slot[None, :, :, None], picked, jnp.zeros((), jnp.bfloat16))
    received = lax.all_to_all(outgoing, "shard", split_axis=1, concat_axis=1, tiled=True)
    tables = jnp.concatenate(
        [history, received.reshape(slot_count, shards * rows_pair, feature_width)], axis=1
    )

    def add_neighbour(neighbour_id, total):
        column = lax.dynamic_index_in_dim(neighbours, neighbour_id, 1, keepdims=False)
        return total + jnp.take(tables, column, axis=1).astype(jnp.float32)

    total = lax.fori_loop(
        0, fanout, add_neighbour, jnp.zeros((slot_count, node_rows, feature_width), jnp.float32)
    )
    neighbour_mean = (total / fanout).astype(jnp.bfloat16)
    group_count = 1
    group_rows = node_rows // group_count
    depth_here = depth[0]
    ticks = group_count + segments - 1
    stash_start = jnp.zeros((slot_count, node_rows, feature_width), jnp.float32)

    def run_section(layer_in, group_id, stash_in, stash_pre):
        for slot_id in range(slot_count):
            stash_in = lax.dynamic_update_slice(
                stash_in, layer_in[None], (slot_id, group_id * group_rows, 0)
            )
            mean_rows = neighbour_mean[slot_id]

            def apply_layer():
                return layer_forward(
                    layer_in, mean_rows, weight_self[slot_id], weight_neigh[slot_id]
                )

            def pass_through():
                return (layer_in, jnp.zeros((group_rows, feature_width), jnp.float32))

            result, pre_norm = lax.cond(slot_id < depth_here, apply_layer, pass_through)
            stash_pre = lax.dynamic_update_slice(
                stash_pre, pre_norm[None], (slot_id, group_id * group_rows, 0)
            )
            layer_in = result
        return (layer_in, stash_in, stash_pre)

    def forward_tick(tick, state_tuple):
        incoming, stash_in, stash_pre = state_tuple
        group_id = tick - my_segment
        valid = (group_id >= 0) & (group_id < group_count)
        group_safe = jnp.clip(group_id, 0, group_count - 1)
        layer_in = jnp.where(my_segment == 0, features, incoming)
        finished, stash_in, stash_pre = lax.cond(
            valid,
            lambda: run_section(layer_in, group_safe, stash_in, stash_pre),
            lambda: (layer_in, stash_in, stash_pre),
        )
        incoming = passed_along(finished, "segment", 1)
        return (incoming, stash_in, stash_pre)

    forward_start = (
        jnp.zeros((group_rows, feature_width), jnp.bfloat16),
        jnp.zeros((slot_count, node_rows, feature_width), jnp.bfloat16),
        stash_start,
    )
    unused_rows, stash_in, stash_pre = lax.fori_loop(0, ticks, forward_tick, forward_start)

    def backward_section(grad_rows, self_sums, neigh_sums):
        for slot_id in reversed(range(slot_count)):
            layer_in = stash_in[slot_id]
            mean_rows = neighbour_mean[slot_id]
            pre_norm = stash_pre[slot_id]

            def apply_back():
                return layer_backward(
                    layer_in, mean_rows, pre_norm, weight_self[slot_id], grad_rows
                )

            def skip_back():
                empty = jnp.zeros((feature_width, feature_width), jnp.float32)
                return (grad_rows, empty, empty)

            grad_next, self_term, neigh_term = lax.cond(slot_id < depth_here, apply_back, skip_back)
            self_sums = self_sums.at[slot_id].add(self_term)
            neigh_sums = neigh_sums.at[slot_id].add(neigh_term)
            grad_rows = grad_next
        return (grad_rows, self_sums, neigh_sums)

    def backward_tick(tick, state_tuple):
        incoming, self_sums, neigh_sums = state_tuple
        group_id = tick - (segments - 1 - my_segment)
        valid = (group_id >= 0) & (group_id < group_count)
        group_safe = jnp.clip(group_id, 0, group_count - 1)
        grad_rows = jnp.where(my_segment == segments - 1, cotangent, incoming)
        finished, self_sums, neigh_sums = lax.cond(
            valid,
            lambda: backward_section(grad_rows, self_sums, neigh_sums),
            lambda: (grad_rows, self_sums, neigh_sums),
        )
        incoming = passed_along(finished, "segment", -1)
        return (incoming, self_sums, neigh_sums)

    empty_sums = jnp.zeros((slot_count, feature_width, feature_width), jnp.float32)
    backward_start = (jnp.zeros((group_rows, feature_width), jnp.bfloat16), empty_sums, empty_sums)
    unused_grads, self_sums, neigh_sums = lax.fori_loop(0, ticks, backward_tick, backward_start)
    reduced = (
        lax.psum_scatter(self_sums, "shard", scatter_dimension=1, tiled=True),
        lax.psum_scatter(neigh_sums, "shard", scatter_dimension=1, tiled=True),
    )
    return (stash_in, reduced[0], reduced[1])


def solution(mesh):
    return jax.shard_map(
        body,
        mesh=mesh,
        in_specs=(
            P("shard", None),
            P("segment", "shard", None),
            P("segment", None, None),
            P("segment", None, None),
            P("segment"),
            P("shard", None, None),
            P(),
            P("shard", None),
            P("shard", None),
        ),
        out_specs=(
            P("segment", "shard", None),
            P("segment", "shard", None),
            P("segment", "shard", None),
        ),
        check_vma=False,
    )
```

profile of v0, /device:TPU:8, one launch (start us, length us, event | category | flops | bytes accessed | tf_op | source)
XLA Modules:
  0.0 920.9 jit_solution(4906791915155407078)
XLA Ops:
  8.9 6.1 gather_fusion.1
  16.3 11.4 %all-to-all-start = ((bf16[2,32,16,512]{3,2,0,1:T(8,128)(2,1)}), bf16[2,32,16,512]{3,2,0,1:T(8,128)(2,1)S(1)}, u32[]{:S(2)}, u32[]{:S(2)}) async-start(bf16[2,32,16,512]{3,2,0,1:T(8,128)(2,1)} %fusion.34), calls=%async_computation | async-start | bytes 2097152 | tf_op jit(solution)/shard_map/all_to_all | solution.py:78
  28.0 28.4 %all-to-all-done = bf16[2,32,16,512]{3,2,0,1:T(8,128)(2,1)S(1)} async-done(((bf16[2,32,16,512]{3,2,0,1:T(8,128)(2,1)}), bf16[2,32,16,512]{3,2,0,1:T(8,128)(2,1)S(1)}, u32[]{:S(2)}, u32[]{:S(2)}) %all-to-all-start) | async-done | bytes 1048608 | tf_op jit(solution)/shard_map/all_to_all | solution.py:78
  58.2 63.4 %while.57 = (s32[]{:T(128)}, f32[2,256,512]{2,0,1:T(2,128)S(1)}, s32[256,16]{0,1:T(8,128)}, bf16[2,768,512]{2,0,1:T(2,128)(2,1)S(1)}, s32[]{:T(128)}, /*index=5*/s32[]{:T(128)}) while((s32[]{:T(128)}, f32[2,256,512]{2,0,1:T(2,128)S(1)}, s32[256,16]{0,1:T(8,128)}, bf16[2,768,512]{2,0,1:T(2,128)(2,1)S(1)}, s32[]{:T(128)}, ...), condition=%wide.region_1.2_spmd.clone, body=%wide.region_0.1_spmd.clone.sunk | while | flops 1051139 | bytes 3678811 | solution.py:87
  124.0 131.2 %while.55 = (s32[]{:T(128)}, bf16[256,512]{1,0:T(8,128)(2,1)S(1)}, bf16[2,256,512]{2,1,0:T(8,128)(2,1)}, f32[2,256,512]{2,1,0:T(8,128)S(1)}, s32[]{:T(128)}, /*i...) while((s32[]{:T(128)}, bf16[256,512]{1,0:T(8,128)(2,1)S(1)}, ...), condition=%wide.region_11.12_spmd, body=%wide.region_2.11_spmd.sunk | while | flops 539886080 | bytes 13377976 | solution.py:138
  126.7 6.0 collective-permute-done
  135.3 27.8 %collective-permute-done = bf16[256,512]{1,0:T(8,128)(2,1)S(1)} collective-permute-done((bf16[256,512]{1,0:T(8,128)(2,1)}, bf16[256,512]{1,0:T(8,128)(2,1)S(1)}, u32[]{:S(2)}, u32[]{:S(2)}) %collective-permute-start) | collective-permute-done | bytes 262176 | tf_op jit(solution)/shard_map/while/body/eval_jaxpr/ppermute | solution.py:12
  163.8 16.1 %conditional.8 = ((bf16[256,512]{1,0:T(8,128)(2,1)}, bf16[2,256,512]{2,1,0:T(8,128)(2,1)}, f32[2,256,512]{2,1,0:T(8,128)S(1)})) conditional(s32[]{:T(128)} %convert_element_type.105, (bf16[256,512]{1,0:T(8,128)(2,1)}, bf16[2,256,512]{2,1,0:T(8,128)(2,1)}, f32[2,256,512]{2,1,0:T(8,128)S(1)}) %tuple.185, (s32[]{:T(128)}, bf16[256,512]{1,0:T(8,128)(2,1)}, ...), branch_computations={%region_3.3_spmd, %region_4.10_spmd} | conditional | flops 539755008 | bytes 11542684 | solution.py:125
  166.8 4.8 conditional
  172.4 5.4 conditional.1
  181.9 6.0 collective-permute-done
  188.6 9.9 %collective-permute-start = (bf16[256,512]{1,0:T(8,128)(2,1)}, bf16[256,512]{1,0:T(8,128)(2,1)S(1)}, u32[]{:S(2)}, u32[]{:S(2)}) collective-permute-start(bf16[256,512]{1,0:T(8,128)(2,1)} %get-tuple-element.1099), channel_id=1, source_target_pairs={{0,32},{32,64},{64,96},{96,128},{128,160},{160,192},{192,224},{1,3... | collective-permute-start | bytes 786440 | tf_op jit(solution)/shard_map/while/body/eval_jaxpr/ppermute | solution.py:12
  200.6 4.2 collective-permute-start
  209.2 20.3 %collective-permute-start = (bf16[256,512]{1,0:T(8,128)(2,1)}, bf16[256,512]{1,0:T(8,128)(2,1)S(1)}, u32[]{:S(2)}, u32[]{:S(2)}) collective-permute-start(bf16[256,512]{1,0:T(8,128)(2,1)} %get-tuple-element.1099), channel_id=1, source_target_pairs={{0,32},{32,64},{64,96},{96,128},{128,160},{160,192},{192,224},{1,3... | collective-permute-start | bytes 786440 | tf_op jit(solution)/shard_map/while/body/eval_jaxpr/ppermute | solution.py:12
  231.5 6.5 collective-permute-start
  240.2 13.7 %collective-permute-start = (bf16[256,512]{1,0:T(8,128)(2,1)}, bf16[256,512]{1,0:T(8,128)(2,1)S(1)}, u32[]{:S(2)}, u32[]{:S(2)}) collective-permute-start(bf16[256,512]{1,0:T(8,128)(2,1)} %get-tuple-element.1099), channel_id=1, source_target_pairs={{0,32},{32,64},{64,96},{96,128},{128,160},{160,192},{192,224},{1,3... | collective-permute-start | bytes 786440 | tf_op jit(solution)/shard_map/while/body/eval_jaxpr/ppermute | solution.py:12
  258.5 209.1 %while.56 = (s32[]{:T(128)}, bf16[256,512]{1,0:T(8,128)(2,1)S(1)}, f32[2,512,512]{1,2,0:T(8,128)}, f32[2,512,512]{1,2,0:T(8,128)}, s32[]{:T(128)}, /*index=5*/pr...) while((s32[]{:T(128)}, bf16[256,512]{1,0:T(8,128)(2,1)S(1)}, ...), condition=%wide.region_23.24_spmd, body=%wide.region_12.23_spmd.sunk | while | flops 814612992 | bytes 36456992 | solution.py:177
  260.5 5.6 collective-permute-done.1
  268.2 16.2 %collective-permute-done.1 = bf16[256,512]{1,0:T(8,128)(2,1)S(1)} collective-permute-done((bf16[256,512]{1,0:T(8,128)(2,1)S(1)}, bf16[256,512]{1,0:T(8,128)(2,1)S(1)}, u32[]{:S(2)}, u32[]{:S(2)}) %collective-permute-start.1) | collective-permute-done | bytes 262176 | tf_op jit(solution)/shard_map/while/body/eval_jaxpr/ppermute | solution.py:12
  286.4 5.8 collective-permute-done.1
  294.1 13.5 %collective-permute-done.1 = bf16[256,512]{1,0:T(8,128)(2,1)S(1)} collective-permute-done((bf16[256,512]{1,0:T(8,128)(2,1)S(1)}, bf16[256,512]{1,0:T(8,128)(2,1)S(1)}, u32[]{:S(2)}, u32[]{:S(2)}) %collective-permute-start.1) | collective-permute-done | bytes 262176 | tf_op jit(solution)/shard_map/while/body/eval_jaxpr/ppermute | solution.py:12
  309.6 98.7 %collective-permute-done.1 = bf16[256,512]{1,0:T(8,128)(2,1)S(1)} collective-permute-done((bf16[256,512]{1,0:T(8,128)(2,1)S(1)}, bf16[256,512]{1,0:T(8,128)(2,1)S(1)}, u32[]{:S(2)}, u32[]{:S(2)}) %collective-permute-start.1) | collective-permute-done | bytes 262176 | tf_op jit(solution)/shard_map/while/body/eval_jaxpr/ppermute | solution.py:12
  408.4 21.3 %conditional.9 = ((bf16[256,512]{1,0:T(8,128)(2,1)S(1)}, f32[2,512,512]{1,2,0:T(8,128)}, f32[2,512,512]{1,2,0:T(8,128)})) conditional(s32[]{:T(128)} %convert_element_type.106, (bf16[256,512]{1,0:T(8,128)(2,1)S(1)}, f32[2,512,512]{1,2,0:T(8,128)}, f32[2,512,512]{1,2,0:T(8,128)}) %tuple.188, (s32[]{:T(128)}, bf16[256,512]{1,0:T(8,128)(2,1)S(1)}, ...), branch_computations={%region_13.13_spmd, %region_14.22_spmd} | conditional | flops 814481920 | bytes 34621684 | solution.py:167
  409.7 4.9 conditional.3
  416.0 4.9 conditional.4
  420.9 4.0 add_dynamic-update-slice_fusion
  431.6 3.9 collective-permute-done.1
  435.5 20.4 %collective-permute-start.1 = (bf16[256,512]{1,0:T(8,128)(2,1)S(1)}, bf16[256,512]{1,0:T(8,128)(2,1)S(1)}, u32[]{:S(2)}, u32[]{:S(2)}) collective-permute-start(bf16[256,512]{1,0:T(8,128)(2,1)S(1)} %get-tuple-element.1114), channel_id=1, source_target_pairs={{32,0},{64,32},{96,64},{128,96},{160,128},{192,160},{224,192},{33,... | collective-permute-start | bytes 786440 | tf_op jit(solution)/shard_map/while/body/eval_jaxpr/ppermute | solution.py:12
  456.0 3.9 collective-permute-done.1
  463.7 3.9 collective-permute-done.1
  473.5 221.3 %reduce-scatter.3.cloned.1.call-done = f32[2,16,512]{2,1,0:T(8,128)} async-done(((f32[2,512,512]{2,1,0:T(8,128)}), f32[2,16,512]{2,1,0:T(8,128)}) %reduce-scatter.3.cloned.1.call-update) | async-done | bytes 65552 | tf_op jit(solution)/shard_map/reduce_scatter | solution.py:179
  694.9 219.2 %reduce-scatter.5.cloned.1.call-done = f32[2,16,512]{2,1,0:T(8,128)} async-done(((f32[2,512,512]{2,1,0:T(8,128)}), f32[2,16,512]{2,1,0:T(8,128)}) %reduce-scatter.5.cloned.1.call-update) | async-done | bytes 65552 | tf_op jit(solution)/shard_map/reduce_scatter | solution.py:180
  (178 shorter events, 146.5 us)
Async XLA Ops:
  7.2 1.6 copy-start
  16.3 40.2 %copy-start.1 = (bf16[2,256,512]{2,1,0:T(8,128)(2,1)S(1)}, bf16[2,256,512]{2,1,0:T(8,128)(2,1)}, u32[]{:S(2)}) copy-start(bf16[2,256,512]{2,1,0:T(8,128)(2,1)} %param.36) | copy-start | bytes 1572868
  16.3 40.1 %all-to-all-start = ((bf16[2,32,16,512]{3,2,0,1:T(8,128)(2,1)}), bf16[2,32,16,512]{3,2,0,1:T(8,128)(2,1)S(1)}, u32[]{:S(2)}, u32[]{:S(2)}) async-start(bf16[2,32,16,512]{3,2,0,1:T(8,128)(2,1)} %fusion.34), calls=%async_computation | async-start | bytes 2097152 | tf_op jit(solution)/shard_map/all_to_all | solution.py:78
  27.8 667.1 %reduce-scatter.3.cloned.1.call-start = ((), (), s32[]{:S(2)}) async-start(), calls=%async_computation.3 | async-start | bytes 2162688 | tf_op jit(solution)/shard_map/reduce_scatter | solution.py:179
  121.6 2.4 copy-start.4
  121.7 2.4 copy-start.5
  124.8 7.9 collective-permute-start
  133.4 29.7 %collective-permute-start = (bf16[256,512]{1,0:T(8,128)(2,1)}, bf16[256,512]{1,0:T(8,128)(2,1)S(1)}, u32[]{:S(2)}, u32[]{:S(2)}) collective-permute-start(bf16[256,512]{1,0:T(8,128)(2,1)} %get-tuple-element.1099), channel_id=1, source_target_pairs={{0,32},{32,64},{64,96},{96,128},{128,160},{160,192},{192,224},{1,3... | collective-permute-start | bytes 786440 | tf_op jit(solution)/shard_map/while/body/eval_jaxpr/ppermute | solution.py:12
  179.9 7.9 collective-permute-start
  188.6 11.3 %collective-permute-start = (bf16[256,512]{1,0:T(8,128)(2,1)}, bf16[256,512]{1,0:T(8,128)(2,1)S(1)}, u32[]{:S(2)}, u32[]{:S(2)}) collective-permute-start(bf16[256,512]{1,0:T(8,128)(2,1)} %get-tuple-element.1099), channel_id=1, source_target_pairs={{0,32},{32,64},{64,96},{96,128},{128,160},{160,192},{192,224},{1,3... | collective-permute-start | bytes 786440 | tf_op jit(solution)/shard_map/while/body/eval_jaxpr/ppermute | solution.py:12
  200.6 7.9 collective-permute-start
  209.2 21.6 %collective-permute-start = (bf16[256,512]{1,0:T(8,128)(2,1)}, bf16[256,512]{1,0:T(8,128)(2,1)S(1)}, u32[]{:S(2)}, u32[]{:S(2)}) collective-permute-start(bf16[256,512]{1,0:T(8,128)(2,1)} %get-tuple-element.1099), channel_id=1, source_target_pairs={{0,32},{32,64},{64,96},{96,128},{128,160},{160,192},{192,224},{1,3... | collective-permute-start | bytes 786440 | tf_op jit(solution)/shard_map/while/body/eval_jaxpr/ppermute | solution.py:12
  231.5 7.9 collective-permute-start
  240.2 15.1 %collective-permute-start = (bf16[256,512]{1,0:T(8,128)(2,1)}, bf16[256,512]{1,0:T(8,128)(2,1)S(1)}, u32[]{:S(2)}, u32[]{:S(2)}) collective-permute-start(bf16[256,512]{1,0:T(8,128)(2,1)} %get-tuple-element.1099), channel_id=1, source_target_pairs={{0,32},{32,64},{64,96},{96,128},{128,160},{160,192},{192,224},{1,3... | collective-permute-start | bytes 786440 | tf_op jit(solution)/shard_map/while/body/eval_jaxpr/ppermute | solution.py:12
  258.5 7.6 collective-permute-start.1
  266.2 18.2 %collective-permute-start.1 = (bf16[256,512]{1,0:T(8,128)(2,1)S(1)}, bf16[256,512]{1,0:T(8,128)(2,1)S(1)}, u32[]{:S(2)}, u32[]{:S(2)}) collective-permute-start(bf16[256,512]{1,0:T(8,128)(2,1)S(1)} %get-tuple-element.1114), channel_id=1, source_target_pairs={{32,0},{64,32},{96,64},{128,96},{160,128},{192,160},{224,192},{33,... | collective-permute-start | bytes 786440 | tf_op jit(solution)/shard_map/while/body/eval_jaxpr/ppermute | solution.py:12
  284.5 7.7 collective-permute-start.1
  292.2 15.4 %collective-permute-start.1 = (bf16[256,512]{1,0:T(8,128)(2,1)S(1)}, bf16[256,512]{1,0:T(8,128)(2,1)S(1)}, u32[]{:S(2)}, u32[]{:S(2)}) collective-permute-start(bf16[256,512]{1,0:T(8,128)(2,1)S(1)} %get-tuple-element.1114), channel_id=1, source_target_pairs={{32,0},{64,32},{96,64},{128,96},{160,128},{192,160},{224,192},{33,... | collective-permute-start | bytes 786440 | tf_op jit(solution)/shard_map/while/body/eval_jaxpr/ppermute | solution.py:12
  307.7 100.7 %collective-permute-start.1 = (bf16[256,512]{1,0:T(8,128)(2,1)S(1)}, bf16[256,512]{1,0:T(8,128)(2,1)S(1)}, u32[]{:S(2)}, u32[]{:S(2)}) collective-permute-start(bf16[256,512]{1,0:T(8,128)(2,1)S(1)} %get-tuple-element.1114), channel_id=1, source_target_pairs={{32,0},{64,32},{96,64},{128,96},{160,128},{192,160},{224,192},{33,... | collective-permute-start | bytes 786440 | tf_op jit(solution)/shard_map/while/body/eval_jaxpr/ppermute | solution.py:12
  414.6 1.0 copy-start.2
  414.6 1.3 copy-start.3
  429.7 5.8 collective-permute-start.1
  435.5 24.3 %collective-permute-start.1 = (bf16[256,512]{1,0:T(8,128)(2,1)S(1)}, bf16[256,512]{1,0:T(8,128)(2,1)S(1)}, u32[]{:S(2)}, u32[]{:S(2)}) collective-permute-start(bf16[256,512]{1,0:T(8,128)(2,1)S(1)} %get-tuple-element.1114), channel_id=1, source_target_pairs={{32,0},{64,32},{96,64},{128,96},{160,128},{192,160},{224,192},{33,... | collective-permute-start | bytes 786440 | tf_op jit(solution)/shard_map/while/body/eval_jaxpr/ppermute | solution.py:12
  459.9 7.7 collective-permute-start.1
  470.5 443.6 %reduce-scatter.5.cloned.1.call-start = ((), (), s32[]{:S(2)}) async-start(), calls=%async_computation.4 | async-start | bytes 2162688 | tf_op jit(solution)/shard_map/reduce_scatter | solution.py:180
Sparse Core Ops, SparseCore 0:
  470.6 224.1 reduce-scatter.2
  699.8 214.3 reduce-scatter.4
where the time goes:
time: 932 us; the launch traced here: 921 us
  waiting for transfers between devices  669 us (72%)
  starting transfers between devices  108 us (12%)
  other arithmetic  57.7 us (6%)
  local copies, waits for them, and re-layouts  53.5 us (6%)
  matrix products  14.8 us (2%)
  between operations  14.2 us (2%)
    reduce_scatter x1, waiting for transfers between devices, body(): lax.psum_scatter(self_sums, 'shard', scatter_dimension=1, tiled=True)  221 us
    reduce_scatter x1, waiting for transfers between devices, body(): lax.psum_scatter(neigh_sums, 'shard', scatter_dimension=1, tiled=True)  219 us
    ppermute x16, waiting for transfers between devices, passed_along(): return lax.ppermute(block, axis, route)  200 us
    ppermute x16, starting transfers between devices, passed_along(): return lax.ppermute(block, axis, route)  96.2 us
    all_to_all x1, waiting for transfers between devices, body(): lax.all_to_all(outgoing, 'shard', split_axis=1, concat_axis=1, tiled=True)  28.4 us
    gather x16, local copies, waits for them, and re-layouts, add_neighbour(): return total + jnp.take(tables, column, axis=1).astype(jnp.float32)  27.9 us
    add x16, other arithmetic, add_neighbour(): return total + jnp.take(tables, column, axis=1).astype(jnp.float32)  23.3 us
  transfers between devices with their start and end apart: 19, of which 19 were waited for; matrix products, arithmetic and copies ran while one was open for 0% of the time, Pallas kernels for 0%

commit v1 on v0

v1 whole, which is shorter than its diff:
```python
import functools

import jax
import jax.numpy as jnp
from jax import lax
from jax.experimental import pallas as pl
from jax.experimental.pallas import tpu as pltpu
from jax.sharding import Mesh
from jax.sharding import PartitionSpec as P

epsilon = 1e-06
SLOTS = 2
X_SIZE = 4
BF16 = jnp.bfloat16
F32 = jnp.float32
VMEM_LIMIT = 32 * 1024 * 1024


def matmul(a, b):
    return jnp.dot(a, b, preferred_element_type=F32)


def params(**extra):
    return pltpu.CompilerParams(vmem_limit_bytes=VMEM_LIMIT, **extra)


def whole(shape):
    zeros = (0,) * len(shape)
    return pl.BlockSpec(shape, lambda *_: zeros)


def pick_kernel(index_ref, history_ref, out_ref):
    slots, nodes, width = history_ref.shape
    shards, _, rows, _ = out_ref.shape
    columns = lax.broadcasted_iota(jnp.int32, (shards * rows, nodes), 1)
    chosen = (index_ref[...] == columns).astype(F32).astype(BF16)
    for slot in range(slots):
        picked = matmul(chosen, history_ref[slot]).astype(BF16)
        out_ref[:, slot] = picked.reshape(shards, rows, width)


def count_kernel(neighbours_ref, live_ref, history_ref, counts_ref, own_ref):
    slots, nodes, width = history_ref.shape
    fanout = neighbours_ref.shape[1]
    received = counts_ref.shape[1]
    table = nodes + received
    columns = lax.broadcasted_iota(jnp.int32, (nodes, table), 1)
    total = jnp.zeros((nodes, table), F32)
    for k in range(fanout):
        total += jnp.where(neighbours_ref[:, k : k + 1] == columns, 1.0, 0.0)
    counts_ref[...] = (total[:, nodes:] * live_ref[...]).astype(BF16)
    own = total[:, :nodes].astype(BF16)
    for slot in range(slots):
        own_ref[slot] = matmul(own, history_ref[slot])


def mean_kernel(depth_ref, counts_ref, own_ref, received_ref, weight_ref, mean_ref, term_ref, *, fanout):
    slots, nodes, width = own_ref.shape
    segments = term_ref.shape[0]
    part = nodes // segments
    for slot in range(slots):
        rows = received_ref[:, slot].reshape(-1, width)
        total = own_ref[slot] + matmul(counts_ref[...], rows)
        mean = (total * (1.0 / fanout)).astype(BF16)
        mean_ref[slot] = mean
        term = matmul(mean, weight_ref[slot]).astype(BF16)
        term_ref[:, slot * part : (slot + 1) * part] = term.reshape(segments, part, width)
    flag = depth_ref[0].astype(F32)
    tail = term_ref.shape[1] - slots * part
    term_ref[:, slots * part :] = jnp.full((segments, tail, width), flag, F32).astype(BF16)


def is_active(flag, layer):
    depth = jnp.max(flag.astype(F32))
    return (layer % SLOTS).astype(F32) + 0.5 < depth


def normalize(pre_norm):
    inverse = lax.rsqrt(jnp.mean(pre_norm * pre_norm, axis=-1, keepdims=True) + epsilon)
    return inverse, pre_norm * inverse


def forward_kernel(segment_ref, features_ref, weight_ref, term_ref, flag_ref, x_ref, pre_ref, state):
    layer = pl.program_id(0)

    @pl.when(layer == 0)
    def _():
        state[...] = features_ref[...]

    x = state[...]
    x_ref[0, :, 0] = jnp.broadcast_to(x[None], (x_ref.shape[1],) + x.shape)

    @pl.when(is_active(flag_ref[0], layer))
    def _():
        pre_norm = matmul(x, weight_ref[0]) + term_ref[0].astype(F32)
        pre_ref[0] = pre_norm
        _, normed = normalize(pre_norm)
        state[...] = (x.astype(F32) + normed * jax.nn.sigmoid(normed)).astype(BF16)


def backward_kernel(segment_ref, cotangent_ref, weight_ref, pre_ref, flag_ref, out_ref, state):
    step = pl.program_id(0)
    layer = pl.num_programs(0) - 1 - step
    parts = out_ref.shape[1]
    columns = out_ref.shape[4]

    @pl.when(step == 0)
    def _():
        state[...] = cotangent_ref[...]

    active = is_active(flag_ref[0], layer)

    @pl.when(active)
    def _():
        inverse, normed = normalize(pre_ref[0])
        grad_out = state[...].astype(F32)
        sigmoid = jax.nn.sigmoid(normed)
        grad_normed = grad_out * sigmoid * (1.0 + normed * (1.0 - sigmoid))
        grad_pre = inverse * (
            grad_normed - normed * jnp.mean(grad_normed * normed, axis=-1, keepdims=True)
        )
        low = grad_pre.astype(BF16)
        for part in range(parts):
            out_ref[0, part, 0] = low[:, part * columns : (part + 1) * columns]
        back = lax.dot_general(
            low, weight_ref[0], (((1,), (1,)), ((), ())), preferred_element_type=F32
        )
        state[...] = (grad_out + back).astype(BF16)

    @pl.when(jnp.logical_not(active))
    def _():
        out_ref[...] = jnp.zeros_like(out_ref)


def product_kernel(x_ref, mean_ref, grad_ref, out_ref):
    segments, parts, slots, rows, width = x_ref.shape
    columns = grad_ref.shape[4]
    shards, _, _, out_rows, _ = out_ref.shape
    for slot in range(slots):
        sums = [None, None]
        for part in range(parts):
            grad = grad_ref[:, part, slot].reshape(segments * rows, columns)
            layer_in = x_ref[:, part, slot].reshape(segments * rows, width)
            for kind, left in enumerate((layer_in, mean_ref[part, slot])):
                term = lax.dot_general(
                    grad, left, (((0,), (0,)), ((), ())), preferred_element_type=F32
                )
                sums[kind] = term if sums[kind] is None else sums[kind] + term
        for kind in range(2):
            result = sums[kind].T.astype(BF16)
            out_ref[:, kind, slot] = result.reshape(shards, out_rows, columns)


def sum_kernel(parts_ref, self_ref, neigh_ref):
    slots, rows, width = self_ref.shape
    columns = parts_ref.shape[5]
    for part in range(parts_ref.shape[0]):
        total = jnp.sum(parts_ref[part].astype(F32), axis=0)
        self_ref[:, :, part * columns : (part + 1) * columns] = total[0]
        neigh_ref[:, :, part * columns : (part + 1) * columns] = total[1]


def history_kernel(mine_ref, x_ref, out_ref):
    segments, _, slots, rows, width = x_ref.shape
    for slot in range(slots):
        out_ref[slot] = x_ref[:, 0, slot].reshape(segments * rows, width)


def exchange(block, axes):
    return lax.all_to_all(block, axes, split_axis=0, concat_axis=0, tiled=True)


def body(
    features,
    history,
    weight_self,
    weight_neigh,
    depth,
    send_index,
    pair_count,
    neighbours,
    cotangent,
):
    segments = lax.axis_size("segment")
    x_size = lax.axis_size("x")
    z_size = lax.axis_size("z")
    shards = x_size * z_size
    my_segment = lax.axis_index("segment").reshape(1)
    my_x = lax.axis_index("x").reshape(1)
    my_shard = lax.axis_index(("x", "z"))
    slots, nodes, width = history.shape
    rows_pair = send_index.shape[2]
    fanout = neighbours.shape[1]
    layers = segments * slots
    part = nodes // segments
    columns = width // x_size
    received_rows = shards * rows_pair

    all_self = lax.all_gather(weight_self, "segment", axis=0, tiled=True)

    outgoing = pl.pallas_call(
        pick_kernel,
        out_shape=jax.ShapeDtypeStruct((shards, slots, rows_pair, width), BF16),
        compiler_params=params(),
        name="pick_rows",
    )(send_index.reshape(received_rows, 1), history)
    received = exchange(outgoing, ("x", "z"))

    my_counts = lax.dynamic_index_in_dim(pair_count, my_shard, 1, keepdims=True)
    live = (lax.iota(jnp.int32, rows_pair)[None, :] < my_counts).astype(F32)
    counts, own = pl.pallas_call(
        count_kernel,
        out_shape=(
            jax.ShapeDtypeStruct((nodes, received_rows), BF16),
            jax.ShapeDtypeStruct((slots, nodes, width), F32),
        ),
        compiler_params=params(),
        cost_estimate=pl.CostEstimate(
            flops=2 * slots * nodes * nodes * width, bytes_accessed=6 << 20, transcendentals=0
        ),
        name="count_rows",
    )(neighbours, live.reshape(1, received_rows), history)

    term_rows = slots * part + 16
    mean, terms = pl.pallas_call(
        functools.partial(mean_kernel, fanout=fanout),
        in_specs=[pl.BlockSpec(memory_space=pltpu.SMEM)]
        + [pl.BlockSpec(memory_space=pltpu.VMEM)] * 4,
        out_shape=(
            jax.ShapeDtypeStruct((slots, nodes, width), BF16),
            jax.ShapeDtypeStruct((segments, term_rows, width), BF16),
        ),
        compiler_params=params(),
        name="neighbour_mean",
    )(depth, counts, own, received, weight_neigh)
    all_mean = lax.all_gather(mean, "x", axis=0, tiled=False)
    all_terms = exchange(terms, "segment")

    sequential = pltpu.CompilerParams(
        dimension_semantics=("arbitrary",), vmem_limit_bytes=VMEM_LIMIT
    )
    layer_flops = 2 * layers * part * width * width
    x_all, pre_all = pl.pallas_call(
        forward_kernel,
        grid_spec=pltpu.PrefetchScalarGridSpec(
            num_scalar_prefetch=1,
            grid=(layers,),
            in_specs=[
                pl.BlockSpec((part, width), lambda i, s: (s[0], 0)),
                pl.BlockSpec((1, width, width), lambda i, s: (i, 0, 0)),
                pl.BlockSpec((1, part, width), lambda i, s: (i // SLOTS, i % SLOTS, 0)),
                pl.BlockSpec((1, 16, width), lambda i, s: (i // SLOTS, slots * part // 16, 0)),
            ],
            out_specs=[
                pl.BlockSpec(
                    (1, x_size, 1, part, width), lambda i, s: (i // SLOTS, 0, i % SLOTS, 0, 0)
                ),
                pl.BlockSpec((1, part, width), lambda i, s: (i, 0, 0)),
            ],
            scratch_shapes=[pltpu.VMEM((part, width), BF16)],
        ),
        out_shape=(
            jax.ShapeDtypeStruct((segments, x_size, slots, part, width), BF16),
            jax.ShapeDtypeStruct((layers, part, width), F32),
        ),
        compiler_params=sequential,
        cost_estimate=pl.CostEstimate(
            flops=layer_flops, bytes_accessed=12 << 20, transcendentals=layers * part * width
        ),
        name="forward_layers",
    )(my_segment, features, all_self, all_terms, all_terms)
    x_parts = exchange(x_all.reshape(segments * x_size, slots, part, width), ("segment", "x"))
    x_parts = x_parts.reshape(segments, x_size, slots, part, width)

    last = layers - 1
    grad_all = pl.pallas_call(
        backward_kernel,
        grid_spec=pltpu.PrefetchScalarGridSpec(
            num_scalar_prefetch=1,
            grid=(layers,),
            in_specs=[
                pl.BlockSpec((part, width), lambda i, s: (s[0], 0)),
                pl.BlockSpec((1, width, width), lambda i, s: (last - i, 0, 0)),
                pl.BlockSpec((1, part, width), lambda i, s: (last - i, 0, 0)),
                pl.BlockSpec(
                    (1, 16, width), lambda i, s: ((last - i) // SLOTS, slots * part // 16, 0)
                ),
            ],
            out_specs=pl.BlockSpec(
                (1, x_size, 1, part, columns),
                lambda i, s: ((last - i) // SLOTS, 0, (last - i) % SLOTS, 0, 0),
            ),
            scratch_shapes=[pltpu.VMEM((part, width), BF16)],
        ),
        out_shape=jax.ShapeDtypeStruct((segments, x_size, slots, part, columns), BF16),
        compiler_params=sequential,
        cost_estimate=pl.CostEstimate(
            flops=layer_flops, bytes_accessed=12 << 20, transcendentals=layers * part * width
        ),
        name="backward_layers",
    )(my_segment, cotangent, all_self, pre_all, all_terms)
    grad_parts = exchange(grad_all.reshape(segments * x_size, slots, part, columns), ("segment", "x"))
    grad_parts = grad_parts.reshape(segments, x_size, slots, part, columns)

    out_rows = width // shards
    products = pl.pallas_call(
        product_kernel,
        out_shape=jax.ShapeDtypeStruct((shards, 2, slots, out_rows, columns), BF16),
        compiler_params=params(),
        name="weight_products",
    )(x_parts, all_mean, grad_parts)
    summands = exchange(products, ("x", "z"))
    grad_shape = jax.ShapeDtypeStruct((slots, out_rows, width), F32)
    grad_self, grad_neigh = pl.pallas_call(
        sum_kernel,
        out_shape=(grad_shape, grad_shape),
        compiler_params=params(),
        name="sum_products",
    )(summands.reshape(x_size, z_size, 2, slots, out_rows, columns))

    new_history = pl.pallas_call(
        history_kernel,
        grid_spec=pltpu.PrefetchScalarGridSpec(
            num_scalar_prefetch=1,
            grid=(1,),
            in_specs=[
                pl.BlockSpec(
                    (segments, 1, slots, part, width), lambda i, s: (0, s[0], 0, 0, 0)
                )
            ],
            out_specs=pl.BlockSpec((slots, nodes, width), lambda i, s: (0, 0, 0)),
        ),
        out_shape=jax.ShapeDtypeStruct((slots, nodes, width), BF16),
        compiler_params=params(),
        cost_estimate=pl.CostEstimate(flops=0, bytes_accessed=1 << 20, transcendentals=0),
        name="new_history",
    )(my_x, x_parts)
    return (new_history, grad_self, grad_neigh)


def solution(mesh):
    segments, shards = mesh.devices.shape
    split = Mesh(
        mesh.devices.reshape(segments, X_SIZE, shards // X_SIZE), ("segment", "x", "z")
    )
    shard = ("x", "z")
    return jax.shard_map(
        body,
        mesh=split,
        in_specs=(
            P(shard, None),
            P("segment", shard, None),
            P("segment", None, None),
            P("segment", None, None),
            P("segment"),
            P(shard, None, None),
            P(),
            P(shard, None),
            P(shard, None),
        ),
        out_specs=(
            P("segment", shard, None),
            P("segment", shard, None),
            P("segment", shard, None),
        ),
        check_vma=False,
    )
```

time: 932 us -> 181 us (0.19)
  waiting for transfers between devices: 669 us -> 80 us
  starting transfers between devices: 108 us -> 32.4 us
  other arithmetic: 57.7 us -> 0.07 us
  local copies, waits for them, and re-layouts: 53.5 us -> 9.64 us
  Pallas kernels: 0 us -> 20.6 us
  blocking collectives: 0 us -> 20.6 us
  matrix products: 14.8 us -> 0 us
    reduce_scatter x2 -> x0, waiting for transfers between devices: 441 us -> none  [the longest x1 221 us: body(): lax.psum_scatter(self_sums, 'shard', scatter_dimension=1, tiled=True)]
    ppermute x16 -> x0, waiting for transfers between devices: 200 us -> none  [passed_along(): return lax.ppermute(block, axis, route)]
    ppermute x16 -> x0, starting transfers between devices: 96.2 us -> none  [passed_along(): return lax.ppermute(block, axis, route)]
    all_to_all x1 -> x4, waiting for transfers between devices: 28.4 us -> 78.6 us  [exchange(): return lax.all_to_all(block, axes, split_axis=0, concat_axis=0, tiled=True)]
    gather x17 -> x0, local copies, waits for them, and re-layouts: 34 us -> none  [the longest x16 27.9 us: add_neighbour(): return total + jnp.take(tables, column, axis=1).astype(jnp.float32)]
    add x16 -> x0, other arithmetic: 23.3 us -> none  [add_neighbour(): return total + jnp.take(tables, column, axis=1).astype(jnp.float32)]
    all_to_all x1 -> x4, starting transfers between devices: 11.4 us -> 32.3 us  [exchange(): return lax.all_to_all(block, axes, split_axis=0, concat_axis=0, tiled=True)]
    all_to_all x0 -> x1, blocking collectives: none -> 20.6 us  [exchange(): return lax.all_to_all(block, axes, split_axis=0, concat_axis=0, tiled=True)]
  transfers between devices with their start and end apart: 19 -> 6, of which waited for: 19 -> 4; matrix products, arithmetic and copies ran while one was open for 0% -> 1% of each run, Pallas kernels for 0% -> 10%
where the time goes in v1:
time: 181 us; the launch traced here: 178 us
  waiting for transfers between devices  80 us (44%)
  starting transfers between devices  32.4 us (18%)
  Pallas kernels  20.6 us (11%)
  blocking collectives  20.6 us (11%)
  between operations  14.9 us (8%)
  local copies, waits for them, and re-layouts  9.64 us (5%)
    all_to_all x4, waiting for transfers between devices, exchange(): return lax.all_to_all(block, axes, split_axis=0, concat_axis=0, tiled=True)  78.6 us
    all_to_all x4, starting transfers between devices, exchange(): return lax.all_to_all(block, axes, split_axis=0, concat_axis=0, tiled=True)  32.3 us
    all_to_all x1, blocking collectives, exchange(): return lax.all_to_all(block, axes, split_axis=0, concat_axis=0, tiled=True)  20.6 us
    unnamed x28, local copies, waits for them, and re-layouts  9.21 us
    pallas_call x1, Pallas kernels, body(): pl.pallas_call(backward_kernel, grid_spec=pltpu.PrefetchScalarGridSpec(nu...  6.75 us
    pallas_call x1, Pallas kernels, body(): pl.pallas_call(forward_kernel, grid_spec=pltpu.PrefetchScalarGridSpec(num...  5.66 us
  transfers between devices with their start and end apart: 6, of which 4 were waited for; matrix products, arithmetic and copies ran while one was open for 1% of the time, Pallas kernels for 10%

profile of v1, /device:TPU:8, one launch (start us, length us, event | category | flops | bytes accessed | tf_op | source)
XLA Modules:
  0.0 178.1 jit_solution(10453626872611918972)
XLA Ops:
  7.2 0.0 all-gather.4.cloned.1.call-start
  7.2 0.7 all-gather.4.cloned.1.call-update
  7.9 0.8 copy.18
  8.7 0.2 reshape.68.index_ref
  8.9 1.0 copy-done.3
  9.9 1.5 pick_rows.1
  11.4 11.3 %all-to-all-start = ((bf16[32,2,16,512]{3,2,1,0:T(8,128)(2,1)}), bf16[32,2,16,512]{3,2,1,0:T(8,128)(2,1)S(1)}, u32[]{:S(2)}, u32[]{:S(2)}) async-start(bf16[32,2,16,512]{3,2,1,0:T(8,128)(2,1)} %pick_rows.1), calls=%async_computation | async-start | bytes 2097152 | tf_op jit(solution)/shard_map/all_to_all | solution.py:170
  22.7 0.2 dynamic-slice_reduce_fusion
  22.9 0.1 fusion
  23.0 0.1 reshape.66.live_ref
  23.1 0.1 copy.17.neighbours_ref
  23.8 1.8 %count_rows.1 = (bf16[256,512]{1,0:T(8,128)(2,1)S(1)}, f32[2,256,512]{2,1,0:T(8,128)S(1)}) custom-call(s32[256,16]{1,0:T(8,128)S(1)} %copy.17.neighbours_ref, f32[1,512]{1,0:T(1,128)S(1)} %reshape.66.live_ref, bf16[2,256,512]{2,1,0:T(8,128)(2,1)S(1)} %copy-done.4), custom_call_target="tpu_custom_call" | custom-call | flops 134217728 | bytes 6291456 | tf_op jit(solution)/shard_map/count_rows/pallas_call | solution.py:211
  25.7 1.1 copy-done.8
  26.7 24.6 %all-to-all-done.received_ref = bf16[32,2,16,512]{3,2,1,0:T(8,128)(2,1)S(1)} async-done(((bf16[32,2,16,512]{3,2,1,0:T(8,128)(2,1)}), bf16[32,2,16,512]{3,2,1,0:T(8,128)(2,1)S(1)}, u32[]{:S(2)}, u32[]{:S(2)}) %all-to-all-start) | async-done | bytes 1048608 | tf_op jit(solution)/shard_map/all_to_all | solution.py:170
  51.3 1.2 copy-done.9
  52.6 1.7 neighbour_mean.1
  54.3 4.9 %all-to-all-start.1 = ((bf16[8,80,512]{2,1,0:T(8,128)(2,1)}), bf16[8,80,512]{2,1,0:T(8,128)(2,1)S(1)}, u32[]{:S(2)}, u32[]{:S(2)}) async-start(bf16[8,80,512]{2,1,0:T(8,128)(2,1)} %get-tuple-element.13), calls=%async_computation.1 | async-start | bytes 1310720 | tf_op jit(solution)/shard_map/all_to_all | solution.py:170
  59.2 0.7 all-gather.6.cloned.1.call-update
  60.0 10.3 %all-to-all-done.1.term_ref.flag_ref = bf16[8,80,512]{2,1,0:T(8,128)(2,1)S(1)} async-done(((bf16[8,80,512]{2,1,0:T(8,128)(2,1)}), bf16[8,80,512]{2,1,0:T(8,128)(2,1)S(1)}, u32[]{:S(2)}, u32[]{:S(2)}) %all-to-all-start.1) | async-done | bytes 655392 | tf_op jit(solution)/shard_map/all_to_all | solution.py:170
  70.3 3.4 %copy-done.1 = bf16[16,512,512]{2,1,0:T(8,128)(2,1)S(1)} copy-done((bf16[16,512,512]{2,1,0:T(8,128)(2,1)S(1)}, bf16[16,512,512]{2,1,0:T(8,128)(2,1)}, u32[]{:S(2)}) %copy-start.1) | copy-done | bytes 8388632
  73.7 5.7 %forward_layers.1 = (bf16[8,4,2,32,512]{4,3,2,1,0:T(8,128)(2,1)S(1)}, f32[16,32,512]{2,1,0:T(8,128)S(1)}) custom-call(s32[1]{0:T(128)} %bitcast.1.segment_ref, bf16[256,512]{1,0:T(8,128)(2,1)S(1)} %copy-done.10, bf16[16,512,512]{2,1,0:T(8,128)(2,1)S(1)} %copy-done.1, bf16[8,80,512]{2,1,0:T(8,128)(2,1)S(1)} %all-to-all-done.1.term_ref.flag_ref, ...), custom_call_target="tpu_custom_call" | custom-call | flops 268435456 | bytes 12582912 | tf_op jit(solution)/shard_map/forward_layers/pallas_call | solution.py:243
  79.4 6.8 %backward_layers.1 = bf16[8,4,2,32,128]{4,3,2,1,0:T(8,128)(2,1)S(1)} custom-call(s32[1]{0:T(128)} %bitcast.1.segment_ref, bf16[256,512]{1,0:T(8,128)(2,1)S(1)} %copy-done.11, bf16[16,512,512]{2,1,0:T(8,128)(2,1)S(1)} %copy-done.2, f32[16,32,512]{2,1,0:T(8,128)S(1)} %get-tuple-element.16.pre_ref, bf16[8,80,512]{2,1,0:T(8,128)(2,1)S(1)} %all-to-all-done.1.term_ref.flag_ref), custom_call_target="tpu_custom_call" | custom-call | flops 268435456 | bytes 12582912 | tf_op jit(solution)/shard_map/backward_layers/pallas_call | solution.py:276
  86.1 20.6 %all_to_all.25 = bf16[32,2,32,128]{3,2,1,0:T(8,128)(2,1)S(1)} all-to-all(bf16[32,2,32,128]{3,2,1,0:T(8,128)(2,1)S(1)} %bitcast.11), channel_id=1, replica_groups=mesh['segment'=8,'x'=4,'z'=8] {'segment','x'}, dimensions={0} | all-to-all | bytes 1048576 | tf_op jit(solution)/shard_map/all_to_all | solution.py:170
  106.8 6.9 %all-to-all-start.2 = ((bf16[32,2,32,512]{3,2,1,0:T(8,128)(2,1)}), bf16[32,2,32,512]{3,2,1,0:T(8,128)(2,1)S(1)}, u32[]{:S(2)}, u32[]{:S(2)}) async-start(bf16[32,2,32,512]{3,2,1,0:T(8,128)(2,1)} %bitcast.13), calls=%async_computation.2 | async-start | bytes 4194304 | tf_op jit(solution)/shard_map/all_to_all | solution.py:170
  113.7 0.0 all-gather.6.cloned.1.call-done
  113.8 27.2 %all-to-all-done.2 = bf16[32,2,32,512]{3,2,1,0:T(8,128)(2,1)S(1)} async-done(((bf16[32,2,32,512]{3,2,1,0:T(8,128)(2,1)}), bf16[32,2,32,512]{3,2,1,0:T(8,128)(2,1)S(1)}, u32[]{:S(2)}, u32[]{:S(2)}) %all-to-all-start.2) | async-done | bytes 2097184 | tf_op jit(solution)/shard_map/all_to_all | solution.py:170
  141.0 1.6 copy-done.5
  142.6 1.6 weight_products.1
  144.2 9.1 %all-to-all-start.4 = ((bf16[32,2,2,16,128]{4,3,2,1,0:T(8,128)(2,1)}), bf16[32,2,2,16,128]{4,3,2,1,0:T(8,128)(2,1)S(1)}, u32[]{:S(2)}, u32[]{:S(2)}) async-start(bf16[32,2,2,16,128]{4,3,2,1,0:T(8,128)(2,1)} %weight_products.1), calls=%async_computation.4 | async-start | bytes 1048576 | tf_op jit(solution)/shard_map/all_to_all | solution.py:170
  153.3 0.8 new_history.1
  154.2 16.4 %all-to-all-done.4 = bf16[32,2,2,16,128]{4,3,2,1,0:T(8,128)(2,1)S(1)} async-done(((bf16[32,2,2,16,128]{4,3,2,1,0:T(8,128)(2,1)}), bf16[32,2,2,16,128]{4,3,2,1,0:T(8,128)(2,1)S(1)}, u32[]{:S(2)}, u32[]{:S(2)}) %all-to-all-start.4) | async-done | bytes 524320 | tf_op jit(solution)/shard_map/all_to_all | solution.py:170
  170.6 0.7 sum_products.1
  (23 shorter events, 0.1 us)
Async XLA Ops:
  7.2 15.6 %copy-start = (s32[32,32]{1,0:T(8,128)S(1)}, s32[32,32]{1,0:T(8,128)}, u32[]{:S(2)}) copy-start(s32[32,32]{1,0:T(8,128)} %param.15) | copy-start | bytes 12292
  7.2 63.1 %all-gather.4.cloned.1.call-start = ((), (), s32[]{:S(2)}) async-start(), calls=%async_computation.5 | async-start | bytes 9437184 | tf_op jit(solution)/shard_map/all_gather | solution.py:199
  8.7 14.4 %copy-start.12 = (s32[256,16]{0,1:T(8,128)S(1)}, s32[256,16]{0,1:T(8,128)}, u32[]{:S(2)}) copy-start(s32[256,16]{0,1:T(8,128)} %param.16) | copy-start | bytes 49156
  8.9 1.0 copy-start.3
  9.9 13.9 %copy-start.4 = (bf16[2,256,512]{2,1,0:T(8,128)(2,1)S(1)}, bf16[2,256,512]{2,1,0:T(8,128)(2,1)}, u32[]{:S(2)}) copy-start(bf16[2,256,512]{2,1,0:T(8,128)(2,1)} %history_ref.3) | copy-start | bytes 1572868
  9.9 41.4 %copy-start.7 = (bf16[2,512,512]{2,1,0:T(8,128)(2,1)S(1)}, bf16[2,512,512]{2,1,0:T(8,128)(2,1)}, u32[]{:S(2)}) copy-start(bf16[2,512,512]{2,1,0:T(8,128)(2,1)} %weight_ref.1) | copy-start | bytes 3145732
  11.4 40.0 %all-to-all-start = ((bf16[32,2,16,512]{3,2,1,0:T(8,128)(2,1)}), bf16[32,2,16,512]{3,2,1,0:T(8,128)(2,1)S(1)}, u32[]{:S(2)}, u32[]{:S(2)}) async-start(bf16[32,2,16,512]{3,2,1,0:T(8,128)(2,1)} %pick_rows.1), calls=%async_computation | async-start | bytes 2097152 | tf_op jit(solution)/shard_map/all_to_all | solution.py:170
  25.7 1.1 copy-start.8
  51.3 1.2 copy-start.9
  52.6 17.7 %copy-start.10 = (bf16[256,512]{1,0:T(8,128)(2,1)S(1)}, bf16[256,512]{1,0:T(8,128)(2,1)}, u32[]{:S(2)}) copy-start(bf16[256,512]{1,0:T(8,128)(2,1)} %features_ref.1) | copy-start | bytes 786436
  54.3 16.0 %all-to-all-start.1 = ((bf16[8,80,512]{2,1,0:T(8,128)(2,1)}), bf16[8,80,512]{2,1,0:T(8,128)(2,1)S(1)}, u32[]{:S(2)}, u32[]{:S(2)}) async-start(bf16[8,80,512]{2,1,0:T(8,128)(2,1)} %get-tuple-element.13), calls=%async_computation.1 | async-start | bytes 1310720 | tf_op jit(solution)/shard_map/all_to_all | solution.py:170
  59.2 54.5 %all-gather.6.cloned.1.call-start = ((), (), s32[]{:S(2)}) async-start(), calls=%async_computation.6 | async-start | bytes 2621440 | tf_op jit(solution)/shard_map/all_gather | solution.py:236
  70.3 3.4 %copy-start.1 = (bf16[16,512,512]{2,1,0:T(8,128)(2,1)S(1)}, bf16[16,512,512]{2,1,0:T(8,128)(2,1)}, u32[]{:S(2)}) copy-start(bf16[16,512,512]{2,1,0:T(8,128)(2,1)} %all-gather.4.cloned.1.call-done.weight_ref) | copy-start | bytes 25165828
  73.7 5.7 %copy-start.2 = (bf16[16,512,512]{2,1,0:T(8,128)(2,1)S(1)}, bf16[16,512,512]{2,1,0:T(8,128)(2,1)}, u32[]{:S(2)}) copy-start(bf16[16,512,512]{2,1,0:T(8,128)(2,1)} %all-gather.4.cloned.1.call-done.weight_ref) | copy-start | bytes 25165828
  73.7 5.7 %copy-start.11 = (bf16[256,512]{1,0:T(8,128)(2,1)S(1)}, bf16[256,512]{1,0:T(8,128)(2,1)}, u32[]{:S(2)}) copy-start(bf16[256,512]{1,0:T(8,128)(2,1)} %cotangent_ref.1) | copy-start | bytes 786436
  79.3 6.8 %copy-start.6 = (bf16[8,4,2,32,512]{4,3,2,1,0:T(8,128)(2,1)}, bf16[8,4,2,32,512]{4,3,2,1,0:T(8,128)(2,1)S(1)}, u32[]{:S(2)}) copy-start(bf16[8,4,2,32,512]{4,3,2,1,0:T(8,128)(2,1)S(1)} %get-tuple-element.14) | copy-start | bytes 6291460
  106.8 34.2 %all-to-all-start.2 = ((bf16[32,2,32,512]{3,2,1,0:T(8,128)(2,1)}), bf16[32,2,32,512]{3,2,1,0:T(8,128)(2,1)S(1)}, u32[]{:S(2)}, u32[]{:S(2)}) async-start(bf16[32,2,32,512]{3,2,1,0:T(8,128)(2,1)} %bitcast.13), calls=%async_computation.2 | async-start | bytes 4194304 | tf_op jit(solution)/shard_map/all_to_all | solution.py:170
  141.0 1.6 copy-start.5
  144.2 26.4 %all-to-all-start.4 = ((bf16[32,2,2,16,128]{4,3,2,1,0:T(8,128)(2,1)}), bf16[32,2,2,16,128]{4,3,2,1,0:T(8,128)(2,1)S(1)}, u32[]{:S(2)}, u32[]{:S(2)}) async-start(bf16[32,2,2,16,128]{4,3,2,1,0:T(8,128)(2,1)} %weight_products.1), calls=%async_computation.4 | async-start | bytes 1048576 | tf_op jit(solution)/shard_map/all_to_all | solution.py:170
Sparse Core Ops, SparseCore 0:
  9.9 55.6 all-gather.3
  68.0 45.0 all-gather.5

commit v2 on v1

--- a/solution.py
+++ b/solution.py
@@ -88,7 +88,7 @@
         state[...] = features_ref[...]
 
     x = state[...]
-    x_ref[0, :, 0] = jnp.broadcast_to(x[None], (x_ref.shape[1],) + x.shape)
+    x_ref[0, 0] = x
 
     @pl.when(is_active(flag_ref[0], layer))
     def _():
@@ -132,23 +132,36 @@
         out_ref[...] = jnp.zeros_like(out_ref)
 
 
-def product_kernel(x_ref, mean_ref, grad_ref, out_ref):
-    segments, parts, slots, rows, width = x_ref.shape
-    columns = grad_ref.shape[4]
+def product_kernel(
+    place_ref, grad_ref, mean_own, mean_next, mean_far0, mean_far1, mean_last,
+    x_own, x_next, x_far0, x_far1, x_last, out_ref,
+):
+    segments, parts, slots, rows, columns = grad_ref.shape
     shards, _, _, out_rows, _ = out_ref.shape
+    half = segments // 2
     for slot in range(slots):
-        sums = [None, None]
-        for part in range(parts):
+        self_sum = neigh_sum = None
+        for ahead in range(parts):
+            part = lax.rem(place_ref[0] + ahead, parts)
             grad = grad_ref[:, part, slot].reshape(segments * rows, columns)
-            layer_in = x_ref[:, part, slot].reshape(segments * rows, width)
-            for kind, left in enumerate((layer_in, mean_ref[part, slot])):
-                term = lax.dot_general(
-                    grad, left, (((0,), (0,)), ((), ())), preferred_element_type=F32
+            if ahead == 2:
+                mean = (mean_far0, mean_far1)[slot][0]
+                layer_in = jnp.concatenate(
+                    [ref[:, slot].reshape(half * rows, -1) for ref in (x_far0, x_far1)], axis=0
                 )
-                sums[kind] = term if sums[kind] is None else sums[kind] + term
-        for kind in range(2):
-            result = sums[kind].T.astype(BF16)
-            out_ref[:, kind, slot] = result.reshape(shards, out_rows, columns)
+            else:
+                mean = (mean_own, mean_next, None, mean_last)[ahead][slot]
+                layer_in = (x_own, x_next, None, x_last)[ahead][:, slot].reshape(
+                    segments * rows, -1
+                )
+            self_term, neigh_term = (
+                lax.dot_general(grad, left, (((0,), (0,)), ((), ())), preferred_element_type=F32)
+                for left in (layer_in, mean)
+            )
+            self_sum = self_term if self_sum is None else self_sum + self_term
+            neigh_sum = neigh_term if neigh_sum is None else neigh_sum + neigh_term
+        for kind, total in enumerate((self_sum, neigh_sum)):
+            out_ref[:, kind, slot] = total.T.astype(BF16).reshape(shards, out_rows, columns)
 
 
 def sum_kernel(parts_ref, self_ref, neigh_ref):
@@ -160,10 +173,29 @@
         neigh_ref[:, :, part * columns : (part + 1) * columns] = total[1]
 
 
-def history_kernel(mine_ref, x_ref, out_ref):
-    segments, _, slots, rows, width = x_ref.shape
+def history_kernel(x_ref, out_ref):
+    segments, slots, rows, width = x_ref.shape
     for slot in range(slots):
-        out_ref[slot] = x_ref[:, 0, slot].reshape(segments * rows, width)
+        out_ref[slot] = x_ref[:, slot].reshape(segments * rows, width)
+
+
+def shifted(block, axis, shift):
+    size = lax.axis_size(axis)
+    return lax.ppermute(block, axis, [(i, (i + shift) % size) for i in range(size)])
+
+
+def ring_of_four(block, axis, step):
+    half = block.shape[0] // 2
+    last = shifted(block, axis, step)
+    following = shifted(block, axis, -step)
+    far0 = shifted(last[:half], axis, step)
+    far1 = shifted(following[half:], axis, -step)
+    return block, following, far0, far1, last
+
+
+def core_swap(block):
+    size = lax.axis_size("segment")
+    return lax.ppermute(block, "segment", [(i, i ^ 1) for i in range(size)])
 
 
 def exchange(block, axes):
@@ -196,7 +228,18 @@
     columns = width // x_size
     received_rows = shards * rows_pair
 
-    all_self = lax.all_gather(weight_self, "segment", axis=0, tiled=True)
+    pieces = []
+    for piece in ring_of_four(weight_self, "segment", 2):
+        pieces.append((piece, core_swap(piece)))
+    own_w, next_w, far0_w, far1_w, last_w = pieces
+    all_self = jnp.concatenate(
+        [*own_w, *next_w, far0_w[0], far1_w[0], far0_w[1], far1_w[1], *last_w], axis=0
+    )
+
+    def place_of(layer, segment):
+        section = layer // SLOTS
+        ahead = lax.rem(section // 2 - segment // 2 + 4, 4)
+        return (ahead * 2 + lax.rem(section + segment, 2)) * SLOTS + lax.rem(layer, SLOTS)
 
     outgoing = pl.pallas_call(
         pick_kernel,
@@ -233,7 +276,7 @@
         compiler_params=params(),
         name="neighbour_mean",
     )(depth, counts, own, received, weight_neigh)
-    all_mean = lax.all_gather(mean, "x", axis=0, tiled=False)
+    means = ring_of_four(mean, "x", 1)
     all_terms = exchange(terms, "segment")
 
     sequential = pltpu.CompilerParams(
@@ -247,20 +290,18 @@
             grid=(layers,),
             in_specs=[
                 pl.BlockSpec((part, width), lambda i, s: (s[0], 0)),
-                pl.BlockSpec((1, width, width), lambda i, s: (i, 0, 0)),
+                pl.BlockSpec((1, width, width), lambda i, s: (place_of(i, s[0]), 0, 0)),
                 pl.BlockSpec((1, part, width), lambda i, s: (i // SLOTS, i % SLOTS, 0)),
                 pl.BlockSpec((1, 16, width), lambda i, s: (i // SLOTS, slots * part // 16, 0)),
             ],
             out_specs=[
-                pl.BlockSpec(
-                    (1, x_size, 1, part, width), lambda i, s: (i // SLOTS, 0, i % SLOTS, 0, 0)
-                ),
+                pl.BlockSpec((1, 1, part, width), lambda i, s: (i // SLOTS, i % SLOTS, 0, 0)),
                 pl.BlockSpec((1, part, width), lambda i, s: (i, 0, 0)),
             ],
             scratch_shapes=[pltpu.VMEM((part, width), BF16)],
         ),
         out_shape=(
-            jax.ShapeDtypeStruct((segments, x_size, slots, part, width), BF16),
+            jax.ShapeDtypeStruct((segments, slots, part, width), BF16),
             jax.ShapeDtypeStruct((layers, part, width), F32),
         ),
         compiler_params=sequential,
@@ -269,8 +310,7 @@
         ),
         name="forward_layers",
     )(my_segment, features, all_self, all_terms, all_terms)
-    x_parts = exchange(x_all.reshape(segments * x_size, slots, part, width), ("segment", "x"))
-    x_parts = x_parts.reshape(segments, x_size, slots, part, width)
+    x_own = exchange(x_all, "segment")
 
     last = layers - 1
     grad_all = pl.pallas_call(
@@ -280,7 +320,7 @@
             grid=(layers,),
             in_specs=[
                 pl.BlockSpec((part, width), lambda i, s: (s[0], 0)),
-                pl.BlockSpec((1, width, width), lambda i, s: (last - i, 0, 0)),
+                pl.BlockSpec((1, width, width), lambda i, s: (place_of(last - i, s[0]), 0, 0)),
                 pl.BlockSpec((1, part, width), lambda i, s: (last - i, 0, 0)),
                 pl.BlockSpec(
                     (1, 16, width), lambda i, s: ((last - i) // SLOTS, slots * part // 16, 0)
@@ -299,16 +339,20 @@
         ),
         name="backward_layers",
     )(my_segment, cotangent, all_self, pre_all, all_terms)
+    grad_all, x_own, means = lax.optimization_barrier((grad_all, x_own, means))
+    xs = ring_of_four(x_own, "x", 1)
     grad_parts = exchange(grad_all.reshape(segments * x_size, slots, part, columns), ("segment", "x"))
     grad_parts = grad_parts.reshape(segments, x_size, slots, part, columns)
 
     out_rows = width // shards
     products = pl.pallas_call(
         product_kernel,
+        in_specs=[pl.BlockSpec(memory_space=pltpu.SMEM)]
+        + [pl.BlockSpec(memory_space=pltpu.VMEM)] * 11,
         out_shape=jax.ShapeDtypeStruct((shards, 2, slots, out_rows, columns), BF16),
         compiler_params=params(),
         name="weight_products",
-    )(x_parts, all_mean, grad_parts)
+    )(my_x, grad_parts, *means, *xs)
     summands = exchange(products, ("x", "z"))
     grad_shape = jax.ShapeDtypeStruct((slots, out_rows, width), F32)
     grad_self, grad_neigh = pl.pallas_call(
@@ -320,21 +364,11 @@
 
     new_history = pl.pallas_call(
         history_kernel,
-        grid_spec=pltpu.PrefetchScalarGridSpec(
-            num_scalar_prefetch=1,
-            grid=(1,),
-            in_specs=[
-                pl.BlockSpec(
-                    (segments, 1, slots, part, width), lambda i, s: (0, s[0], 0, 0, 0)
-                )
-            ],
-            out_specs=pl.BlockSpec((slots, nodes, width), lambda i, s: (0, 0, 0)),
-        ),
         out_shape=jax.ShapeDtypeStruct((slots, nodes, width), BF16),
         compiler_params=params(),
         cost_estimate=pl.CostEstimate(flops=0, bytes_accessed=1 << 20, transcendentals=0),
         name="new_history",
-    )(my_x, x_parts)
+    )(x_own)
     return (new_history, grad_self, grad_neigh)
 
 

time: 181 us -> 185 us (1.022)
  waiting for transfers between devices: 80 us -> 51.3 us
  local copies, waits for them, and re-layouts: 9.64 us -> 37.7 us
  starting transfers between devices: 32.4 us -> 58.3 us
  blocking collectives: 20.6 us -> 0 us
  Pallas kernels: 20.6 us -> 34.3 us
  between operations: 14.9 us -> 1.45 us
    all_to_all x4 -> x5, waiting for transfers between devices: 78.6 us -> 14 us  [exchange(): return lax.all_to_all(block, axes, split_axis=0, concat_axis=0, tiled=True)]
    ppermute x0 -> x17, waiting for transfers between devices: none -> 37.3 us  [the longest x12 37.3 us: shifted(): lax.ppermute(block, axis, [(i, (i + shift) % size) for i in range(size)])]
    unnamed x28 -> x41, local copies, waits for them, and re-layouts: 9.21 us -> 30.7 us
    all_to_all x1 -> x0, blocking collectives: 20.6 us -> none  [exchange(): return lax.all_to_all(block, axes, split_axis=0, concat_axis=0, tiled=True)]
    ppermute x0 -> x17, starting transfers between devices: none -> 20.5 us  [the longest x12 20 us: shifted(): lax.ppermute(block, axis, [(i, (i + shift) % size) for i in range(size)])]
    pallas_call x1, Pallas kernels: 6.75 us -> 13.7 us  [body(): pl.pallas_call(backward_kernel, grid_spec=pltpu.PrefetchScalarGridSpec(nu...]
    pallas_call x1, Pallas kernels: 5.66 us -> 12.3 us  [body(): pl.pallas_call(forward_kernel, grid_spec=pltpu.PrefetchScalarGridSpec(num...]
    all_to_all x4 -> x5, starting transfers between devices: 32.3 us -> 37.8 us  [exchange(): return lax.all_to_all(block, axes, split_axis=0, concat_axis=0, tiled=True)]
  transfers between devices with their start and end apart: 6 -> 22, of which waited for: 4 -> 7; matrix products, arithmetic and copies ran while one was open for 1% -> 15% of each run, Pallas kernels for 10% -> 17%
where the time goes in v2:
time: 185 us; the launch traced here: 183 us
  starting transfers between devices  58.3 us (32%)
  waiting for transfers between devices  51.3 us (28%)
  local copies, waits for them, and re-layouts  37.7 us (20%)
  Pallas kernels  34.3 us (19%)
    all_to_all x5, starting transfers between devices, exchange(): return lax.all_to_all(block, axes, split_axis=0, concat_axis=0, tiled=True)  37.8 us
    ppermute x12, waiting for transfers between devices, shifted(): lax.ppermute(block, axis, [(i, (i + shift) % size) for i in range(size)])  37.3 us
    unnamed x41, local copies, waits for them, and re-layouts  30.7 us
    ppermute x12, starting transfers between devices, shifted(): lax.ppermute(block, axis, [(i, (i + shift) % size) for i in range(size)])  20 us
    all_to_all x5, waiting for transfers between devices, exchange(): return lax.all_to_all(block, axes, split_axis=0, concat_axis=0, tiled=True)  14 us
    pallas_call x1, Pallas kernels, body(): pl.pallas_call(backward_kernel, grid_spec=pltpu.PrefetchScalarGridSpec(nu...  13.7 us
    pallas_call x1, Pallas kernels, body(): pl.pallas_call(forward_kernel, grid_spec=pltpu.PrefetchScalarGridSpec(num...  12.3 us
  transfers between devices with their start and end apart: 22, of which 7 were waited for; matrix products, arithmetic and copies ran while one was open for 15% of the time, Pallas kernels for 17%

profile of v2, /device:TPU:8, one launch (start us, length us, event | category | flops | bytes accessed | tf_op | source)
XLA Modules:
  0.0 183.2 jit_solution(471354893243682438)
XLA Ops:
  0.6 2.3 %collective-permute-start.1 = (bf16[2,512,512]{2,1,0:T(8,128)(2,1)}, bf16[2,512,512]{2,1,0:T(8,128)(2,1)}, u32[]{:S(2)}, u32[]{:S(2)}) collective-permute-start(bf16[2,512,512]{2,1,0:T(8,128)(2,1)} %param.11), channel_id=1, source_target_pairs={{0,192},{32,224},{64,0},{96,32},{128,64},{160,96},{192,128},{224,1... | collective-permute-start | bytes 3145736 | tf_op jit(solution)/shard_map/ppermute | solution.py:184
  6.4 9.6 %all-to-all-start = ((bf16[32,2,16,512]{3,2,1,0:T(8,128)(2,1)}), bf16[32,2,16,512]{3,2,1,0:T(8,128)(2,1)S(1)}, u32[]{:S(2)}, u32[]{:S(2)}) async-start(bf16[32,2,16,512]{3,2,1,0:T(8,128)(2,1)} %pick_rows.1), calls=%async_computation | async-start | bytes 2097152 | tf_op jit(solution)/shard_map/all_to_all | solution.py:202
  15.9 1.7 collective-permute-start.3
  17.6 8.3 %collective-permute-done.1 = bf16[2,512,512]{2,1,0:T(8,128)(2,1)} collective-permute-done((bf16[2,512,512]{2,1,0:T(8,128)(2,1)}, bf16[2,512,512]{2,1,0:T(8,128)(2,1)}, u32[]{:S(2)}, u32[]{:S(2)}) %collective-permute-start.1) | collective-permute-done | bytes 1048608 | tf_op jit(solution)/shard_map/ppermute | solution.py:184
  25.9 15.9 %collective-permute-done.3 = bf16[2,512,512]{2,1,0:T(8,128)(2,1)S(1)} collective-permute-done((bf16[2,512,512]{2,1,0:T(8,128)(2,1)}, bf16[2,512,512]{2,1,0:T(8,128)(2,1)S(1)}, u32[]{:S(2)}, u32[]{:S(2)}) %collective-permute-start.3) | collective-permute-done | bytes 1048608 | tf_op jit(solution)/shard_map/ppermute | solution.py:184
  43.9 1.9 %slice.25 = bf16[1,512,512]{2,1,0:T(8,128)(2,1)} slice(bf16[2,512,512]{2,1,0:T(8,128)(2,1)} %collective-permute-done.1), slice={[1:2], [0:512], [0:512]} | slice | bytes 1048576 | tf_op jit(solution)/shard_map/slice | solution.py:192
  45.8 2.7 %collective-permute-start.5 = (bf16[1,512,512]{2,1,0:T(8,128)(2,1)}, bf16[1,512,512]{2,1,0:T(8,128)(2,1)}, u32[]{:S(2)}, u32[]{:S(2)}) collective-permute-start(bf16[1,512,512]{2,1,0:T(8,128)(2,1)} %slice.25), channel_id=1, source_target_pairs={{0,192},{32,224},{64,0},{96,32},{128,64},{160,96},{192,128},{224,1... | collective-permute-start | bytes 1572872 | tf_op jit(solution)/shard_map/ppermute | solution.py:184
  51.4 1.8 count_rows.1
  53.2 2.4 %constant_dynamic-update-slice_fusion.9 = bf16[16,512,512]{2,1,0:T(8,128)(2,1)} fusion(bf16[2,512,512]{2,1,0:T(8,128)(2,1)} %param.11), kind=kLoop, calls=%fused_computation.9 | loop fusion | bytes 2097152
  55.6 2.3 %constant_dynamic-update-slice_fusion.8 = bf16[16,512,512]{2,1,0:T(8,128)(2,1)} fusion(bf16[16,512,512]{2,1,0:T(8,128)(2,1)} %constant_dynamic-update-slice_fusion.9, bf16[2,512,512]{2,1,0:T(8,128)(2,1)} %collective-permute-done), kind=kLoop, calls=%fused_computation.8 | loop fusion | bytes 2097152
  58.5 2.3 %constant_dynamic-update-slice_fusion.7 = bf16[16,512,512]{2,1,0:T(8,128)(2,1)} fusion(bf16[16,512,512]{2,1,0:T(8,128)(2,1)} %constant_dynamic-update-slice_fusion.8, bf16[2,512,512]{2,1,0:T(8,128)(2,1)} %collective-permute-done.1), kind=kLoop, calls=%fused_computation.7 | loop fusion | bytes 2097152
  64.3 8.0 %all-to-all-start.1 = ((bf16[8,80,512]{2,1,0:T(8,128)(2,1)}), bf16[8,80,512]{2,1,0:T(8,128)(2,1)S(1)}, u32[]{:S(2)}, u32[]{:S(2)}) async-start(bf16[8,80,512]{2,1,0:T(8,128)(2,1)} %copy-done.4), calls=%async_computation.1 | async-start | bytes 1310720 | tf_op jit(solution)/shard_map/all_to_all | solution.py:202
  72.3 2.5 %collective-permute-start.9 = (bf16[2,256,512]{2,1,0:T(8,128)(2,1)}, bf16[2,256,512]{2,1,0:T(8,128)(2,1)S(1)}, u32[]{:S(2)}, u32[]{:S(2)}) collective-permute-start(bf16[2,256,512]{2,1,0:T(8,128)(2,1)} %copy-done.6), channel_id=1, source_target_pairs={{0,24},{8,0},{16,8},{24,16},{1,25},{9,1},{17,9},{25,17},{2,26},{10... | collective-permute-start | bytes 1572872 | tf_op jit(solution)/shard_map/ppermute | solution.py:184
  74.8 2.3 %constant_dynamic-update-slice_fusion.6 = bf16[16,512,512]{2,1,0:T(8,128)(2,1)} fusion(bf16[16,512,512]{2,1,0:T(8,128)(2,1)} %constant_dynamic-update-slice_fusion.7, bf16[2,512,512]{2,1,0:T(8,128)(2,1)} %collective-permute-done.2), kind=kLoop, calls=%fused_computation.6 | loop fusion | bytes 2097152
  77.1 1.9 %constant_dynamic-update-slice_fusion.5 = bf16[16,512,512]{2,1,0:T(8,128)(2,1)} fusion(bf16[16,512,512]{2,1,0:T(8,128)(2,1)} %constant_dynamic-update-slice_fusion.6, bf16[1,512,512]{2,1,0:T(8,128)(2,1)} %collective-permute-done.4), kind=kLoop, calls=%fused_computation.5 | loop fusion | bytes 1048576
  79.0 1.9 %constant_dynamic-update-slice_fusion.4 = bf16[16,512,512]{2,1,0:T(8,128)(2,1)} fusion(bf16[16,512,512]{2,1,0:T(8,128)(2,1)} %constant_dynamic-update-slice_fusion.5, bf16[1,512,512]{2,1,0:T(8,128)(2,1)} %collective-permute-done.5), kind=kLoop, calls=%fused_computation.4 | loop fusion | bytes 1048576
  80.9 1.9 %constant_dynamic-update-slice_fusion.3 = bf16[16,512,512]{2,1,0:T(8,128)(2,1)} fusion(bf16[16,512,512]{2,1,0:T(8,128)(2,1)} %constant_dynamic-update-slice_fusion.4, bf16[1,512,512]{2,1,0:T(8,128)(2,1)} %collective-permute-done.6), kind=kLoop, calls=%fused_computation.3 | loop fusion | bytes 1048576
  82.7 1.9 %constant_dynamic-update-slice_fusion.2 = bf16[16,512,512]{2,1,0:T(8,128)(2,1)} fusion(bf16[16,512,512]{2,1,0:T(8,128)(2,1)} %constant_dynamic-update-slice_fusion.3, bf16[1,512,512]{2,1,0:T(8,128)(2,1)} %collective-permute-done.7), kind=kLoop, calls=%fused_computation.2 | loop fusion | bytes 1048576
  84.6 2.3 %constant_dynamic-update-slice_fusion.1 = bf16[16,512,512]{2,1,0:T(8,128)(2,1)} fusion(bf16[16,512,512]{2,1,0:T(8,128)(2,1)} %constant_dynamic-update-slice_fusion.2, bf16[2,512,512]{2,1,0:T(8,128)(2,1)} %copy-done.14), kind=kLoop, calls=%fused_computation.1 | loop fusion | bytes 2097152
  86.9 2.4 %constant_dynamic-update-slice_fusion.weight_ref = bf16[16,512,512]{2,1,0:T(8,128)(2,1)} fusion(bf16[16,512,512]{2,1,0:T(8,128)(2,1)} %constant_dynamic-update-slice_fusion.1, bf16[2,512,512]{2,1,0:T(8,128)(2,1)} %collective-permute-done.8), kind=kLoop, calls=%fused_computation | loop fusion | bytes 2097152 | tf_op jit(solution)/shard_map/concatenate | solution.py:235
  89.3 12.3 %forward_layers.1 = (bf16[8,2,32,512]{3,2,1,0:T(8,128)(2,1)S(1)}, f32[16,32,512]{2,1,0:T(8,128)S(1)}) custom-call(s32[1]{0:T(128)} %bitcast.segment_ref, bf16[256,512]{1,0:T(8,128)(2,1)S(1)} %copy-done.8, bf16[16,512,512]{2,1,0:T(8,128)(2,1)} %constant_dynamic-update-slice_fusion.weight_ref, bf16[8,80,512]{2,1,0:T(8,128)(2,1)S(1)} %all-to-all-done.1.term_ref.flag_ref, ...), custom_call_target="tpu_custom_call" | custom-call | flops 268435456 | bytes 12582912 | tf_op jit(solution)/shard_map/forward_layers/pallas_call | solution.py:286
  102.3 4.8 %all-to-all-start.2 = ((bf16[8,2,32,512]{3,2,1,0:T(8,128)(2,1)}), bf16[8,2,32,512]{3,2,1,0:T(8,128)(2,1)S(1)}, u32[]{:S(2)}, u32[]{:S(2)}) async-start(bf16[8,2,32,512]{3,2,1,0:T(8,128)(2,1)} %copy-done.5), calls=%async_computation.2 | async-start | bytes 1048576 | tf_op jit(solution)/shard_map/all_to_all | solution.py:202
  108.2 2.6 %collective-permute-start.12 = (bf16[1,256,512]{2,1,0:T(8,128)(2,1)S(1)}, bf16[1,256,512]{2,1,0:T(8,128)(2,1)S(1)}, u32[]{:S(2)}, u32[]{:S(2)}) collective-permute-start(bf16[1,256,512]{2,1,0:T(8,128)(2,1)S(1)} %slice.27), channel_id=1, source_target_pairs={{0,24},{8,0},{16,8},{24,16},{1,25},{9,1},{17,9},{25,17},{2,26},{10... | collective-permute-start | bytes 786440 | tf_op jit(solution)/shard_map/ppermute | solution.py:184
  111.7 13.7 %backward_layers.1 = bf16[8,4,2,32,128]{4,3,2,1,0:T(8,128)(2,1)} custom-call(s32[1]{0:T(128)} %bitcast.segment_ref, bf16[256,512]{1,0:T(8,128)(2,1)S(1)} %copy-done.9, bf16[16,512,512]{2,1,0:T(8,128)(2,1)} %constant_dynamic-update-slice_fusion.weight_ref, f32[16,32,512]{2,1,0:T(8,128)S(1)} %get-tuple-element.21.pre_ref, ...), custom_call_target="tpu_custom_call" | custom-call | flops 268435456 | bytes 12582912 | tf_op jit(solution)/shard_map/backward_layers/pallas_call | solution.py:316
  126.2 3.2 %collective-permute-start.13 = (bf16[8,2,32,512]{3,2,1,0:T(8,128)(2,1)S(1)}, bf16[8,2,32,512]{3,2,1,0:T(8,128)(2,1)S(1)}, u32[]{:S(2)}, u32[]{:S(2)}) collective-permute-start(bf16[8,2,32,512]{3,2,1,0:T(8,128)(2,1)S(1)} %all-to-all-done.2.x_ref.x_own), channel_id=1, source_target_pairs={{0,24},{8,0},{16,8},{24,16},{1,25},{9,1},{17,9},{25,17},{2,26},{10... | collective-permute-start | bytes 1572872 | tf_op jit(solution)/shard_map/ppermute | solution.py:184
  129.4 5.2 %all-to-all-start.3 = ((bf16[32,2,32,128]{3,2,1,0:T(8,128)(2,1)}), bf16[32,2,32,128]{3,2,1,0:T(8,128)(2,1)S(1)}, u32[]{:S(2)}, u32[]{:S(2)}) async-start(bf16[32,2,32,128]{3,2,1,0:T(8,128)(2,1)} %bitcast.2), calls=%async_computation.3 | async-start | bytes 1048576 | tf_op jit(solution)/shard_map/all_to_all | solution.py:202
  134.6 8.8 %collective-permute-done.14.x_last = bf16[8,2,32,512]{3,2,1,0:T(8,128)(2,1)S(1)} collective-permute-done((bf16[8,2,32,512]{3,2,1,0:T(8,128)(2,1)S(1)}, bf16[8,2,32,512]{3,2,1,0:T(8,128)(2,1)S(1)}, u32[]{:S(2)}, u32[]{:S(2)}) %collective-permute-start.14) | collective-permute-done | bytes 524320 | tf_op jit(solution)/shard_map/ppermute | solution.py:184
  144.8 3.8 %collective-permute-start.16 = (bf16[4,2,32,512]{3,2,1,0:T(8,128)(2,1)}, bf16[4,2,32,512]{3,2,1,0:T(8,128)(2,1)}, u32[]{:S(2)}, u32[]{:S(2)}) collective-permute-start(bf16[4,2,32,512]{3,2,1,0:T(8,128)(2,1)} %slice.29), channel_id=1, source_target_pairs={{0,24},{8,0},{16,8},{24,16},{1,25},{9,1},{17,9},{25,17},{2,26},{10... | collective-permute-start | bytes 786440 | tf_op jit(solution)/shard_map/ppermute | solution.py:184
  148.7 3.7 %collective-permute-done.15.x_far0 = bf16[4,2,32,512]{3,2,1,0:T(8,128)(2,1)} collective-permute-done((bf16[4,2,32,512]{3,2,1,0:T(8,128)(2,1)}, bf16[4,2,32,512]{3,2,1,0:T(8,128)(2,1)}, u32[]{:S(2)}, u32[]{:S(2)}) %collective-permute-start.15) | collective-permute-done | bytes 262176 | tf_op jit(solution)/shard_map/ppermute | solution.py:184
  154.9 2.6 %weight_products.1 = bf16[32,2,2,16,128]{4,3,2,1,0:T(8,128)(2,1)} custom-call(s32[1]{0:T(128)} %bitcast.1.place_ref, bf16[8,4,2,32,128]{4,3,2,1,0:T(8,128)(2,1)S(1)} %bitcast.6, bf16[2,256,512]{2,1,0:T(8,128)(2,1)S(1)} %copy-done.7, bf16[2,256,512]{2,1,0:T(8,128)(2,1)S(1)} %collective-permute-done.9.mean_next, ...), custom_call_target="tpu_custom_call" | custom-call | tf_op jit(solution)/shard_map/weight_products/pallas_call | solution.py:348
  157.5 10.2 %all-to-all-start.4 = ((bf16[32,2,2,16,128]{4,3,2,1,0:T(8,128)(2,1)}), bf16[32,2,2,16,128]{4,3,2,1,0:T(8,128)(2,1)S(1)}, u32[]{:S(2)}, u32[]{:S(2)}) async-start(bf16[32,2,2,16,128]{4,3,2,1,0:T(8,128)(2,1)} %weight_products.1), calls=%async_computation.4 | async-start | bytes 1048576 | tf_op jit(solution)/shard_map/all_to_all | solution.py:202
  168.5 13.9 %all-to-all-done.4 = bf16[32,2,2,16,128]{4,3,2,1,0:T(8,128)(2,1)S(1)} async-done(((bf16[32,2,2,16,128]{4,3,2,1,0:T(8,128)(2,1)}), bf16[32,2,2,16,128]{4,3,2,1,0:T(8,128)(2,1)S(1)}, u32[]{:S(2)}, u32[]{:S(2)}) %all-to-all-start.4) | async-done | bytes 524320 | tf_op jit(solution)/shard_map/all_to_all | solution.py:202
  (72 shorter events, 20.9 us)
Async XLA Ops:
  0.6 49.3 %copy-start = (s32[32,32]{1,0:T(8,128)S(1)}, s32[32,32]{1,0:T(8,128)}, u32[]{:S(2)}) copy-start(s32[32,32]{1,0:T(8,128)} %param.15) | copy-start | bytes 12292
  0.6 25.3 %collective-permute-start.1 = (bf16[2,512,512]{2,1,0:T(8,128)(2,1)}, bf16[2,512,512]{2,1,0:T(8,128)(2,1)}, u32[]{:S(2)}, u32[]{:S(2)}) collective-permute-start(bf16[2,512,512]{2,1,0:T(8,128)(2,1)} %param.11), channel_id=1, source_target_pairs={{0,192},{32,224},{64,0},{96,32},{128,64},{160,96},{192,128},{224,1... | collective-permute-start | bytes 3145736 | tf_op jit(solution)/shard_map/ppermute | solution.py:184
  3.8 1.0 copy-start.1
  4.9 55.9 %copy-start.3 = (bf16[2,512,512]{2,1,0:T(8,128)(2,1)S(1)}, bf16[2,512,512]{2,1,0:T(8,128)(2,1)}, u32[]{:S(2)}) copy-start(bf16[2,512,512]{2,1,0:T(8,128)(2,1)} %weight_ref.1) | copy-start | bytes 3145732
  6.4 54.4 %all-to-all-start = ((bf16[32,2,16,512]{3,2,1,0:T(8,128)(2,1)}), bf16[32,2,16,512]{3,2,1,0:T(8,128)(2,1)S(1)}, u32[]{:S(2)}, u32[]{:S(2)}) async-start(bf16[32,2,16,512]{3,2,1,0:T(8,128)(2,1)} %pick_rows.1), calls=%async_computation | async-start | bytes 2097152 | tf_op jit(solution)/shard_map/all_to_all | solution.py:202
  15.9 25.9 %collective-permute-start.3 = (bf16[2,512,512]{2,1,0:T(8,128)(2,1)}, bf16[2,512,512]{2,1,0:T(8,128)(2,1)S(1)}, u32[]{:S(2)}, u32[]{:S(2)}) collective-permute-start(bf16[2,512,512]{2,1,0:T(8,128)(2,1)} %param.11), channel_id=1, source_target_pairs={{0,64},{32,96},{64,128},{96,160},{128,192},{160,224},{192,0},{224,... | collective-permute-start | bytes 3145736 | tf_op jit(solution)/shard_map/ppermute | solution.py:184
  17.6 38.0 %collective-permute-start = (bf16[2,512,512]{2,1,0:T(8,128)(2,1)}, bf16[2,512,512]{2,1,0:T(8,128)(2,1)}, u32[]{:S(2)}, u32[]{:S(2)}) collective-permute-start(bf16[2,512,512]{2,1,0:T(8,128)(2,1)} %param.11), channel_id=1, source_target_pairs={{0,32},{32,0},{64,96},{96,64},{128,160},{160,128},{192,224},{224,1... | collective-permute-start | bytes 3145736 | tf_op jit(solution)/shard_map/ppermute | solution.py:198
  25.9 48.9 %collective-permute-start.2 = (bf16[2,512,512]{2,1,0:T(8,128)(2,1)}, bf16[2,512,512]{2,1,0:T(8,128)(2,1)}, u32[]{:S(2)}, u32[]{:S(2)}) collective-permute-start(bf16[2,512,512]{2,1,0:T(8,128)(2,1)} %collective-permute-done.1), channel_id=1, source_target_pairs={{0,32},{32,0},{64,96},{96,64},{128,160},{160,128},{192,224},{224,1... | collective-permute-start | bytes 3145736 | tf_op jit(solution)/shard_map/ppermute | solution.py:198
  41.8 1.0 copy-start.14
  43.6 14.2 %collective-permute-start.4 = (bf16[1,512,512]{2,1,0:T(8,128)(2,1)}, bf16[1,512,512]{2,1,0:T(8,128)(2,1)}, u32[]{:S(2)}, u32[]{:S(2)}) collective-permute-start(bf16[1,512,512]{2,1,0:T(8,128)(2,1)} %slice.24), channel_id=1, source_target_pairs={{0,64},{32,96},{64,128},{96,160},{128,192},{160,224},{192,0},{224,... | collective-permute-start | bytes 1572872 | tf_op jit(solution)/shard_map/ppermute | solution.py:184
  45.8 12.7 %collective-permute-start.5 = (bf16[1,512,512]{2,1,0:T(8,128)(2,1)}, bf16[1,512,512]{2,1,0:T(8,128)(2,1)}, u32[]{:S(2)}, u32[]{:S(2)}) collective-permute-start(bf16[1,512,512]{2,1,0:T(8,128)(2,1)} %slice.25), channel_id=1, source_target_pairs={{0,192},{32,224},{64,0},{96,32},{128,64},{160,96},{192,128},{224,1... | collective-permute-start | bytes 1572872 | tf_op jit(solution)/shard_map/ppermute | solution.py:184
  50.3 1.1 copy-start.2
  53.2 5.3 %copy-start.10 = (bf16[256,512]{1,0:T(8,128)(2,1)}, bf16[256,512]{1,0:T(8,128)(2,1)S(1)}, u32[]{:S(2)}) copy-start(bf16[256,512]{1,0:T(8,128)(2,1)S(1)} %get-tuple-element.18.counts_ref) | copy-start | bytes 786436
  55.6 31.4 %collective-permute-start.8 = (bf16[2,512,512]{2,1,0:T(8,128)(2,1)}, bf16[2,512,512]{2,1,0:T(8,128)(2,1)}, u32[]{:S(2)}, u32[]{:S(2)}) collective-permute-start(bf16[2,512,512]{2,1,0:T(8,128)(2,1)} %copy-done.14), channel_id=1, source_target_pairs={{0,32},{32,0},{64,96},{96,64},{128,160},{160,128},{192,224},{224,1... | collective-permute-start | bytes 3145736 | tf_op jit(solution)/shard_map/ppermute | solution.py:198
  57.8 31.5 %copy-start.8 = (bf16[256,512]{1,0:T(8,128)(2,1)S(1)}, bf16[256,512]{1,0:T(8,128)(2,1)}, u32[]{:S(2)}) copy-start(bf16[256,512]{1,0:T(8,128)(2,1)} %features_ref.1) | copy-start | bytes 786436
  57.8 23.1 %collective-permute-start.6 = (bf16[1,512,512]{2,1,0:T(8,128)(2,1)}, bf16[1,512,512]{2,1,0:T(8,128)(2,1)}, u32[]{:S(2)}, u32[]{:S(2)}) collective-permute-start(bf16[1,512,512]{2,1,0:T(8,128)(2,1)} %collective-permute-done.4), channel_id=1, source_target_pairs={{0,32},{32,0},{64,96},{96,64},{128,160},{160,128},{192,224},{224,1... | collective-permute-start | bytes 1572872 | tf_op jit(solution)/shard_map/ppermute | solution.py:198
  58.5 24.3 %collective-permute-start.7 = (bf16[1,512,512]{2,1,0:T(8,128)(2,1)}, bf16[1,512,512]{2,1,0:T(8,128)(2,1)}, u32[]{:S(2)}, u32[]{:S(2)}) collective-permute-start(bf16[1,512,512]{2,1,0:T(8,128)(2,1)} %collective-permute-done.5), channel_id=1, source_target_pairs={{0,32},{32,0},{64,96},{96,64},{128,160},{160,128},{192,224},{224,1... | collective-permute-start | bytes 1572872 | tf_op jit(solution)/shard_map/ppermute | solution.py:198
  60.8 1.0 copy-start.11
  64.3 25.0 %all-to-all-start.1 = ((bf16[8,80,512]{2,1,0:T(8,128)(2,1)}), bf16[8,80,512]{2,1,0:T(8,128)(2,1)S(1)}, u32[]{:S(2)}, u32[]{:S(2)}) async-start(bf16[8,80,512]{2,1,0:T(8,128)(2,1)} %copy-done.4), calls=%async_computation.1 | async-start | bytes 1310720 | tf_op jit(solution)/shard_map/all_to_all | solution.py:202
  72.3 35.9 %collective-permute-start.9 = (bf16[2,256,512]{2,1,0:T(8,128)(2,1)}, bf16[2,256,512]{2,1,0:T(8,128)(2,1)S(1)}, u32[]{:S(2)}, u32[]{:S(2)}) collective-permute-start(bf16[2,256,512]{2,1,0:T(8,128)(2,1)} %copy-done.6), channel_id=1, source_target_pairs={{0,24},{8,0},{16,8},{24,16},{1,25},{9,1},{17,9},{25,17},{2,26},{10... | collective-permute-start | bytes 1572872 | tf_op jit(solution)/shard_map/ppermute | solution.py:184
  74.8 32.3 %collective-permute-start.10 = (bf16[2,256,512]{2,1,0:T(8,128)(2,1)}, bf16[2,256,512]{2,1,0:T(8,128)(2,1)S(1)}, u32[]{:S(2)}, u32[]{:S(2)}) collective-permute-start(bf16[2,256,512]{2,1,0:T(8,128)(2,1)} %copy-done.6), channel_id=1, source_target_pairs={{0,8},{8,16},{16,24},{24,0},{1,9},{9,17},{17,25},{25,1},{2,10},{10... | collective-permute-start | bytes 1572872 | tf_op jit(solution)/shard_map/ppermute | solution.py:184
  102.3 23.8 %all-to-all-start.2 = ((bf16[8,2,32,512]{3,2,1,0:T(8,128)(2,1)}), bf16[8,2,32,512]{3,2,1,0:T(8,128)(2,1)S(1)}, u32[]{:S(2)}, u32[]{:S(2)}) async-start(bf16[8,2,32,512]{3,2,1,0:T(8,128)(2,1)} %copy-done.5), calls=%async_computation.2 | async-start | bytes 1048576 | tf_op jit(solution)/shard_map/all_to_all | solution.py:202
  107.2 18.3 %collective-permute-start.11 = (bf16[1,256,512]{2,1,0:T(8,128)(2,1)S(1)}, bf16[1,256,512]{2,1,0:T(8,128)(2,1)S(1)}, u32[]{:S(2)}, u32[]{:S(2)}) collective-permute-start(bf16[1,256,512]{2,1,0:T(8,128)(2,1)S(1)} %slice.26), channel_id=1, source_target_pairs={{0,8},{8,16},{16,24},{24,0},{1,9},{9,17},{17,25},{25,1},{2,10},{10... | collective-permute-start | bytes 786440 | tf_op jit(solution)/shard_map/ppermute | solution.py:184
  108.2 17.3 %collective-permute-start.12 = (bf16[1,256,512]{2,1,0:T(8,128)(2,1)S(1)}, bf16[1,256,512]{2,1,0:T(8,128)(2,1)S(1)}, u32[]{:S(2)}, u32[]{:S(2)}) collective-permute-start(bf16[1,256,512]{2,1,0:T(8,128)(2,1)S(1)} %slice.27), channel_id=1, source_target_pairs={{0,24},{8,0},{16,8},{24,16},{1,25},{9,1},{17,9},{25,17},{2,26},{10... | collective-permute-start | bytes 786440 | tf_op jit(solution)/shard_map/ppermute | solution.py:184
  110.8 0.9 copy-start.9
  126.2 17.2 %collective-permute-start.14 = (bf16[8,2,32,512]{3,2,1,0:T(8,128)(2,1)S(1)}, bf16[8,2,32,512]{3,2,1,0:T(8,128)(2,1)S(1)}, u32[]{:S(2)}, u32[]{:S(2)}) collective-permute-start(bf16[8,2,32,512]{3,2,1,0:T(8,128)(2,1)S(1)} %all-to-all-done.2.x_ref.x_own), channel_id=1, source_target_pairs={{0,8},{8,16},{16,24},{24,0},{1,9},{9,17},{17,25},{25,1},{2,10},{10... | collective-permute-start | bytes 1572872 | tf_op jit(solution)/shard_map/ppermute | solution.py:184
  126.2 17.9 %collective-permute-start.13 = (bf16[8,2,32,512]{3,2,1,0:T(8,128)(2,1)S(1)}, bf16[8,2,32,512]{3,2,1,0:T(8,128)(2,1)S(1)}, u32[]{:S(2)}, u32[]{:S(2)}) collective-permute-start(bf16[8,2,32,512]{3,2,1,0:T(8,128)(2,1)S(1)} %all-to-all-done.2.x_ref.x_own), channel_id=1, source_target_pairs={{0,24},{8,0},{16,8},{24,16},{1,25},{9,1},{17,9},{25,17},{2,26},{10... | collective-permute-start | bytes 1572872 | tf_op jit(solution)/shard_map/ppermute | solution.py:184
  129.4 19.3 %all-to-all-start.3 = ((bf16[32,2,32,128]{3,2,1,0:T(8,128)(2,1)}), bf16[32,2,32,128]{3,2,1,0:T(8,128)(2,1)S(1)}, u32[]{:S(2)}, u32[]{:S(2)}) async-start(bf16[32,2,32,128]{3,2,1,0:T(8,128)(2,1)} %bitcast.2), calls=%async_computation.3 | async-start | bytes 1048576 | tf_op jit(solution)/shard_map/all_to_all | solution.py:202
  144.1 8.3 %collective-permute-start.15 = (bf16[4,2,32,512]{3,2,1,0:T(8,128)(2,1)}, bf16[4,2,32,512]{3,2,1,0:T(8,128)(2,1)}, u32[]{:S(2)}, u32[]{:S(2)}) collective-permute-start(bf16[4,2,32,512]{3,2,1,0:T(8,128)(2,1)} %slice.28), channel_id=1, source_target_pairs={{0,8},{8,16},{16,24},{24,0},{1,9},{9,17},{17,25},{25,1},{2,10},{10... | collective-permute-start | bytes 786440 | tf_op jit(solution)/shard_map/ppermute | solution.py:184
  144.8 8.0 %collective-permute-start.16 = (bf16[4,2,32,512]{3,2,1,0:T(8,128)(2,1)}, bf16[4,2,32,512]{3,2,1,0:T(8,128)(2,1)}, u32[]{:S(2)}, u32[]{:S(2)}) collective-permute-start(bf16[4,2,32,512]{3,2,1,0:T(8,128)(2,1)} %slice.29), channel_id=1, source_target_pairs={{0,24},{8,0},{16,8},{24,16},{1,25},{9,1},{17,9},{25,17},{2,26},{10... | collective-permute-start | bytes 786440 | tf_op jit(solution)/shard_map/ppermute | solution.py:184
  152.9 1.0 copy-start.7
  157.5 24.9 %all-to-all-start.4 = ((bf16[32,2,2,16,128]{4,3,2,1,0:T(8,128)(2,1)}), bf16[32,2,2,16,128]{4,3,2,1,0:T(8,128)(2,1)S(1)}, u32[]{:S(2)}, u32[]{:S(2)}) async-start(bf16[32,2,2,16,128]{4,3,2,1,0:T(8,128)(2,1)} %weight_products.1), calls=%async_computation.4 | async-start | bytes 1048576 | tf_op jit(solution)/shard_map/all_to_all | solution.py:202
  (5 other events, 4.1 us)

commit v3 on v1

v3 whole, which is shorter than its diff:
```python
import functools

import jax
import jax.numpy as jnp
from jax import lax
from jax.experimental import pallas as pl
from jax.experimental.pallas import tpu as pltpu
from jax.sharding import Mesh
from jax.sharding import PartitionSpec as P

epsilon = 1e-06
SLOTS = 2
PAIR = 2
BF16 = jnp.bfloat16
F32 = jnp.float32
MIB = 1024 * 1024


def matmul(a, b):
    return jnp.dot(a, b, preferred_element_type=F32)


def params(mib):
    return pltpu.CompilerParams(vmem_limit_bytes=int(mib * MIB))


def lasting(microseconds):
    return pl.CostEstimate(
        flops=int(microseconds * 1.15e9), bytes_accessed=4 * MIB, transcendentals=0
    )


def pick_kernel(index_ref, history_ref, out_ref):
    slots, nodes, width = history_ref.shape
    shards, _, rows, _ = out_ref.shape
    columns = lax.broadcasted_iota(jnp.int32, (shards * rows, nodes), 1)
    chosen = (index_ref[...] == columns).astype(F32).astype(BF16)
    for slot in range(slots):
        picked = matmul(chosen, history_ref[slot]).astype(BF16)
        out_ref[:, slot] = picked.reshape(shards, rows, width)


def token_kernel(in_ref, out_ref):
    out_ref[0, 0] = in_ref[0, 0]


def count_kernel(neighbours_ref, live_ref, out_ref, counts_ref, sem):
    nodes, table = counts_ref.shape
    columns = lax.broadcasted_iota(jnp.int32, (nodes, table), 1)
    total = jnp.zeros((nodes, table), F32)
    for k in range(neighbours_ref.shape[1]):
        total += jnp.where(neighbours_ref[:, k : k + 1] == columns, 1.0, 0.0)
    counts_ref[...] = (total * live_ref[...]).astype(BF16)
    copy = pltpu.make_async_copy(counts_ref, out_ref, sem)
    copy.start()
    copy.wait()


def mean_kernel(
    depth_ref, half_ref, received_ref, counts_hbm, history_hbm, weight_hbm,
    mine_hbm, others_hbm, term_hbm,
    counts_ref, history_ref, weight_ref, mine_ref, others_ref, term_ref, sems, *, fanout,
):
    slots, nodes, width = history_ref.shape
    segments = term_ref.shape[0]
    part = nodes // segments
    loads = [
        pltpu.make_async_copy(hbm, ref, sems.at[i])
        for i, (hbm, ref) in enumerate(
            ((counts_hbm, counts_ref), (history_hbm, history_ref), (weight_hbm, weight_ref))
        )
    ]
    for load in loads:
        load.start()
    flag = depth_ref[0].astype(F32)
    tail = term_ref.shape[1] - slots * part
    term_ref[:, slots * part :] = jnp.full((segments, tail, width), flag, F32).astype(BF16)
    loads[0].wait()
    far = [
        matmul(counts_ref[:, nodes:], received_ref[:, slot].reshape(-1, width))
        for slot in range(slots)
    ]
    loads[1].wait()
    means = [
        ((far[slot] + matmul(counts_ref[:, :nodes], history_ref[slot])) * (1.0 / fanout)).astype(
            BF16
        )
        for slot in range(slots)
    ]
    loads[2].wait()
    for slot in range(slots):
        term = matmul(means[slot], weight_ref[slot]).astype(BF16)
        term_ref[:, slot * part : (slot + 1) * part] = term.reshape(segments, part, width)
    stores = [pltpu.make_async_copy(term_ref, term_hbm, sems.at[3])]
    stores[0].start()
    for half in range(2):

        @pl.when(half_ref[0] == half)
        def _():
            for slot in range(slots):
                mean = means[slot]
                mine_ref[slot] = mean[:, half * width // 2 : (half + 1) * width // 2]
                others_ref[slot] = mean[:, (1 - half) * width // 2 : (2 - half) * width // 2]

    stores.append(pltpu.make_async_copy(mine_ref, mine_hbm, sems.at[4]))
    stores.append(pltpu.make_async_copy(others_ref, others_hbm, sems.at[5]))
    for store in stores[1:]:
        store.start()
    for store in stores:
        store.wait()


def normalize(pre_norm):
    inverse = lax.rsqrt(jnp.mean(pre_norm * pre_norm, axis=-1, keepdims=True) + epsilon)
    return inverse, pre_norm * inverse


def start_weights(segment_ref, pieces, weights, sems, order):
    for segment in range(len(order) // SLOTS):

        @pl.when(segment_ref[0] == segment)
        def _():
            for layer in order:
                section = layer // SLOTS
                ahead = (section // 2 - segment // 2) % 4
                piece = pieces[ahead * 2 + (section + segment) % 2]
                pltpu.make_async_copy(
                    piece.at[layer % SLOTS], weights.at[layer], sems.at[layer]
                ).start()


def wait_weights(pieces, weights, sems, layer):
    pltpu.make_async_copy(pieces[0].at[0], weights.at[layer], sems.at[layer]).wait()


def two_slots(terms_ref, section):
    rows = terms_ref.shape[1]
    return jnp.max(terms_ref[section, rows - 16 :, :128].astype(F32)) > 1.5


def layers_kernel(segment_ref, features_ref, cotangent_ref, terms_hbm, *refs):
    pieces, refs = refs[:8], refs[8:]
    out_hbm, out_ref, terms_ref, state, weights, pre, sems, term_sems, out_sems = refs
    segments, halves, _, _, slots, part, columns = out_ref.shape
    layers = segments * slots

    def load_terms(section):
        return pltpu.make_async_copy(
            terms_hbm.at[section], terms_ref.at[section], term_sems.at[section]
        )

    def store_rows(section):
        return pltpu.make_async_copy(
            out_ref.at[section], out_hbm.at[section], out_sems.at[section]
        )

    load_terms(0).start()
    start_weights(segment_ref, pieces, weights, sems, range(layers))
    for section in range(1, segments):
        load_terms(section).start()
    state[...] = features_ref[...]

    def keep_input(section, slot):
        x = state[...]
        for i in range(halves):
            for j in range(halves):
                out_ref[section, i, j, 0, slot] = x[:, i * columns : (i + 1) * columns]

    def forward(section, slot):
        layer = section * slots + slot
        x = state[...]
        pre_norm = matmul(x, weights[layer]) + terms_ref[
            section, slot * part : (slot + 1) * part
        ].astype(F32)
        pre[layer] = pre_norm
        _, normed = normalize(pre_norm)
        state[...] = (x.astype(F32) + normed * jax.nn.sigmoid(normed)).astype(BF16)

    @pl.loop(0, segments)
    def _(section):
        load_terms(section).wait()
        both = two_slots(terms_ref, section)
        wait_weights(pieces, weights, sems, section * slots)
        keep_input(section, 0)
        forward(section, 0)
        wait_weights(pieces, weights, sems, section * slots + 1)
        keep_input(section, 1)

        @pl.when(both)
        def _():
            forward(section, 1)

    state[...] = cotangent_ref[...]

    def backward(section, slot):
        layer = section * slots + slot
        inverse, normed = normalize(pre[layer])
        grad_out = state[...].astype(F32)
        sigmoid = jax.nn.sigmoid(normed)
        grad_normed = grad_out * sigmoid * (1.0 + normed * (1.0 - sigmoid))
        grad_pre = inverse * (
            grad_normed - normed * jnp.mean(grad_normed * normed, axis=-1, keepdims=True)
        )
        low = grad_pre.astype(BF16)
        for i in range(halves):
            for j in range(halves):
                out_ref[section, i, j, 1, slot] = low[:, j * columns : (j + 1) * columns]
        back = lax.dot_general(
            low, weights[layer], (((1,), (1,)), ((), ())), preferred_element_type=F32
        )
        state[...] = (grad_out + back).astype(BF16)

    @pl.loop(0, segments)
    def _(step):
        section = segments - 1 - step
        both = two_slots(terms_ref, section)

        @pl.when(both)
        def _():
            backward(section, 1)

        @pl.when(jnp.logical_not(both))
        def _():
            for i in range(halves):
                for j in range(halves):
                    out_ref[section, i, j, 1, 1] = jnp.zeros((part, columns), BF16)

        backward(section, 0)
        store_rows(section).start()

    for section in range(segments):
        store_rows(section).wait()


def product_kernel(
    place_ref, rows_ref, mean0, mean1, mean2, mean3, out_ref, own_ref, partner_ref
):
    segments, parts, _, slots, rows, columns = rows_ref.shape
    shards, _, _, out_rows, _ = out_ref.shape
    place = place_ref[0]
    own_ref[...] = rows_ref[:, place, 0]
    partner_ref[...] = rows_ref[:, place ^ 2, 0]
    for slot in range(slots):
        self_sum = neigh_sum = None
        for step, mean in enumerate((mean0, mean1, mean2, mean3)):
            part = place ^ step
            grad = rows_ref[:, part, 1, slot].reshape(segments * rows, columns).T
            layer_in = rows_ref[:, part, 0, slot].reshape(segments * rows, columns)
            self_term, neigh_term = matmul(grad, layer_in), matmul(grad, mean[slot])
            self_sum = self_term if self_sum is None else self_sum + self_term
            neigh_sum = neigh_term if neigh_sum is None else neigh_sum + neigh_term
        for kind, total in enumerate((self_sum, neigh_sum)):
            out_ref[:, kind, slot] = total.T.astype(BF16).reshape(shards, out_rows, columns)


def finish_kernel(half_ref, parts_ref, own_ref, missing_ref, self_ref, neigh_ref, out_ref):
    width = parts_ref.shape[5]
    for part in range(parts_ref.shape[0]):
        total = jnp.sum(parts_ref[part].astype(F32), axis=0)
        self_ref[:, :, part * width : (part + 1) * width] = total[0]
        neigh_ref[:, :, part * width : (part + 1) * width] = total[1]
    segments, slots, rows, columns = own_ref.shape
    for half in range(2):

        @pl.when(half_ref[0] == half)
        def _():
            for ref, at in ((own_ref, half), (missing_ref, 1 - half)):
                for slot in range(slots):
                    out_ref[slot, :, at * columns : (at + 1) * columns] = ref[:, slot].reshape(
                        segments * rows, columns
                    )


def round_y(block, step_of):
    size = lax.axis_size("segment")
    route = [(i, (i + 2 * step_of(i % 2)) % size) for i in range(size)]
    return lax.ppermute(block, "segment", route)


def core_swap(block):
    size = lax.axis_size("segment")
    return lax.ppermute(block, "segment", [(i, i ^ 1) for i in range(size)])


def x_swap(block, step):
    return lax.ppermute(block, ("xa", "xb"), [(i, i ^ step) for i in range(PAIR * PAIR)])


def exchange(block, axes):
    return lax.all_to_all(block, axes, split_axis=0, concat_axis=0, tiled=True)


def body(
    features,
    history,
    weight_self,
    weight_neigh,
    depth,
    send_index,
    pair_count,
    neighbours,
    cotangent,
):
    segments = lax.axis_size("segment")
    x_size = PAIR * PAIR
    z_size = lax.axis_size("z")
    shards = x_size * z_size
    my_segment = lax.axis_index("segment").reshape(1)
    my_half = lax.axis_index("xa").reshape(1)
    my_place = lax.axis_index(("xa", "xb")).reshape(1)
    my_shard = lax.axis_index(("xa", "xb", "z"))
    slots, nodes, width = history.shape
    rows_pair = send_index.shape[2]
    fanout = neighbours.shape[1]
    layers = segments * slots
    part = nodes // segments
    columns = width // 2
    received_rows = shards * rows_pair

    last_w = round_y(weight_self, lambda core: 1)
    next_w = round_y(weight_self, lambda core: -1)

    outgoing = pl.pallas_call(
        pick_kernel,
        out_shape=jax.ShapeDtypeStruct((shards, slots, rows_pair, width), BF16),
        compiler_params=params(12),
        name="pick_rows",
    )(send_index.reshape(received_rows, 1), history)
    received = exchange(outgoing, ("xa", "xb", "z"))

    own_rows = functools.partial(
        lax.dynamic_slice_in_dim, start_index=lax.axis_index("segment") * part, slice_size=part
    )
    my_features, my_cotangent, neighbours = lax.optimization_barrier(
        (own_rows(features), own_rows(cotangent), neighbours)
    )
    last_w, next_w, other_w, token = lax.optimization_barrier(
        (last_w, next_w, core_swap(weight_self), depth.reshape(1, 1))
    )
    token = pl.pallas_call(
        token_kernel,
        out_shape=jax.ShapeDtypeStruct((1, 1), jnp.int32),
        in_specs=[pl.BlockSpec(memory_space=pltpu.SMEM)],
        out_specs=pl.BlockSpec(memory_space=pltpu.SMEM),
        cost_estimate=lasting(40),
        name="after_first_wave",
    )(token)
    my_counts = lax.dynamic_index_in_dim(pair_count, my_shard, 1, keepdims=True)
    live = (lax.iota(jnp.int32, rows_pair)[None, :] < my_counts).astype(F32)
    live = jnp.concatenate(
        [jnp.ones((1, nodes), F32), live.reshape(1, received_rows)], axis=1
    )
    smem = pl.BlockSpec(memory_space=pltpu.SMEM)
    vmem = pl.BlockSpec(memory_space=pltpu.VMEM)
    hbm = pl.BlockSpec(memory_space=pltpu.MemorySpace.HBM)
    counts_shape = (nodes, nodes + received_rows)
    counts = pl.pallas_call(
        count_kernel,
        out_specs=hbm,
        out_shape=jax.ShapeDtypeStruct(counts_shape, BF16),
        scratch_shapes=[pltpu.VMEM(counts_shape, BF16), pltpu.SemaphoreType.DMA],
        compiler_params=params(12),
        cost_estimate=lasting(2),
        name="count_rows",
    )(neighbours, live)

    _, last_w, next_w = lax.optimization_barrier((token, last_w, next_w))
    forwarded = jnp.where(lax.rem(my_segment[0], 2) == 0, last_w, next_w)
    far_w = round_y(forwarded, lambda core: 1 - 2 * core)
    next_other, last_other = core_swap(next_w), core_swap(last_w)

    term_rows = slots * part + 16
    half_shape = jax.ShapeDtypeStruct((slots, nodes, columns), BF16)
    mean, others_mean, terms = pl.pallas_call(
        functools.partial(mean_kernel, fanout=fanout),
        in_specs=[smem, smem, vmem, hbm, hbm, hbm],
        out_specs=(hbm, hbm, hbm),
        scratch_shapes=[
            pltpu.VMEM(counts_shape, BF16),
            pltpu.VMEM(history.shape, BF16),
            pltpu.VMEM(weight_neigh.shape, BF16),
            pltpu.VMEM(half_shape.shape, BF16),
            pltpu.VMEM(half_shape.shape, BF16),
            pltpu.VMEM((segments, term_rows, width), BF16),
            pltpu.SemaphoreType.DMA((6,)),
        ],
        out_shape=(
            half_shape,
            half_shape,
            jax.ShapeDtypeStruct((segments, term_rows, width), BF16),
        ),
        compiler_params=params(59.3),
        cost_estimate=lasting(2),
        name="neighbour_mean",
    )(depth, my_half, received, counts, history, weight_neigh)
    all_terms = exchange(terms, "segment")
    _, far_w, next_other, last_other = lax.optimization_barrier(
        (mean, far_w, next_other, last_other)
    )
    pieces = (
        weight_self, other_w, next_w, next_other, far_w, core_swap(far_w), last_w, last_other
    )

    anywhere = pl.BlockSpec(memory_space=pl.ANY)
    rows = pl.pallas_call(
        layers_kernel,
        in_specs=[smem, vmem, vmem, anywhere] + [anywhere] * len(pieces),
        out_specs=anywhere,
        out_shape=jax.ShapeDtypeStruct((segments, 2, 2, 2, slots, part, columns), BF16),
        scratch_shapes=[
            pltpu.VMEM((segments, 2, 2, 2, slots, part, columns), BF16),
            pltpu.VMEM((segments, term_rows, width), BF16),
            pltpu.VMEM((part, width), BF16),
            pltpu.VMEM((layers, width, width), BF16),
            pltpu.VMEM((layers, part, width), F32),
            pltpu.SemaphoreType.DMA((layers,)),
            pltpu.SemaphoreType.DMA((segments,)),
            pltpu.SemaphoreType.DMA((segments,)),
        ],
        compiler_params=params(60),
        cost_estimate=lasting(13),
        name="all_layers",
    )(my_segment, my_features, my_cotangent, all_terms, *pieces)
    rows, *other_means = lax.optimization_barrier(
        (rows, x_swap(mean, 1), x_swap(others_mean, 2), x_swap(others_mean, 3))
    )
    means = (mean, *other_means)
    rows = rows.reshape(segments * x_size, 2, slots, part, columns)
    rows = exchange(rows, ("segment", "xa", "xb"))

    out_rows = width // shards
    sources = PAIR * z_size
    kept_shape = jax.ShapeDtypeStruct((segments, slots, part, columns), BF16)
    products, kept, for_partner = pl.pallas_call(
        product_kernel,
        in_specs=[smem] + [vmem] * 5,
        out_shape=(
            jax.ShapeDtypeStruct((sources, 2, slots, out_rows, columns), BF16),
            kept_shape,
            kept_shape,
        ),
        compiler_params=params(16),
        cost_estimate=lasting(3),
        name="weight_products",
    )(my_place, rows.reshape(segments, x_size, 2, slots, part, columns), *means)
    summands = exchange(products, ("xb", "z"))
    grad_shape = jax.ShapeDtypeStruct((slots, out_rows, width), F32)
    grad_self, grad_neigh, new_history = pl.pallas_call(
        finish_kernel,
        in_specs=[smem, vmem, vmem, vmem],
        out_shape=(grad_shape, grad_shape, jax.ShapeDtypeStruct((slots, nodes, width), BF16)),
        compiler_params=params(12),
        name="finish",
    )(
        my_half,
        summands.reshape(PAIR, z_size, 2, slots, out_rows, columns),
        kept,
        x_swap(for_partner, 2),
    )
    return (new_history, grad_self, grad_neigh)


def solution(mesh):
    segments, shards = mesh.devices.shape
    split = Mesh(
        mesh.devices.reshape(segments, PAIR, PAIR, shards // (PAIR * PAIR)),
        ("segment", "xa", "xb", "z"),
    )
    shard = ("xa", "xb", "z")
    return jax.shard_map(
        body,
        mesh=split,
        in_specs=(
            P(shard, None),
            P("segment", shard, None),
            P("segment", None, None),
            P("segment", None, None),
            P("segment"),
            P(shard, None, None),
            P(),
            P(shard, None),
            P(shard, None),
        ),
        out_specs=(
            P("segment", shard, None),
            P("segment", shard, None),
            P("segment", shard, None),
        ),
        check_vma=False,
    )
```

time: 181 us -> 139 us (0.77)
  blocking collectives: 20.6 us -> 0 us
  between operations: 14.9 us -> 1.51 us
  waiting for transfers between devices: 80 us -> 67 us
  starting transfers between devices: 32.4 us -> 36.4 us
  Pallas kernels: 20.6 us -> 23.9 us
  local copies, waits for them, and re-layouts: 9.64 us -> 6.46 us
    all_to_all x4, waiting for transfers between devices: 78.6 us -> 46.1 us  [exchange(): return lax.all_to_all(block, axes, split_axis=0, concat_axis=0, tiled=True)]
    ppermute x0 -> x11, waiting for transfers between devices: none -> 20.9 us  [the longest x4 11.4 us: x_swap(): lax.ppermute(block, ('xa', 'xb'), [(i, i ^ step) for i in range(PAIR * PA...]
    all_to_all x1 -> x0, blocking collectives: 20.6 us -> none  [exchange(): return lax.all_to_all(block, axes, split_axis=0, concat_axis=0, tiled=True)]
    ppermute x0 -> x11, starting transfers between devices: none -> 10.9 us  [the longest x4 6.7 us: x_swap(): lax.ppermute(block, ('xa', 'xb'), [(i, i ^ step) for i in range(PAIR * PA...]
    all_to_all x4, starting transfers between devices: 32.3 us -> 25.5 us  [exchange(): return lax.all_to_all(block, axes, split_axis=0, concat_axis=0, tiled=True)]
    unnamed x28 -> x21, local copies, waits for them, and re-layouts: 9.21 us -> 4.52 us
    pallas_call x7 -> x5, Pallas kernels: 19.1 us -> 22.4 us  [the longest x1 13.5 us: body(): pl.pallas_call(layers_kernel, in_specs=[smem, vmem, vmem, anywhere] + [an...]
  transfers between devices with their start and end apart: 6 -> 15, of which waited for: 4 -> 7; matrix products, arithmetic and copies ran while one was open for 1% -> 3% of each run, Pallas kernels for 10% -> 16%
where the time goes in v3:
time: 139 us; the launch traced here: 137 us
  waiting for transfers between devices  67 us (48%)
  starting transfers between devices  36.4 us (26%)
  Pallas kernels  23.9 us (17%)
  local copies, waits for them, and re-layouts  6.46 us (5%)
  between operations  1.51 us (1%)
  other arithmetic  1.4 us (1%)
    all_to_all x4, waiting for transfers between devices, exchange(): return lax.all_to_all(block, axes, split_axis=0, concat_axis=0, tiled=True)  46.1 us
    all_to_all x4, starting transfers between devices, exchange(): return lax.all_to_all(block, axes, split_axis=0, concat_axis=0, tiled=True)  25.5 us
    pallas_call x1, Pallas kernels, body(): pl.pallas_call(layers_kernel, in_specs=[smem, vmem, vmem, anywhere] + [an...  13.5 us
    ppermute x4, waiting for transfers between devices, x_swap(): lax.ppermute(block, ('xa', 'xb'), [(i, i ^ step) for i in range(PAIR * PA...  11.4 us
    ppermute x3, waiting for transfers between devices, round_y(): return lax.ppermute(block, 'segment', route)  9.48 us
    ppermute x4, starting transfers between devices, x_swap(): lax.ppermute(block, ('xa', 'xb'), [(i, i ^ step) for i in range(PAIR * PA...  6.7 us
    unnamed x21, local copies, waits for them, and re-layouts  4.52 us
    pallas_call x1, Pallas kernels, body(): pl.pallas_call(functools.partial(mean_kernel, fanout=fanout), in_specs=[s...  4.49 us
  transfers between devices with their start and end apart: 15, of which 7 were waited for; matrix products, arithmetic and copies ran while one was open for 3% of the time, Pallas kernels for 16%

profile of v3, /device:TPU:8, one launch (start us, length us, event | category | flops | bytes accessed | tf_op | source)
XLA Modules:
  0.0 136.7 jit_solution(6266082113977070871)
XLA Ops:
  0.6 1.7 %collective-permute-start = (bf16[2,512,512]{2,1,0:T(8,128)(2,1)}, bf16[2,512,512]{2,1,0:T(8,128)(2,1)S(1)}, u32[]{:S(2)}, u32[]{:S(2)}) collective-permute-start(bf16[2,512,512]{2,1,0:T(8,128)(2,1)} %refs_0_.1), channel_id=1, source_target_pairs={{0,64},{32,96},{64,128},{96,160},{128,192},{160,224},{192,0},{224,... | collective-permute-start | bytes 3145736 | tf_op jit(solution)/shard_map/ppermute | solution.py:277
  2.3 0.7 collective-permute-start.1
  3.0 0.8 copy.14
  4.0 1.0 copy-done.1
  5.0 1.4 %pick_rows.1 = bf16[32,2,16,512]{3,2,1,0:T(8,128)(2,1)} custom-call(s32[512,1]{1,0:T(8,128)S(1)} %reshape.63.index_ref, bf16[2,256,512]{2,1,0:T(8,128)(2,1)S(1)} %copy-done.1), custom_call_target="tpu_custom_call" | custom-call | tf_op jit(solution)/shard_map/pick_rows/pallas_call | solution.py:323
  6.4 11.2 %all-to-all-start = ((bf16[32,2,16,512]{3,2,1,0:T(8,128)(2,1)}), bf16[32,2,16,512]{3,2,1,0:T(8,128)(2,1)}, u32[]{:S(2)}, u32[]{:S(2)}) async-start(bf16[32,2,16,512]{3,2,1,0:T(8,128)(2,1)} %pick_rows.1), calls=%async_computation | async-start | bytes 2097152 | tf_op jit(solution)/shard_map/all_to_all | solution.py:290
  17.7 8.2 %collective-permute-done.refs_6_ = bf16[2,512,512]{2,1,0:T(8,128)(2,1)S(1)} collective-permute-done((bf16[2,512,512]{2,1,0:T(8,128)(2,1)}, bf16[2,512,512]{2,1,0:T(8,128)(2,1)S(1)}, u32[]{:S(2)}, u32[]{:S(2)}) %collective-permute-start) | collective-permute-done | bytes 1048608 | tf_op jit(solution)/shard_map/ppermute | solution.py:277
  25.8 1.3 collective-permute-done.1.refs_2_
  27.1 1.3 broadcast_select_fusion
  28.4 1.3 collective-permute-start.3
  29.7 0.5 collective-permute-start.5
  30.2 1.4 %constant_dynamic-slice_fusion = (bf16[32,512]{1,0:T(8,128)(2,1)}, bf16[32,512]{1,0:T(8,128)(2,1)}) fusion(bf16[256,512]{1,0:T(8,128)(2,1)} %param.17, s32[]{:T(128)S(6)} %select_n.16, bf16[256,512]{1,0:T(8,128)(2,1)} %param.9), kind=kLoop, calls=%fused_computation.4 | loop fusion | bytes 131076 | tf_op jit(solution)/shard_map/dynamic_slice | solution.py:335
  32.8 1.9 %count_rows.1.counts_hbm = bf16[256,768]{1,0:T(8,128)(2,1)S(1)} custom-call(s32[256,16]{1,0:T(8,128)S(1)} %copy.16.neighbours_ref, f32[1,768]{1,0:T(1,128)S(1)} %pad_convert_fusion.live_ref), custom_call_target="tpu_custom_call" | custom-call | flops 2300000000 | bytes 4194304 | tf_op jit(solution)/shard_map/count_rows/pallas_call | solution.py:357
  34.7 0.7 copy-done.4
  35.4 11.4 %all-to-all-done.received_ref = bf16[32,2,16,512]{3,2,1,0:T(8,128)(2,1)} async-done(((bf16[32,2,16,512]{3,2,1,0:T(8,128)(2,1)}), bf16[32,2,16,512]{3,2,1,0:T(8,128)(2,1)}, u32[]{:S(2)}, u32[]{:S(2)}) %all-to-all-start) | async-done | bytes 1048608 | tf_op jit(solution)/shard_map/all_to_all | solution.py:290
  46.8 4.5 %neighbour_mean.1 = (bf16[2,256,256]{2,1,0:T(8,128)(2,1)}, bf16[2,256,256]{2,1,0:T(8,128)(2,1)}, bf16[8,80,512]{2,1,0:T(8,128)(2,1)}) custom-call(s32[1]{0:T(128)S(6)} %copy.17.depth_ref, s32[1]{0:T(128)} %bitcast.half_ref, bf16[32,2,16,512]{3,2,1,0:T(8,128)(2,1)} %all-to-all-done.received_ref, bf16[256,768]{1,0:T(8,128)(2,1)} %copy-done.4, ...), custom_call_target="tpu_custom_call" | custom-call | flops 2300000000 | bytes 4194304 | tf_op jit(solution)/shard_map/neighbour_mean/pallas_call | solution.py:374
  51.5 5.1 %all-to-all-start.1 = ((bf16[8,80,512]{2,1,0:T(8,128)(2,1)}), bf16[8,80,512]{2,1,0:T(8,128)(2,1)S(1)}, u32[]{:S(2)}, u32[]{:S(2)}) async-start(bf16[8,80,512]{2,1,0:T(8,128)(2,1)} %get-tuple-element.30), calls=%async_computation.1 | async-start | bytes 1310720 | tf_op jit(solution)/shard_map/all_to_all | solution.py:290
  56.6 2.3 %collective-permute-start.8 = (bf16[2,256,256]{2,1,0:T(8,128)(2,1)}, bf16[2,256,256]{2,1,0:T(8,128)(2,1)S(1)}, u32[]{:S(2)}, u32[]{:S(2)}) collective-permute-start(bf16[2,256,256]{2,1,0:T(8,128)(2,1)} %get-tuple-element.40), channel_id=1, source_target_pairs={{0,16},{8,24},{16,0},{24,8},{1,17},{9,25},{17,1},{25,9},{2,18},{10... | collective-permute-start | bytes 786440 | tf_op jit(solution)/shard_map/ppermute | solution.py:286
  58.9 2.4 %collective-permute-start.9 = (bf16[2,256,256]{2,1,0:T(8,128)(2,1)}, bf16[2,256,256]{2,1,0:T(8,128)(2,1)S(1)}, u32[]{:S(2)}, u32[]{:S(2)}) collective-permute-start(bf16[2,256,256]{2,1,0:T(8,128)(2,1)} %get-tuple-element.40), channel_id=1, source_target_pairs={{0,24},{8,16},{16,8},{24,0},{1,25},{9,17},{17,9},{25,1},{2,26},{10... | collective-permute-start | bytes 786440 | tf_op jit(solution)/shard_map/ppermute | solution.py:286
  61.3 5.6 %all-to-all-done.1.terms_hbm = bf16[8,80,512]{2,1,0:T(8,128)(2,1)S(1)} async-done(((bf16[8,80,512]{2,1,0:T(8,128)(2,1)}), bf16[8,80,512]{2,1,0:T(8,128)(2,1)S(1)}, u32[]{:S(2)}, u32[]{:S(2)}) %all-to-all-start.1) | async-done | bytes 655392 | tf_op jit(solution)/shard_map/all_to_all | solution.py:290
  66.9 0.8 copy-done.7
  67.7 0.4 copy-done.9
  68.2 13.5 %all_layers.1 = bf16[8,2,2,2,2,32,256]{6,5,4,3,2,1,0:T(8,128)(2,1)} custom-call(s32[1]{0:T(128)} %bitcast.2.segment_ref, bf16[32,512]{1,0:T(8,128)(2,1)} %get-tuple-element.27.features_ref, bf16[32,512]{1,0:T(8,128)(2,1)} %get-tuple-element.28.cotangent_ref, bf16[8,80,512]{2,1,0:T(8,128)(2,1)} %copy-done.7, bf16[2,512,512]{2,1,0:T(8,128)(2,1)} %refs_0_.1, ...), custom_call_target="tpu_custom_call" | custom-call | flops 14949999616 | bytes 4194304 | tf_op jit(solution)/shard_map/all_layers/pallas_call | solution.py:405
  81.7 5.3 %all-to-all-start.2 = ((bf16[32,2,2,32,256]{4,3,2,1,0:T(8,128)(2,1)}), bf16[32,2,2,32,256]{4,3,2,1,0:T(8,128)(2,1)S(1)}, u32[]{:S(2)}, u32[]{:S(2)}) async-start(bf16[32,2,2,32,256]{4,3,2,1,0:T(8,128)(2,1)} %bitcast.8), calls=%async_computation.2 | async-start | bytes 4194304 | tf_op jit(solution)/shard_map/all_to_all | solution.py:290
  87.0 27.3 %all-to-all-done.2 = bf16[32,2,2,32,256]{4,3,2,1,0:T(8,128)(2,1)S(1)} async-done(((bf16[32,2,2,32,256]{4,3,2,1,0:T(8,128)(2,1)}), bf16[32,2,2,32,256]{4,3,2,1,0:T(8,128)(2,1)S(1)}, u32[]{:S(2)}, u32[]{:S(2)}) %all-to-all-start.2) | async-done | bytes 2097184 | tf_op jit(solution)/shard_map/all_to_all | solution.py:290
  114.3 1.6 %weight_products.1 = (bf16[16,2,2,16,256]{4,3,2,1,0:T(8,128)(2,1)}, bf16[8,2,32,256]{3,2,1,0:T(8,128)(2,1)S(1)}, bf16[8,2,32,256]{3,2,1,0:T(8,128)(2,1)S(1)}) custom-call(s32[1]{0:T(128)} %bitcast.1.place_ref, bf16[8,4,2,2,32,256]{5,4,3,2,1,0:T(8,128)(2,1)S(1)} %bitcast.6, bf16[2,256,256]{2,1,0:T(8,128)(2,1)S(1)} %copy-done.2, ...), custom_call_target="tpu_custom_call" | custom-call | flops 3449999872 | bytes 4194304 | tf_op jit(solution)/shard_map/weight_products/pallas_call | solution.py:434
  116.0 0.7 copy-done.3
  116.7 3.9 %all-to-all-start.3 = ((bf16[16,2,2,16,256]{4,3,2,1,0:T(8,128)(2,1)}), bf16[16,2,2,16,256]{4,3,2,1,0:T(8,128)(2,1)S(1)}, u32[]{:S(2)}, u32[]{:S(2)}) async-start(bf16[16,2,2,16,256]{4,3,2,1,0:T(8,128)(2,1)} %get-tuple-element.45), calls=%async_computation.3 | async-start | bytes 1048576 | tf_op jit(solution)/shard_map/all_to_all | solution.py:290
  120.6 2.0 %collective-permute-start.10 = (bf16[8,2,32,256]{3,2,1,0:T(8,128)(2,1)}, bf16[8,2,32,256]{3,2,1,0:T(8,128)(2,1)S(1)}, u32[]{:S(2)}, u32[]{:S(2)}) collective-permute-start(bf16[8,2,32,256]{3,2,1,0:T(8,128)(2,1)} %copy-done.3), channel_id=1, source_target_pairs={{0,16},{8,24},{16,0},{24,8},{1,17},{9,25},{17,1},{25,9},{2,18},{10... | collective-permute-start | bytes 786440 | tf_op jit(solution)/shard_map/ppermute | solution.py:286
  122.6 11.4 %collective-permute-done.10.missing_ref = bf16[8,2,32,256]{3,2,1,0:T(8,128)(2,1)S(1)} collective-permute-done((bf16[8,2,32,256]{3,2,1,0:T(8,128)(2,1)}, bf16[8,2,32,256]{3,2,1,0:T(8,128)(2,1)S(1)}, u32[]{:S(2)}, u32[]{:S(2)}) %collective-permute-start.10) | collective-permute-done | bytes 262176 | tf_op jit(solution)/shard_map/ppermute | solution.py:286
  134.0 1.8 %all-to-all-done.3 = bf16[16,2,2,16,256]{4,3,2,1,0:T(8,128)(2,1)S(1)} async-done(((bf16[16,2,2,16,256]{4,3,2,1,0:T(8,128)(2,1)}), bf16[16,2,2,16,256]{4,3,2,1,0:T(8,128)(2,1)S(1)}, u32[]{:S(2)}, u32[]{:S(2)}) %all-to-all-start.3) | async-done | bytes 524320 | tf_op jit(solution)/shard_map/all_to_all | solution.py:290
  135.8 0.9 finish.1
  (33 shorter events, 0.8 us)
Async XLA Ops:
  0.6 31.1 %copy-start = (s32[32,32]{1,0:T(8,128)S(1)}, s32[32,32]{1,0:T(8,128)}, u32[]{:S(2)}) copy-start(s32[32,32]{1,0:T(8,128)} %param.15) | copy-start | bytes 12292
  0.6 25.2 %collective-permute-start = (bf16[2,512,512]{2,1,0:T(8,128)(2,1)}, bf16[2,512,512]{2,1,0:T(8,128)(2,1)S(1)}, u32[]{:S(2)}, u32[]{:S(2)}) collective-permute-start(bf16[2,512,512]{2,1,0:T(8,128)(2,1)} %refs_0_.1), channel_id=1, source_target_pairs={{0,64},{32,96},{64,128},{96,160},{128,192},{160,224},{192,0},{224,... | collective-permute-start | bytes 3145736 | tf_op jit(solution)/shard_map/ppermute | solution.py:277
  2.3 24.8 %collective-permute-start.1 = (bf16[2,512,512]{2,1,0:T(8,128)(2,1)}, bf16[2,512,512]{2,1,0:T(8,128)(2,1)S(1)}, u32[]{:S(2)}, u32[]{:S(2)}) collective-permute-start(bf16[2,512,512]{2,1,0:T(8,128)(2,1)} %refs_0_.1), channel_id=1, source_target_pairs={{0,192},{32,224},{64,0},{96,32},{128,64},{160,96},{192,128},{224,1... | collective-permute-start | bytes 3145736 | tf_op jit(solution)/shard_map/ppermute | solution.py:277
  3.0 24.1 %collective-permute-start.2 = (bf16[2,512,512]{2,1,0:T(8,128)(2,1)}, bf16[2,512,512]{2,1,0:T(8,128)(2,1)}, u32[]{:S(2)}, u32[]{:S(2)}) collective-permute-start(bf16[2,512,512]{2,1,0:T(8,128)(2,1)} %refs_0_.1), channel_id=1, source_target_pairs={{0,32},{32,0},{64,96},{96,64},{128,160},{160,128},{192,224},{224,1... | collective-permute-start | bytes 3145736 | tf_op jit(solution)/shard_map/ppermute | solution.py:282
  3.9 1.0 copy-start.1
  6.4 40.4 %all-to-all-start = ((bf16[32,2,16,512]{3,2,1,0:T(8,128)(2,1)}), bf16[32,2,16,512]{3,2,1,0:T(8,128)(2,1)}, u32[]{:S(2)}, u32[]{:S(2)}) async-start(bf16[32,2,16,512]{3,2,1,0:T(8,128)(2,1)} %pick_rows.1), calls=%async_computation | async-start | bytes 2097152 | tf_op jit(solution)/shard_map/all_to_all | solution.py:290
  17.6 14.0 %copy-start.8 = (s32[256,16]{0,1:T(8,128)S(1)}, s32[256,16]{0,1:T(8,128)}, u32[]{:S(2)}) copy-start(s32[256,16]{0,1:T(8,128)} %param.16) | copy-start | bytes 49156
  25.8 8.8 %copy-start.5 = (bf16[2,512,512]{2,1,0:T(8,128)(2,1)}, bf16[2,512,512]{2,1,0:T(8,128)(2,1)S(1)}, u32[]{:S(2)}) copy-start(bf16[2,512,512]{2,1,0:T(8,128)(2,1)S(1)} %collective-permute-done.refs_6_) | copy-start | bytes 3145732
  27.1 7.5 %copy-start.6 = (bf16[2,512,512]{2,1,0:T(8,128)(2,1)}, bf16[2,512,512]{2,1,0:T(8,128)(2,1)S(1)}, u32[]{:S(2)}) copy-start(bf16[2,512,512]{2,1,0:T(8,128)(2,1)S(1)} %collective-permute-done.1.refs_2_) | copy-start | bytes 3145732
  28.4 22.9 %collective-permute-start.3 = (bf16[2,512,512]{2,1,0:T(8,128)(2,1)}, bf16[2,512,512]{2,1,0:T(8,128)(2,1)}, u32[]{:S(2)}, u32[]{:S(2)}) collective-permute-start(bf16[2,512,512]{2,1,0:T(8,128)(2,1)} %broadcast_select_fusion), channel_id=1, source_target_pairs={{0,64},{32,224},{64,128},{96,32},{128,192},{160,96},{192,0},{224,1... | collective-permute-start | bytes 3145736 | tf_op jit(solution)/shard_map/ppermute | solution.py:277
  29.7 21.6 %collective-permute-start.4 = (bf16[2,512,512]{2,1,0:T(8,128)(2,1)S(1)}, bf16[2,512,512]{2,1,0:T(8,128)(2,1)}, u32[]{:S(2)}, u32[]{:S(2)}) collective-permute-start(bf16[2,512,512]{2,1,0:T(8,128)(2,1)S(1)} %collective-permute-done.1.refs_2_), channel_id=1, source_target_pairs={{0,32},{32,0},{64,96},{96,64},{128,160},{160,128},{192,224},{224,1... | collective-permute-start | bytes 3145736 | tf_op jit(solution)/shard_map/ppermute | solution.py:282
  29.7 21.6 %collective-permute-start.5 = (bf16[2,512,512]{2,1,0:T(8,128)(2,1)S(1)}, bf16[2,512,512]{2,1,0:T(8,128)(2,1)}, u32[]{:S(2)}, u32[]{:S(2)}) collective-permute-start(bf16[2,512,512]{2,1,0:T(8,128)(2,1)S(1)} %collective-permute-done.refs_6_), channel_id=1, source_target_pairs={{0,32},{32,0},{64,96},{96,64},{128,160},{160,128},{192,224},{224,1... | collective-permute-start | bytes 3145736 | tf_op jit(solution)/shard_map/ppermute | solution.py:282
  34.7 0.7 copy-start.4
  51.4 15.5 %collective-permute-start.6 = (bf16[2,512,512]{2,1,0:T(8,128)(2,1)}, bf16[2,512,512]{2,1,0:T(8,128)(2,1)S(1)}, u32[]{:S(2)}, u32[]{:S(2)}) collective-permute-start(bf16[2,512,512]{2,1,0:T(8,128)(2,1)} %collective-permute-done.3.refs_4_), channel_id=1, source_target_pairs={{0,32},{32,0},{64,96},{96,64},{128,160},{160,128},{192,224},{224,1... | collective-permute-start | bytes 3145736 | tf_op jit(solution)/shard_map/ppermute | solution.py:282
  51.5 15.4 %all-to-all-start.1 = ((bf16[8,80,512]{2,1,0:T(8,128)(2,1)}), bf16[8,80,512]{2,1,0:T(8,128)(2,1)S(1)}, u32[]{:S(2)}, u32[]{:S(2)}) async-start(bf16[8,80,512]{2,1,0:T(8,128)(2,1)} %get-tuple-element.30), calls=%async_computation.1 | async-start | bytes 1310720 | tf_op jit(solution)/shard_map/all_to_all | solution.py:290
  56.6 25.1 %collective-permute-start.7 = (bf16[2,256,256]{2,1,0:T(8,128)(2,1)}, bf16[2,256,256]{2,1,0:T(8,128)(2,1)S(1)}, u32[]{:S(2)}, u32[]{:S(2)}) collective-permute-start(bf16[2,256,256]{2,1,0:T(8,128)(2,1)} %get-tuple-element.35.mean0), channel_id=1, source_target_pairs={{0,8},{8,0},{16,24},{24,16},{1,9},{9,1},{17,25},{25,17},{2,10},{10... | collective-permute-start | bytes 786440 | tf_op jit(solution)/shard_map/ppermute | solution.py:286
  56.6 25.1 %collective-permute-start.8 = (bf16[2,256,256]{2,1,0:T(8,128)(2,1)}, bf16[2,256,256]{2,1,0:T(8,128)(2,1)S(1)}, u32[]{:S(2)}, u32[]{:S(2)}) collective-permute-start(bf16[2,256,256]{2,1,0:T(8,128)(2,1)} %get-tuple-element.40), channel_id=1, source_target_pairs={{0,16},{8,24},{16,0},{24,8},{1,17},{9,25},{17,1},{25,9},{2,18},{10... | collective-permute-start | bytes 786440 | tf_op jit(solution)/shard_map/ppermute | solution.py:286
  58.9 22.8 %collective-permute-start.9 = (bf16[2,256,256]{2,1,0:T(8,128)(2,1)}, bf16[2,256,256]{2,1,0:T(8,128)(2,1)S(1)}, u32[]{:S(2)}, u32[]{:S(2)}) collective-permute-start(bf16[2,256,256]{2,1,0:T(8,128)(2,1)} %get-tuple-element.40), channel_id=1, source_target_pairs={{0,24},{8,16},{16,8},{24,0},{1,25},{9,17},{17,9},{25,1},{2,26},{10... | collective-permute-start | bytes 786440 | tf_op jit(solution)/shard_map/ppermute | solution.py:286
  66.9 0.8 copy-start.7
  66.9 1.2 copy-start.9
  81.7 32.6 %copy-start.2 = (bf16[2,256,256]{2,1,0:T(8,128)(2,1)S(1)}, bf16[2,256,256]{2,1,0:T(8,128)(2,1)}, u32[]{:S(2)}) copy-start(bf16[2,256,256]{2,1,0:T(8,128)(2,1)} %get-tuple-element.35.mean0) | copy-start | bytes 786436
  81.7 32.6 %all-to-all-start.2 = ((bf16[32,2,2,32,256]{4,3,2,1,0:T(8,128)(2,1)}), bf16[32,2,2,32,256]{4,3,2,1,0:T(8,128)(2,1)S(1)}, u32[]{:S(2)}, u32[]{:S(2)}) async-start(bf16[32,2,2,32,256]{4,3,2,1,0:T(8,128)(2,1)} %bitcast.8), calls=%async_computation.2 | async-start | bytes 4194304 | tf_op jit(solution)/shard_map/all_to_all | solution.py:290
  116.0 0.7 copy-start.3
  116.7 19.1 %all-to-all-start.3 = ((bf16[16,2,2,16,256]{4,3,2,1,0:T(8,128)(2,1)}), bf16[16,2,2,16,256]{4,3,2,1,0:T(8,128)(2,1)S(1)}, u32[]{:S(2)}, u32[]{:S(2)}) async-start(bf16[16,2,2,16,256]{4,3,2,1,0:T(8,128)(2,1)} %get-tuple-element.45), calls=%async_computation.3 | async-start | bytes 1048576 | tf_op jit(solution)/shard_map/all_to_all | solution.py:290
  120.6 13.4 %collective-permute-start.10 = (bf16[8,2,32,256]{3,2,1,0:T(8,128)(2,1)}, bf16[8,2,32,256]{3,2,1,0:T(8,128)(2,1)S(1)}, u32[]{:S(2)}, u32[]{:S(2)}) collective-permute-start(bf16[8,2,32,256]{3,2,1,0:T(8,128)(2,1)} %copy-done.3), channel_id=1, source_target_pairs={{0,16},{8,24},{16,0},{24,8},{1,17},{9,25},{17,1},{25,9},{2,18},{10... | collective-permute-start | bytes 786440 | tf_op jit(solution)/shard_map/ppermute | solution.py:286

commit v4 on v3

--- a/solution.py
+++ b/solution.py
@@ -14,6 +14,8 @@
 BF16 = jnp.bfloat16
 F32 = jnp.float32
 MIB = 1024 * 1024
+INACTIVE = 1e30
+AHEAD = 3
 
 
 def matmul(a, b):
@@ -57,9 +59,9 @@
 
 
 def mean_kernel(
-    depth_ref, half_ref, received_ref, counts_hbm, history_hbm, weight_hbm,
+    depth_ref, half_ref, received_hbm, counts_hbm, history_hbm, weight_hbm,
     mine_hbm, others_hbm, term_hbm,
-    counts_ref, history_ref, weight_ref, mine_ref, others_ref, term_ref, sems, *, fanout,
+    received_ref, counts_ref, history_ref, weight_ref, mine_ref, others_ref, term_ref, sems, *, fanout,
 ):
     slots, nodes, width = history_ref.shape
     segments = term_ref.shape[0]
@@ -67,31 +69,36 @@
     loads = [
         pltpu.make_async_copy(hbm, ref, sems.at[i])
         for i, (hbm, ref) in enumerate(
-            ((counts_hbm, counts_ref), (history_hbm, history_ref), (weight_hbm, weight_ref))
+            (
+                (counts_hbm, counts_ref),
+                (received_hbm, received_ref),
+                (history_hbm, history_ref),
+                (weight_hbm, weight_ref),
+            )
         )
     ]
     for load in loads:
         load.start()
-    flag = depth_ref[0].astype(F32)
-    tail = term_ref.shape[1] - slots * part
-    term_ref[:, slots * part :] = jnp.full((segments, tail, width), flag, F32).astype(BF16)
     loads[0].wait()
+    loads[1].wait()
     far = [
         matmul(counts_ref[:, nodes:], received_ref[:, slot].reshape(-1, width))
         for slot in range(slots)
     ]
-    loads[1].wait()
+    loads[2].wait()
     means = [
         ((far[slot] + matmul(counts_ref[:, :nodes], history_ref[slot])) * (1.0 / fanout)).astype(
             BF16
         )
         for slot in range(slots)
     ]
-    loads[2].wait()
+    loads[3].wait()
     for slot in range(slots):
         term = matmul(means[slot], weight_ref[slot]).astype(BF16)
+        if slot:
+            term = jnp.where(slot < depth_ref[0], term, jnp.full_like(term, INACTIVE))
         term_ref[:, slot * part : (slot + 1) * part] = term.reshape(segments, part, width)
-    stores = [pltpu.make_async_copy(term_ref, term_hbm, sems.at[3])]
+    stores = [pltpu.make_async_copy(term_ref, term_hbm, sems.at[4])]
     stores[0].start()
     for half in range(2):
 
@@ -102,8 +109,8 @@
                 mine_ref[slot] = mean[:, half * width // 2 : (half + 1) * width // 2]
                 others_ref[slot] = mean[:, (1 - half) * width // 2 : (2 - half) * width // 2]
 
-    stores.append(pltpu.make_async_copy(mine_ref, mine_hbm, sems.at[4]))
-    stores.append(pltpu.make_async_copy(others_ref, others_hbm, sems.at[5]))
+    stores.append(pltpu.make_async_copy(mine_ref, mine_hbm, sems.at[5]))
+    stores.append(pltpu.make_async_copy(others_ref, others_hbm, sems.at[6]))
     for store in stores[1:]:
         store.start()
     for store in stores:
@@ -115,32 +122,30 @@
     return inverse, pre_norm * inverse
 
 
-def start_weights(segment_ref, pieces, weights, sems, order):
-    for segment in range(len(order) // SLOTS):
-
-        @pl.when(segment_ref[0] == segment)
-        def _():
-            for layer in order:
-                section = layer // SLOTS
-                ahead = (section // 2 - segment // 2) % 4
-                piece = pieces[ahead * 2 + (section + segment) % 2]
-                pltpu.make_async_copy(
-                    piece.at[layer % SLOTS], weights.at[layer], sems.at[layer]
-                ).start()
-
-
-def wait_weights(pieces, weights, sems, layer):
-    pltpu.make_async_copy(pieces[0].at[0], weights.at[layer], sems.at[layer]).wait()
+def start_weights(segment_ref, pieces, weights, sems, section):
+    mine = segment_ref[0]
+    ahead = lax.rem(section // 2 - mine // 2 + 4, 4)
+    index = ahead * 2 + lax.rem(section + mine, 2)
+    for at, piece in enumerate(pieces):
+
+        @pl.when(index == at)
+        def _():
+            weight_copy(piece, weights, sems, section).start()
+
+
+def weight_copy(piece, weights, sems, section):
+    slots = weights.at[pl.ds(section * SLOTS, SLOTS)]
+    return pltpu.make_async_copy(piece, slots, sems.at[section])
 
 
 def two_slots(terms_ref, section):
-    rows = terms_ref.shape[1]
-    return jnp.max(terms_ref[section, rows - 16 :, :128].astype(F32)) > 1.5
-
-
-def layers_kernel(segment_ref, features_ref, cotangent_ref, terms_hbm, *refs):
+    part = terms_ref.shape[1] // SLOTS
+    return jnp.max(terms_ref[section, part : part + 16, :128].astype(F32)) < INACTIVE / 2
+
+
+def layers_kernel(segment_ref, features_hbm, cotangent_hbm, terms_hbm, *refs):
     pieces, refs = refs[:8], refs[8:]
-    out_hbm, out_ref, terms_ref, state, weights, pre, sems, term_sems, out_sems = refs
+    out_hbm, out_ref, terms_ref, state, cotangent, weights, pre, sems, term_sems, out_sems = refs
     segments, halves, _, _, slots, part, columns = out_ref.shape
     layers = segments * slots
 
@@ -154,11 +159,16 @@
             out_ref.at[section], out_hbm.at[section], out_sems.at[section]
         )
 
-    load_terms(0).start()
-    start_weights(segment_ref, pieces, weights, sems, range(layers))
-    for section in range(1, segments):
+    my_rows = pl.ds(pl.multiple_of(segment_ref[0] * part, part), part)
+    load_features = pltpu.make_async_copy(features_hbm.at[my_rows], state, out_sems.at[0])
+    load_cotangent = pltpu.make_async_copy(cotangent_hbm.at[my_rows], cotangent, out_sems.at[1])
+    load_features.start()
+    for section in range(AHEAD):
+        start_weights(segment_ref, pieces, weights, sems, section)
+    for section in range(segments):
         load_terms(section).start()
-    state[...] = features_ref[...]
+    load_cotangent.start()
+    load_features.wait()
 
     def keep_input(section, slot):
         x = state[...]
@@ -174,29 +184,34 @@
         ].astype(F32)
         pre[layer] = pre_norm
         _, normed = normalize(pre_norm)
-        state[...] = (x.astype(F32) + normed * jax.nn.sigmoid(normed)).astype(BF16)
-
-    @pl.loop(0, segments)
+        state[...] = (x.astype(F32) + normed * (0.5 + 0.5 * jnp.tanh(0.5 * normed))).astype(BF16)
+
+    @pl.loop(0, segments, unroll=8)
     def _(section):
         load_terms(section).wait()
         both = two_slots(terms_ref, section)
-        wait_weights(pieces, weights, sems, section * slots)
+        weight_copy(pieces[0], weights, sems, section).wait()
+
+        @pl.when(section + AHEAD < segments)
+        def _():
+            start_weights(segment_ref, pieces, weights, sems, section + AHEAD)
+
         keep_input(section, 0)
         forward(section, 0)
-        wait_weights(pieces, weights, sems, section * slots + 1)
         keep_input(section, 1)
 
         @pl.when(both)
         def _():
             forward(section, 1)
 
-    state[...] = cotangent_ref[...]
+    load_cotangent.wait()
+    state[...] = cotangent[...]
 
     def backward(section, slot):
         layer = section * slots + slot
         inverse, normed = normalize(pre[layer])
         grad_out = state[...].astype(F32)
-        sigmoid = jax.nn.sigmoid(normed)
+        sigmoid = (0.5 + 0.5 * jnp.tanh(0.5 * normed))
         grad_normed = grad_out * sigmoid * (1.0 + normed * (1.0 - sigmoid))
         grad_pre = inverse * (
             grad_normed - normed * jnp.mean(grad_normed * normed, axis=-1, keepdims=True)
@@ -210,7 +225,7 @@
         )
         state[...] = (grad_out + back).astype(BF16)
 
-    @pl.loop(0, segments)
+    @pl.loop(0, segments, unroll=8)
     def _(step):
         section = segments - 1 - step
         both = two_slots(terms_ref, section)
@@ -328,12 +343,6 @@
     )(send_index.reshape(received_rows, 1), history)
     received = exchange(outgoing, ("xa", "xb", "z"))
 
-    own_rows = functools.partial(
-        lax.dynamic_slice_in_dim, start_index=lax.axis_index("segment") * part, slice_size=part
-    )
-    my_features, my_cotangent, neighbours = lax.optimization_barrier(
-        (own_rows(features), own_rows(cotangent), neighbours)
-    )
     last_w, next_w, other_w, token = lax.optimization_barrier(
         (last_w, next_w, core_swap(weight_self), depth.reshape(1, 1))
     )
@@ -369,20 +378,21 @@
     far_w = round_y(forwarded, lambda core: 1 - 2 * core)
     next_other, last_other = core_swap(next_w), core_swap(last_w)
 
-    term_rows = slots * part + 16
+    term_rows = slots * part
     half_shape = jax.ShapeDtypeStruct((slots, nodes, columns), BF16)
     mean, others_mean, terms = pl.pallas_call(
         functools.partial(mean_kernel, fanout=fanout),
-        in_specs=[smem, smem, vmem, hbm, hbm, hbm],
+        in_specs=[smem, smem, hbm, hbm, hbm, hbm],
         out_specs=(hbm, hbm, hbm),
         scratch_shapes=[
+            pltpu.VMEM(received.shape, BF16),
             pltpu.VMEM(counts_shape, BF16),
             pltpu.VMEM(history.shape, BF16),
             pltpu.VMEM(weight_neigh.shape, BF16),
             pltpu.VMEM(half_shape.shape, BF16),
             pltpu.VMEM(half_shape.shape, BF16),
             pltpu.VMEM((segments, term_rows, width), BF16),
-            pltpu.SemaphoreType.DMA((6,)),
+            pltpu.SemaphoreType.DMA((7,)),
         ],
         out_shape=(
             half_shape,
@@ -404,23 +414,24 @@
     anywhere = pl.BlockSpec(memory_space=pl.ANY)
     rows = pl.pallas_call(
         layers_kernel,
-        in_specs=[smem, vmem, vmem, anywhere] + [anywhere] * len(pieces),
+        in_specs=[smem] + [anywhere] * (3 + len(pieces)),
         out_specs=anywhere,
         out_shape=jax.ShapeDtypeStruct((segments, 2, 2, 2, slots, part, columns), BF16),
         scratch_shapes=[
             pltpu.VMEM((segments, 2, 2, 2, slots, part, columns), BF16),
             pltpu.VMEM((segments, term_rows, width), BF16),
             pltpu.VMEM((part, width), BF16),
+            pltpu.VMEM((part, width), BF16),
             pltpu.VMEM((layers, width, width), BF16),
             pltpu.VMEM((layers, part, width), F32),
-            pltpu.SemaphoreType.DMA((layers,)),
+            pltpu.SemaphoreType.DMA((segments,)),
             pltpu.SemaphoreType.DMA((segments,)),
             pltpu.SemaphoreType.DMA((segments,)),
         ],
-        compiler_params=params(60),
+        compiler_params=params(57.5),
         cost_estimate=lasting(13),
         name="all_layers",
-    )(my_segment, my_features, my_cotangent, all_terms, *pieces)
+    )(my_segment, features, cotangent, all_terms, *pieces)
     rows, *other_means = lax.optimization_barrier(
         (rows, x_swap(mean, 1), x_swap(others_mean, 2), x_swap(others_mean, 3))
     )

time: 139 us -> 134 us (0.964)
  Pallas kernels: 23.9 us -> 19.7 us
  local copies, waits for them, and re-layouts: 6.46 us -> 5.04 us
    pallas_call x1, Pallas kernels: 13.5 us -> 10.3 us  [body(): pl.pallas_call(layers_kernel, in_specs=[smem] + [anywhere] * (3 + len(pie...]
    dynamic_slice x1 -> x0, local copies, waits for them, and re-layouts: 1.4 us -> none  [body(): own_rows(cotangent)]
    unnamed x21 -> x24, local copies, waits for them, and re-layouts: 4.52 us -> 4.61 us
  transfers between devices with their start and end apart: 15 -> 15, of which waited for: 7 -> 7; matrix products, arithmetic and copies ran while one was open for 3% -> 2% of each run, Pallas kernels for 16% -> 13%
where the time goes in v4:
time: 134 us; the launch traced here: 131 us
  waiting for transfers between devices  67 us (50%)
  starting transfers between devices  36.4 us (27%)
  Pallas kernels  19.7 us (15%)
  local copies, waits for them, and re-layouts  5.04 us (4%)
  between operations  1.52 us (1%)
  other arithmetic  1.39 us (1%)
    all_to_all x4, waiting for transfers between devices, exchange(): return lax.all_to_all(block, axes, split_axis=0, concat_axis=0, tiled=True)  46.1 us
    all_to_all x4, starting transfers between devices, exchange(): return lax.all_to_all(block, axes, split_axis=0, concat_axis=0, tiled=True)  25.4 us
    ppermute x4, waiting for transfers between devices, x_swap(): lax.ppermute(block, ('xa', 'xb'), [(i, i ^ step) for i in range(PAIR * PA...  11.4 us
    pallas_call x1, Pallas kernels, body(): pl.pallas_call(layers_kernel, in_specs=[smem] + [anywhere] * (3 + len(pie...  10.3 us
    ppermute x3, waiting for transfers between devices, round_y(): return lax.ppermute(block, 'segment', route)  9.48 us
    ppermute x4, starting transfers between devices, x_swap(): lax.ppermute(block, ('xa', 'xb'), [(i, i ^ step) for i in range(PAIR * PA...  6.71 us
    unnamed x24, local copies, waits for them, and re-layouts  4.61 us
    ppermute x3, starting transfers between devices, round_y(): return lax.ppermute(block, 'segment', route)  3.64 us
  transfers between devices with their start and end apart: 15, of which 7 were waited for; matrix products, arithmetic and copies ran while one was open for 2% of the time, Pallas kernels for 13%

profile of v4, /device:TPU:8, one launch (start us, length us, event | category | flops | bytes accessed | tf_op | source)
XLA Modules:
  0.0 131.1 jit_solution(16344635379661975508)
XLA Ops:
  0.6 1.7 %collective-permute-start = (bf16[2,512,512]{2,1,0:T(8,128)(2,1)}, bf16[2,512,512]{2,1,0:T(8,128)(2,1)S(1)}, u32[]{:S(2)}, u32[]{:S(2)}) collective-permute-start(bf16[2,512,512]{2,1,0:T(8,128)(2,1)} %refs_0_.1), channel_id=1, source_target_pairs={{0,64},{32,96},{64,128},{96,160},{128,192},{160,224},{192,0},{224,... | collective-permute-start | bytes 3145736 | tf_op jit(solution)/shard_map/ppermute | solution.py:292
  2.3 0.7 collective-permute-start.1
  3.0 0.8 copy.14
  4.0 1.0 copy-done.1
  5.0 1.4 %pick_rows.1 = bf16[32,2,16,512]{3,2,1,0:T(8,128)(2,1)} custom-call(s32[512,1]{1,0:T(8,128)S(1)} %reshape.63.index_ref, bf16[2,256,512]{2,1,0:T(8,128)(2,1)S(1)} %copy-done.1), custom_call_target="tpu_custom_call" | custom-call | tf_op jit(solution)/shard_map/pick_rows/pallas_call | solution.py:338
  6.4 11.2 %all-to-all-start = ((bf16[32,2,16,512]{3,2,1,0:T(8,128)(2,1)}), bf16[32,2,16,512]{3,2,1,0:T(8,128)(2,1)}, u32[]{:S(2)}, u32[]{:S(2)}) async-start(bf16[32,2,16,512]{3,2,1,0:T(8,128)(2,1)} %pick_rows.1), calls=%async_computation | async-start | bytes 2097152 | tf_op jit(solution)/shard_map/all_to_all | solution.py:305
  17.7 8.2 %collective-permute-done.refs_6_ = bf16[2,512,512]{2,1,0:T(8,128)(2,1)S(1)} collective-permute-done((bf16[2,512,512]{2,1,0:T(8,128)(2,1)}, bf16[2,512,512]{2,1,0:T(8,128)(2,1)S(1)}, u32[]{:S(2)}, u32[]{:S(2)}) %collective-permute-start) | collective-permute-done | bytes 1048608 | tf_op jit(solution)/shard_map/ppermute | solution.py:292
  25.8 1.3 collective-permute-done.1.refs_2_
  27.1 1.3 %broadcast_select_fusion = bf16[2,512,512]{2,1,0:T(8,128)(2,1)} fusion(bf16[2,512,512]{2,1,0:T(8,128)(2,1)S(1)} %collective-permute-done.refs_6_, bf16[2,512,512]{2,1,0:T(8,128)(2,1)S(1)} %collective-permute-done.1.refs_2_, pred[]{:T(512)S(6)} %eq.3), kind=kLoop, calls=%fused_computation | loop fusion | flops 524288 | bytes 3145729 | tf_op jit(solution)/shard_map/jit(_where)/select_n | solution.py:377
  28.4 1.3 collective-permute-start.3
  29.7 0.5 collective-permute-start.5
  30.2 0.2 dynamic-slice_reduce_fusion
  31.4 1.9 %count_rows.1.counts_hbm = bf16[256,768]{1,0:T(8,128)(2,1)S(1)} custom-call(s32[256,16]{1,0:T(8,128)S(1)} %copy.16.neighbours_ref, f32[1,768]{1,0:T(1,128)S(1)} %pad_convert_fusion.live_ref), custom_call_target="tpu_custom_call" | custom-call | flops 2300000000 | bytes 4194304 | tf_op jit(solution)/shard_map/count_rows/pallas_call | solution.py:366
  33.3 0.7 copy-done.4
  34.0 12.8 %all-to-all-done.received_hbm = bf16[32,2,16,512]{3,2,1,0:T(8,128)(2,1)} async-done(((bf16[32,2,16,512]{3,2,1,0:T(8,128)(2,1)}), bf16[32,2,16,512]{3,2,1,0:T(8,128)(2,1)}, u32[]{:S(2)}, u32[]{:S(2)}) %all-to-all-start) | async-done | bytes 1048608 | tf_op jit(solution)/shard_map/all_to_all | solution.py:305
  46.8 3.5 %neighbour_mean.1 = (bf16[2,256,256]{2,1,0:T(8,128)(2,1)}, bf16[2,256,256]{2,1,0:T(8,128)(2,1)}, bf16[8,64,512]{2,1,0:T(8,128)(2,1)}) custom-call(s32[1]{0:T(128)S(6)} %copy.17.depth_ref, s32[1]{0:T(128)} %bitcast.half_ref, bf16[32,2,16,512]{3,2,1,0:T(8,128)(2,1)} %all-to-all-done.received_hbm, bf16[256,768]{1,0:T(8,128)(2,1)} %copy-done.4, ...), custom_call_target="tpu_custom_call" | custom-call | flops 2300000000 | bytes 4194304 | tf_op jit(solution)/shard_map/neighbour_mean/pallas_call | solution.py:383
  50.5 5.1 %all-to-all-start.1 = ((bf16[8,64,512]{2,1,0:T(8,128)(2,1)}), bf16[8,64,512]{2,1,0:T(8,128)(2,1)S(1)}, u32[]{:S(2)}, u32[]{:S(2)}) async-start(bf16[8,64,512]{2,1,0:T(8,128)(2,1)} %get-tuple-element.24), calls=%async_computation.1 | async-start | bytes 1048576 | tf_op jit(solution)/shard_map/all_to_all | solution.py:305
  55.6 2.3 %collective-permute-start.8 = (bf16[2,256,256]{2,1,0:T(8,128)(2,1)}, bf16[2,256,256]{2,1,0:T(8,128)(2,1)S(1)}, u32[]{:S(2)}, u32[]{:S(2)}) collective-permute-start(bf16[2,256,256]{2,1,0:T(8,128)(2,1)} %get-tuple-element.34), channel_id=1, source_target_pairs={{0,16},{8,24},{16,0},{24,8},{1,17},{9,25},{17,1},{25,9},{2,18},{10... | collective-permute-start | bytes 786440 | tf_op jit(solution)/shard_map/ppermute | solution.py:301
  57.8 2.4 %collective-permute-start.9 = (bf16[2,256,256]{2,1,0:T(8,128)(2,1)}, bf16[2,256,256]{2,1,0:T(8,128)(2,1)S(1)}, u32[]{:S(2)}, u32[]{:S(2)}) collective-permute-start(bf16[2,256,256]{2,1,0:T(8,128)(2,1)} %get-tuple-element.34), channel_id=1, source_target_pairs={{0,24},{8,16},{16,8},{24,0},{1,25},{9,17},{17,9},{25,1},{2,26},{10... | collective-permute-start | bytes 786440 | tf_op jit(solution)/shard_map/ppermute | solution.py:301
  60.3 4.2 %all-to-all-done.1.terms_hbm = bf16[8,64,512]{2,1,0:T(8,128)(2,1)S(1)} async-done(((bf16[8,64,512]{2,1,0:T(8,128)(2,1)}), bf16[8,64,512]{2,1,0:T(8,128)(2,1)S(1)}, u32[]{:S(2)}, u32[]{:S(2)}) %all-to-all-start.1) | async-done | bytes 524320 | tf_op jit(solution)/shard_map/all_to_all | solution.py:305
  64.5 0.8 copy-done.7
  65.3 0.4 copy-done.10
  65.7 10.3 %all_layers.1 = bf16[8,2,2,2,2,32,256]{6,5,4,3,2,1,0:T(8,128)(2,1)} custom-call(s32[1]{0:T(128)} %bitcast.2.segment_ref, bf16[256,512]{1,0:T(8,128)(2,1)} %features_hbm.1, bf16[256,512]{1,0:T(8,128)(2,1)} %cotangent_hbm.1, bf16[8,64,512]{2,1,0:T(8,128)(2,1)} %copy-done.7, bf16[2,512,512]{2,1,0:T(8,128)(2,1)} %refs_0_.1, bf16[2,512,512]{2,1,0:T(8,128)(2,1)} %copy-done.9, ...), custom_call_target="tpu_custom_call" | custom-call | flops 14949999616 | bytes 4194304 | tf_op jit(solution)/shard_map/all_layers/pallas_call | solution.py:415
  76.0 5.3 %all-to-all-start.2 = ((bf16[32,2,2,32,256]{4,3,2,1,0:T(8,128)(2,1)}), bf16[32,2,2,32,256]{4,3,2,1,0:T(8,128)(2,1)S(1)}, u32[]{:S(2)}, u32[]{:S(2)}) async-start(bf16[32,2,2,32,256]{4,3,2,1,0:T(8,128)(2,1)} %bitcast.8), calls=%async_computation.2 | async-start | bytes 4194304 | tf_op jit(solution)/shard_map/all_to_all | solution.py:305
  81.4 27.3 %all-to-all-done.2 = bf16[32,2,2,32,256]{4,3,2,1,0:T(8,128)(2,1)S(1)} async-done(((bf16[32,2,2,32,256]{4,3,2,1,0:T(8,128)(2,1)}), bf16[32,2,2,32,256]{4,3,2,1,0:T(8,128)(2,1)S(1)}, u32[]{:S(2)}, u32[]{:S(2)}) %all-to-all-start.2) | async-done | bytes 2097184 | tf_op jit(solution)/shard_map/all_to_all | solution.py:305
  108.7 1.6 %weight_products.1 = (bf16[16,2,2,16,256]{4,3,2,1,0:T(8,128)(2,1)}, bf16[8,2,32,256]{3,2,1,0:T(8,128)(2,1)S(1)}, bf16[8,2,32,256]{3,2,1,0:T(8,128)(2,1)S(1)}) custom-call(s32[1]{0:T(128)} %bitcast.1.place_ref, bf16[8,4,2,2,32,256]{5,4,3,2,1,0:T(8,128)(2,1)S(1)} %bitcast.6, bf16[2,256,256]{2,1,0:T(8,128)(2,1)S(1)} %copy-done.2, ...), custom_call_target="tpu_custom_call" | custom-call | flops 3449999872 | bytes 4194304 | tf_op jit(solution)/shard_map/weight_products/pallas_call | solution.py:445
  110.3 0.7 copy-done.3
  111.0 3.9 %all-to-all-start.3 = ((bf16[16,2,2,16,256]{4,3,2,1,0:T(8,128)(2,1)}), bf16[16,2,2,16,256]{4,3,2,1,0:T(8,128)(2,1)S(1)}, u32[]{:S(2)}, u32[]{:S(2)}) async-start(bf16[16,2,2,16,256]{4,3,2,1,0:T(8,128)(2,1)} %get-tuple-element.39), calls=%async_computation.3 | async-start | bytes 1048576 | tf_op jit(solution)/shard_map/all_to_all | solution.py:305
  114.9 2.0 %collective-permute-start.10 = (bf16[8,2,32,256]{3,2,1,0:T(8,128)(2,1)}, bf16[8,2,32,256]{3,2,1,0:T(8,128)(2,1)S(1)}, u32[]{:S(2)}, u32[]{:S(2)}) collective-permute-start(bf16[8,2,32,256]{3,2,1,0:T(8,128)(2,1)} %copy-done.3), channel_id=1, source_target_pairs={{0,16},{8,24},{16,0},{24,8},{1,17},{9,25},{17,1},{25,9},{2,18},{10... | collective-permute-start | bytes 786440 | tf_op jit(solution)/shard_map/ppermute | solution.py:301
  116.9 11.4 %collective-permute-done.10.missing_ref = bf16[8,2,32,256]{3,2,1,0:T(8,128)(2,1)S(1)} collective-permute-done((bf16[8,2,32,256]{3,2,1,0:T(8,128)(2,1)}, bf16[8,2,32,256]{3,2,1,0:T(8,128)(2,1)S(1)}, u32[]{:S(2)}, u32[]{:S(2)}) %collective-permute-start.10) | collective-permute-done | bytes 262176 | tf_op jit(solution)/shard_map/ppermute | solution.py:301
  128.3 1.8 %all-to-all-done.3 = bf16[16,2,2,16,256]{4,3,2,1,0:T(8,128)(2,1)S(1)} async-done(((bf16[16,2,2,16,256]{4,3,2,1,0:T(8,128)(2,1)}), bf16[16,2,2,16,256]{4,3,2,1,0:T(8,128)(2,1)S(1)}, u32[]{:S(2)}, u32[]{:S(2)}) %all-to-all-start.3) | async-done | bytes 524320 | tf_op jit(solution)/shard_map/all_to_all | solution.py:305
  130.1 0.9 finish.1
  (34 shorter events, 0.6 us)
Async XLA Ops:
  0.6 29.6 %copy-start = (s32[32,32]{1,0:T(8,128)S(1)}, s32[32,32]{1,0:T(8,128)}, u32[]{:S(2)}) copy-start(s32[32,32]{1,0:T(8,128)} %param.15) | copy-start | bytes 12292
  0.6 25.2 %collective-permute-start = (bf16[2,512,512]{2,1,0:T(8,128)(2,1)}, bf16[2,512,512]{2,1,0:T(8,128)(2,1)S(1)}, u32[]{:S(2)}, u32[]{:S(2)}) collective-permute-start(bf16[2,512,512]{2,1,0:T(8,128)(2,1)} %refs_0_.1), channel_id=1, source_target_pairs={{0,64},{32,96},{64,128},{96,160},{128,192},{160,224},{192,0},{224,... | collective-permute-start | bytes 3145736 | tf_op jit(solution)/shard_map/ppermute | solution.py:292
  2.3 24.8 %collective-permute-start.1 = (bf16[2,512,512]{2,1,0:T(8,128)(2,1)}, bf16[2,512,512]{2,1,0:T(8,128)(2,1)S(1)}, u32[]{:S(2)}, u32[]{:S(2)}) collective-permute-start(bf16[2,512,512]{2,1,0:T(8,128)(2,1)} %refs_0_.1), channel_id=1, source_target_pairs={{0,192},{32,224},{64,0},{96,32},{128,64},{160,96},{192,128},{224,1... | collective-permute-start | bytes 3145736 | tf_op jit(solution)/shard_map/ppermute | solution.py:292
  3.0 24.1 %collective-permute-start.2 = (bf16[2,512,512]{2,1,0:T(8,128)(2,1)}, bf16[2,512,512]{2,1,0:T(8,128)(2,1)S(1)}, u32[]{:S(2)}, u32[]{:S(2)}) collective-permute-start(bf16[2,512,512]{2,1,0:T(8,128)(2,1)} %refs_0_.1), channel_id=1, source_target_pairs={{0,32},{32,0},{64,96},{96,64},{128,160},{160,128},{192,224},{224,1... | collective-permute-start | bytes 3145736 | tf_op jit(solution)/shard_map/ppermute | solution.py:297
  3.9 1.0 copy-start.1
  6.4 40.4 %all-to-all-start = ((bf16[32,2,16,512]{3,2,1,0:T(8,128)(2,1)}), bf16[32,2,16,512]{3,2,1,0:T(8,128)(2,1)}, u32[]{:S(2)}, u32[]{:S(2)}) async-start(bf16[32,2,16,512]{3,2,1,0:T(8,128)(2,1)} %pick_rows.1), calls=%async_computation | async-start | bytes 2097152 | tf_op jit(solution)/shard_map/all_to_all | solution.py:305
  17.6 13.0 %copy-start.8 = (s32[256,16]{0,1:T(8,128)S(1)}, s32[256,16]{0,1:T(8,128)}, u32[]{:S(2)}) copy-start(s32[256,16]{0,1:T(8,128)} %param.16) | copy-start | bytes 49156
  25.8 7.4 %copy-start.5 = (bf16[2,512,512]{2,1,0:T(8,128)(2,1)}, bf16[2,512,512]{2,1,0:T(8,128)(2,1)S(1)}, u32[]{:S(2)}) copy-start(bf16[2,512,512]{2,1,0:T(8,128)(2,1)S(1)} %collective-permute-done.refs_6_) | copy-start | bytes 3145732
  27.1 6.1 %copy-start.6 = (bf16[2,512,512]{2,1,0:T(8,128)(2,1)}, bf16[2,512,512]{2,1,0:T(8,128)(2,1)S(1)}, u32[]{:S(2)}) copy-start(bf16[2,512,512]{2,1,0:T(8,128)(2,1)S(1)} %collective-permute-done.1.refs_2_) | copy-start | bytes 3145732
  27.1 6.1 %copy-start.9 = (bf16[2,512,512]{2,1,0:T(8,128)(2,1)}, bf16[2,512,512]{2,1,0:T(8,128)(2,1)S(1)}, u32[]{:S(2)}) copy-start(bf16[2,512,512]{2,1,0:T(8,128)(2,1)S(1)} %collective-permute-done.2.refs_1_) | copy-start | bytes 3145732
  28.4 21.9 %collective-permute-start.3 = (bf16[2,512,512]{2,1,0:T(8,128)(2,1)}, bf16[2,512,512]{2,1,0:T(8,128)(2,1)}, u32[]{:S(2)}, u32[]{:S(2)}) collective-permute-start(bf16[2,512,512]{2,1,0:T(8,128)(2,1)} %broadcast_select_fusion), channel_id=1, source_target_pairs={{0,64},{32,224},{64,128},{96,32},{128,192},{160,96},{192,0},{224,1... | collective-permute-start | bytes 3145736 | tf_op jit(solution)/shard_map/ppermute | solution.py:292
  29.7 20.6 %collective-permute-start.4 = (bf16[2,512,512]{2,1,0:T(8,128)(2,1)S(1)}, bf16[2,512,512]{2,1,0:T(8,128)(2,1)}, u32[]{:S(2)}, u32[]{:S(2)}) collective-permute-start(bf16[2,512,512]{2,1,0:T(8,128)(2,1)S(1)} %collective-permute-done.1.refs_2_), channel_id=1, source_target_pairs={{0,32},{32,0},{64,96},{96,64},{128,160},{160,128},{192,224},{224,1... | collective-permute-start | bytes 3145736 | tf_op jit(solution)/shard_map/ppermute | solution.py:297
  29.7 20.6 %collective-permute-start.5 = (bf16[2,512,512]{2,1,0:T(8,128)(2,1)S(1)}, bf16[2,512,512]{2,1,0:T(8,128)(2,1)}, u32[]{:S(2)}, u32[]{:S(2)}) collective-permute-start(bf16[2,512,512]{2,1,0:T(8,128)(2,1)S(1)} %collective-permute-done.refs_6_), channel_id=1, source_target_pairs={{0,32},{32,0},{64,96},{96,64},{128,160},{160,128},{192,224},{224,1... | collective-permute-start | bytes 3145736 | tf_op jit(solution)/shard_map/ppermute | solution.py:297
  33.3 0.8 copy-start.4
  50.4 14.1 %collective-permute-start.6 = (bf16[2,512,512]{2,1,0:T(8,128)(2,1)}, bf16[2,512,512]{2,1,0:T(8,128)(2,1)S(1)}, u32[]{:S(2)}, u32[]{:S(2)}) collective-permute-start(bf16[2,512,512]{2,1,0:T(8,128)(2,1)} %collective-permute-done.3.refs_4_), channel_id=1, source_target_pairs={{0,32},{32,0},{64,96},{96,64},{128,160},{160,128},{192,224},{224,1... | collective-permute-start | bytes 3145736 | tf_op jit(solution)/shard_map/ppermute | solution.py:297
  50.5 14.0 %all-to-all-start.1 = ((bf16[8,64,512]{2,1,0:T(8,128)(2,1)}), bf16[8,64,512]{2,1,0:T(8,128)(2,1)S(1)}, u32[]{:S(2)}, u32[]{:S(2)}) async-start(bf16[8,64,512]{2,1,0:T(8,128)(2,1)} %get-tuple-element.24), calls=%async_computation.1 | async-start | bytes 1048576 | tf_op jit(solution)/shard_map/all_to_all | solution.py:305
  55.6 20.4 %collective-permute-start.7 = (bf16[2,256,256]{2,1,0:T(8,128)(2,1)}, bf16[2,256,256]{2,1,0:T(8,128)(2,1)S(1)}, u32[]{:S(2)}, u32[]{:S(2)}) collective-permute-start(bf16[2,256,256]{2,1,0:T(8,128)(2,1)} %get-tuple-element.29.mean0), channel_id=1, source_target_pairs={{0,8},{8,0},{16,24},{24,16},{1,9},{9,1},{17,25},{25,17},{2,10},{10... | collective-permute-start | bytes 786440 | tf_op jit(solution)/shard_map/ppermute | solution.py:301
  55.6 20.5 %collective-permute-start.8 = (bf16[2,256,256]{2,1,0:T(8,128)(2,1)}, bf16[2,256,256]{2,1,0:T(8,128)(2,1)S(1)}, u32[]{:S(2)}, u32[]{:S(2)}) collective-permute-start(bf16[2,256,256]{2,1,0:T(8,128)(2,1)} %get-tuple-element.34), channel_id=1, source_target_pairs={{0,16},{8,24},{16,0},{24,8},{1,17},{9,25},{17,1},{25,9},{2,18},{10... | collective-permute-start | bytes 786440 | tf_op jit(solution)/shard_map/ppermute | solution.py:301
  57.8 18.2 %collective-permute-start.9 = (bf16[2,256,256]{2,1,0:T(8,128)(2,1)}, bf16[2,256,256]{2,1,0:T(8,128)(2,1)S(1)}, u32[]{:S(2)}, u32[]{:S(2)}) collective-permute-start(bf16[2,256,256]{2,1,0:T(8,128)(2,1)} %get-tuple-element.34), channel_id=1, source_target_pairs={{0,24},{8,16},{16,8},{24,0},{1,25},{9,17},{17,9},{25,1},{2,26},{10... | collective-permute-start | bytes 786440 | tf_op jit(solution)/shard_map/ppermute | solution.py:301
  64.5 0.8 copy-start.7
  64.5 1.2 copy-start.10
  76.0 32.6 %copy-start.2 = (bf16[2,256,256]{2,1,0:T(8,128)(2,1)S(1)}, bf16[2,256,256]{2,1,0:T(8,128)(2,1)}, u32[]{:S(2)}) copy-start(bf16[2,256,256]{2,1,0:T(8,128)(2,1)} %get-tuple-element.29.mean0) | copy-start | bytes 786436
  76.0 32.6 %all-to-all-start.2 = ((bf16[32,2,2,32,256]{4,3,2,1,0:T(8,128)(2,1)}), bf16[32,2,2,32,256]{4,3,2,1,0:T(8,128)(2,1)S(1)}, u32[]{:S(2)}, u32[]{:S(2)}) async-start(bf16[32,2,2,32,256]{4,3,2,1,0:T(8,128)(2,1)} %bitcast.8), calls=%async_computation.2 | async-start | bytes 4194304 | tf_op jit(solution)/shard_map/all_to_all | solution.py:305
  110.3 0.7 copy-start.3
  111.0 19.1 %all-to-all-start.3 = ((bf16[16,2,2,16,256]{4,3,2,1,0:T(8,128)(2,1)}), bf16[16,2,2,16,256]{4,3,2,1,0:T(8,128)(2,1)S(1)}, u32[]{:S(2)}, u32[]{:S(2)}) async-start(bf16[16,2,2,16,256]{4,3,2,1,0:T(8,128)(2,1)} %get-tuple-element.39), calls=%async_computation.3 | async-start | bytes 1048576 | tf_op jit(solution)/shard_map/all_to_all | solution.py:305
  114.9 13.4 %collective-permute-start.10 = (bf16[8,2,32,256]{3,2,1,0:T(8,128)(2,1)}, bf16[8,2,32,256]{3,2,1,0:T(8,128)(2,1)S(1)}, u32[]{:S(2)}, u32[]{:S(2)}) collective-permute-start(bf16[8,2,32,256]{3,2,1,0:T(8,128)(2,1)} %copy-done.3), channel_id=1, source_target_pairs={{0,16},{8,24},{16,0},{24,8},{1,17},{9,25},{17,1},{25,9},{2,18},{10... | collective-permute-start | bytes 786440 | tf_op jit(solution)/shard_map/ppermute | solution.py:301

commit v5 on v4

--- a/solution.py
+++ b/solution.py
@@ -143,21 +143,16 @@
     return jnp.max(terms_ref[section, part : part + 16, :128].astype(F32)) < INACTIVE / 2
 
 
-def layers_kernel(segment_ref, features_hbm, cotangent_hbm, terms_hbm, *refs):
+def layers_kernel(segment_ref, features_hbm, cotangent_hbm, terms_ref, *refs):
     pieces, refs = refs[:8], refs[8:]
-    out_hbm, out_ref, terms_ref, state, cotangent, weights, pre, sems, term_sems, out_sems = refs
-    segments, halves, _, _, slots, part, columns = out_ref.shape
+    out_hbm, out_ref, state, cotangent, weights, kept_normed, slopes, sems, out_sems = refs
+    _, _, slots, part, columns = out_ref.shape
+    segments, halves = terms_ref.shape[0], 2
     layers = segments * slots
 
-    def load_terms(section):
-        return pltpu.make_async_copy(
-            terms_hbm.at[section], terms_ref.at[section], term_sems.at[section]
-        )
-
     def store_rows(section):
-        return pltpu.make_async_copy(
-            out_ref.at[section], out_hbm.at[section], out_sems.at[section]
-        )
+        rows = pl.ds(section * halves * halves, halves * halves)
+        return pltpu.make_async_copy(out_ref.at[rows], out_hbm.at[rows], out_sems.at[section])
 
     my_rows = pl.ds(pl.multiple_of(segment_ref[0] * part, part), part)
     load_features = pltpu.make_async_copy(features_hbm.at[my_rows], state, out_sems.at[0])
@@ -165,8 +160,6 @@
     load_features.start()
     for section in range(AHEAD):
         start_weights(segment_ref, pieces, weights, sems, section)
-    for section in range(segments):
-        load_terms(section).start()
     load_cotangent.start()
     load_features.wait()
 
@@ -174,7 +167,7 @@
         x = state[...]
         for i in range(halves):
             for j in range(halves):
-                out_ref[section, i, j, 0, slot] = x[:, i * columns : (i + 1) * columns]
+                out_ref[(section * halves + i) * halves + j, 0, slot] = x[:, i * columns : (i + 1) * columns]
 
     def forward(section, slot):
         layer = section * slots + slot
@@ -182,13 +175,14 @@
         pre_norm = matmul(x, weights[layer]) + terms_ref[
             section, slot * part : (slot + 1) * part
         ].astype(F32)
-        pre[layer] = pre_norm
-        _, normed = normalize(pre_norm)
-        state[...] = (x.astype(F32) + normed * (0.5 + 0.5 * jnp.tanh(0.5 * normed))).astype(BF16)
+        inverse, normed = normalize(pre_norm)
+        sigmoid = 0.5 + 0.5 * jnp.tanh(0.5 * normed)
+        state[...] = (x.astype(F32) + normed * sigmoid).astype(BF16)
+        kept_normed[layer] = normed
+        slopes[layer] = inverse * (sigmoid * (1.0 + normed * (1.0 - sigmoid)))
 
     @pl.loop(0, segments, unroll=8)
     def _(section):
-        load_terms(section).wait()
         both = two_slots(terms_ref, section)
         weight_copy(pieces[0], weights, sems, section).wait()
 
@@ -209,17 +203,14 @@
 
     def backward(section, slot):
         layer = section * slots + slot
-        inverse, normed = normalize(pre[layer])
+        normed = kept_normed[layer]
         grad_out = state[...].astype(F32)
-        sigmoid = (0.5 + 0.5 * jnp.tanh(0.5 * normed))
-        grad_normed = grad_out * sigmoid * (1.0 + normed * (1.0 - sigmoid))
-        grad_pre = inverse * (
-            grad_normed - normed * jnp.mean(grad_normed * normed, axis=-1, keepdims=True)
-        )
+        scaled = grad_out * slopes[layer]
+        grad_pre = scaled - normed * jnp.mean(scaled * normed, axis=-1, keepdims=True)
         low = grad_pre.astype(BF16)
         for i in range(halves):
             for j in range(halves):
-                out_ref[section, i, j, 1, slot] = low[:, j * columns : (j + 1) * columns]
+                out_ref[(section * halves + i) * halves + j, 1, slot] = low[:, j * columns : (j + 1) * columns]
         back = lax.dot_general(
             low, weights[layer], (((1,), (1,)), ((), ())), preferred_element_type=F32
         )
@@ -238,7 +229,7 @@
         def _():
             for i in range(halves):
                 for j in range(halves):
-                    out_ref[section, i, j, 1, 1] = jnp.zeros((part, columns), BF16)
+                    out_ref[(section * halves + i) * halves + j, 1, 1] = jnp.zeros((part, columns), BF16)
 
         backward(section, 0)
         store_rows(section).start()
@@ -414,21 +405,20 @@
     anywhere = pl.BlockSpec(memory_space=pl.ANY)
     rows = pl.pallas_call(
         layers_kernel,
-        in_specs=[smem] + [anywhere] * (3 + len(pieces)),
+        in_specs=[smem, anywhere, anywhere, vmem] + [anywhere] * len(pieces),
         out_specs=anywhere,
-        out_shape=jax.ShapeDtypeStruct((segments, 2, 2, 2, slots, part, columns), BF16),
+        out_shape=jax.ShapeDtypeStruct((segments * x_size, 2, slots, part, columns), BF16),
         scratch_shapes=[
-            pltpu.VMEM((segments, 2, 2, 2, slots, part, columns), BF16),
-            pltpu.VMEM((segments, term_rows, width), BF16),
+            pltpu.VMEM((segments * x_size, 2, slots, part, columns), BF16),
             pltpu.VMEM((part, width), BF16),
             pltpu.VMEM((part, width), BF16),
             pltpu.VMEM((layers, width, width), BF16),
             pltpu.VMEM((layers, part, width), F32),
-            pltpu.SemaphoreType.DMA((segments,)),
+            pltpu.VMEM((layers, part, width), F32),
             pltpu.SemaphoreType.DMA((segments,)),
             pltpu.SemaphoreType.DMA((segments,)),
         ],
-        compiler_params=params(57.5),
+        compiler_params=params(50),
         cost_estimate=lasting(13),
         name="all_layers",
     )(my_segment, features, cotangent, all_terms, *pieces)
@@ -436,7 +426,6 @@
         (rows, x_swap(mean, 1), x_swap(others_mean, 2), x_swap(others_mean, 3))
     )
     means = (mean, *other_means)
-    rows = rows.reshape(segments * x_size, 2, slots, part, columns)
     rows = exchange(rows, ("segment", "xa", "xb"))
 
     out_rows = width // shards

time: 134 us -> 133 us (level); the launches traced: 131 us -> 132 us
  Pallas kernels: 19.7 us -> 21.7 us
    unnamed x24 -> x20, local copies, waits for them, and re-layouts: 4.61 us -> 3.64 us
  transfers between devices with their start and end apart: 15 -> 15, of which waited for: 7 -> 7; matrix products, arithmetic and copies ran while one was open for 2% -> 3% of each run, Pallas kernels for 13% -> 14%
where the time goes in v5:
time: 133 us; the launch traced here: 132 us
  waiting for transfers between devices  66 us (50%)
  starting transfers between devices  36.2 us (27%)
  Pallas kernels  21.7 us (16%)
  local copies, waits for them, and re-layouts  4.07 us (3%)
  other arithmetic  2.43 us (2%)
  between operations  1.5 us (1%)
    all_to_all x4, waiting for transfers between devices, exchange(): return lax.all_to_all(block, axes, split_axis=0, concat_axis=0, tiled=True)  44.8 us
    all_to_all x4, starting transfers between devices, exchange(): return lax.all_to_all(block, axes, split_axis=0, concat_axis=0, tiled=True)  25.2 us
    ppermute x4, waiting for transfers between devices, x_swap(): lax.ppermute(block, ('xa', 'xb'), [(i, i ^ step) for i in range(PAIR * PA...  11.4 us
    pallas_call x1, Pallas kernels, body(): pl.pallas_call(layers_kernel, in_specs=[smem, anywhere, anywhere, vmem] +...  11.1 us
    ppermute x3, waiting for transfers between devices, round_y(): return lax.ppermute(block, 'segment', route)  9.72 us
    ppermute x4, starting transfers between devices, x_swap(): lax.ppermute(block, ('xa', 'xb'), [(i, i ^ step) for i in range(PAIR * PA...  6.72 us
    unnamed x20, local copies, waits for them, and re-layouts  3.64 us
    ppermute x3, starting transfers between devices, round_y(): return lax.ppermute(block, 'segment', route)  3.64 us
  transfers between devices with their start and end apart: 15, of which 7 were waited for; matrix products, arithmetic and copies ran while one was open for 3% of the time, Pallas kernels for 14%

profile of v5, /device:TPU:8, one launch (start us, length us, event | category | flops | bytes accessed | tf_op | source)
XLA Modules:
  0.0 131.9 jit_solution(5339571277220920177)
XLA Ops:
  0.6 1.7 %collective-permute-start = (bf16[2,512,512]{2,1,0:T(8,128)(2,1)}, bf16[2,512,512]{2,1,0:T(8,128)(2,1)}, u32[]{:S(2)}, u32[]{:S(2)}) collective-permute-start(bf16[2,512,512]{2,1,0:T(8,128)(2,1)} %refs_0_.1), channel_id=1, source_target_pairs={{0,64},{32,96},{64,128},{96,160},{128,192},{160,224},{192,0},{224,... | collective-permute-start | bytes 3145736 | tf_op jit(solution)/shard_map/ppermute | solution.py:283
  2.3 0.7 collective-permute-start.1
  3.0 0.8 copy.14
  3.8 0.2 reshape.59.index_ref
  4.0 1.0 copy-done.1
  5.0 1.4 %pick_rows.1 = bf16[32,2,16,512]{3,2,1,0:T(8,128)(2,1)} custom-call(s32[512,1]{1,0:T(8,128)S(1)} %reshape.59.index_ref, bf16[2,256,512]{2,1,0:T(8,128)(2,1)S(1)} %copy-done.1), custom_call_target="tpu_custom_call" | custom-call | tf_op jit(solution)/shard_map/pick_rows/pallas_call | solution.py:329
  6.4 11.1 %all-to-all-start = ((bf16[32,2,16,512]{3,2,1,0:T(8,128)(2,1)}), bf16[32,2,16,512]{3,2,1,0:T(8,128)(2,1)S(1)}, u32[]{:S(2)}, u32[]{:S(2)}) async-start(bf16[32,2,16,512]{3,2,1,0:T(8,128)(2,1)} %pick_rows.1), calls=%async_computation | async-start | bytes 2097152 | tf_op jit(solution)/shard_map/all_to_all | solution.py:296
  17.5 8.4 %collective-permute-done.refs_6_ = bf16[2,512,512]{2,1,0:T(8,128)(2,1)} collective-permute-done((bf16[2,512,512]{2,1,0:T(8,128)(2,1)}, bf16[2,512,512]{2,1,0:T(8,128)(2,1)}, u32[]{:S(2)}, u32[]{:S(2)}) %collective-permute-start) | collective-permute-done | bytes 1048608 | tf_op jit(solution)/shard_map/ppermute | solution.py:283
  25.9 1.3 collective-permute-done.1.refs_2_
  27.2 2.4 %broadcast_select_fusion = bf16[2,512,512]{2,1,0:T(8,128)(2,1)} fusion(bf16[2,512,512]{2,1,0:T(8,128)(2,1)} %collective-permute-done.refs_6_, bf16[2,512,512]{2,1,0:T(8,128)(2,1)} %collective-permute-done.1.refs_2_, pred[]{:T(512)S(6)} %eq.3), kind=kLoop, calls=%fused_computation | loop fusion | flops 524288 | bytes 3145729 | tf_op jit(solution)/shard_map/jit(_where)/select_n | solution.py:368
  29.6 1.3 collective-permute-start.3
  30.9 0.5 collective-permute-start.5
  31.4 0.2 dynamic-slice_reduce_fusion
  31.7 0.1 copy.16.neighbours_ref
  32.5 1.9 %count_rows.1.counts_hbm = bf16[256,768]{1,0:T(8,128)(2,1)S(1)} custom-call(s32[256,16]{1,0:T(8,128)S(1)} %copy.16.neighbours_ref, f32[1,768]{1,0:T(1,128)S(1)} %pad_convert_fusion.live_ref), custom_call_target="tpu_custom_call" | custom-call | flops 2300000000 | bytes 4194304 | tf_op jit(solution)/shard_map/count_rows/pallas_call | solution.py:357
  34.4 0.7 copy-done.6
  35.2 11.6 %all-to-all-done.received_hbm = bf16[32,2,16,512]{3,2,1,0:T(8,128)(2,1)S(1)} async-done(((bf16[32,2,16,512]{3,2,1,0:T(8,128)(2,1)}), bf16[32,2,16,512]{3,2,1,0:T(8,128)(2,1)S(1)}, u32[]{:S(2)}, u32[]{:S(2)}) %all-to-all-start) | async-done | bytes 1048608 | tf_op jit(solution)/shard_map/all_to_all | solution.py:296
  46.7 1.0 copy-done.7
  47.7 3.6 %neighbour_mean.1 = (bf16[2,256,256]{2,1,0:T(8,128)(2,1)}, bf16[2,256,256]{2,1,0:T(8,128)(2,1)}, bf16[8,64,512]{2,1,0:T(8,128)(2,1)}) custom-call(s32[1]{0:T(128)S(6)} %copy.17.depth_ref, s32[1]{0:T(128)} %bitcast.half_ref, bf16[32,2,16,512]{3,2,1,0:T(8,128)(2,1)} %copy-done.7, bf16[256,768]{1,0:T(8,128)(2,1)} %copy-done.6, ...), custom_call_target="tpu_custom_call" | custom-call | flops 2300000000 | bytes 4194304 | tf_op jit(solution)/shard_map/neighbour_mean/pallas_call | solution.py:374
  51.5 5.1 %all-to-all-start.1 = ((bf16[8,64,512]{2,1,0:T(8,128)(2,1)}), bf16[8,64,512]{2,1,0:T(8,128)(2,1)S(1)}, u32[]{:S(2)}, u32[]{:S(2)}) async-start(bf16[8,64,512]{2,1,0:T(8,128)(2,1)} %get-tuple-element.24), calls=%async_computation.1 | async-start | bytes 1048576 | tf_op jit(solution)/shard_map/all_to_all | solution.py:296
  56.5 2.3 %collective-permute-start.8 = (bf16[2,256,256]{2,1,0:T(8,128)(2,1)}, bf16[2,256,256]{2,1,0:T(8,128)(2,1)}, u32[]{:S(2)}, u32[]{:S(2)}) collective-permute-start(bf16[2,256,256]{2,1,0:T(8,128)(2,1)} %get-tuple-element.34), channel_id=1, source_target_pairs={{0,16},{8,24},{16,0},{24,8},{1,17},{9,25},{17,1},{25,9},{2,18},{10... | collective-permute-start | bytes 786440 | tf_op jit(solution)/shard_map/ppermute | solution.py:292
  58.8 2.4 %collective-permute-start.9 = (bf16[2,256,256]{2,1,0:T(8,128)(2,1)}, bf16[2,256,256]{2,1,0:T(8,128)(2,1)}, u32[]{:S(2)}, u32[]{:S(2)}) collective-permute-start(bf16[2,256,256]{2,1,0:T(8,128)(2,1)} %get-tuple-element.34), channel_id=1, source_target_pairs={{0,24},{8,16},{16,8},{24,0},{1,25},{9,17},{17,9},{25,1},{2,26},{10... | collective-permute-start | bytes 786440 | tf_op jit(solution)/shard_map/ppermute | solution.py:292
  61.2 4.2 %all-to-all-done.1.terms_ref = bf16[8,64,512]{2,1,0:T(8,128)(2,1)S(1)} async-done(((bf16[8,64,512]{2,1,0:T(8,128)(2,1)}), bf16[8,64,512]{2,1,0:T(8,128)(2,1)S(1)}, u32[]{:S(2)}, u32[]{:S(2)}) %all-to-all-start.1) | async-done | bytes 524320 | tf_op jit(solution)/shard_map/all_to_all | solution.py:296
  65.5 11.1 %all_layers.1 = bf16[32,2,2,32,256]{4,3,2,1,0:T(8,128)(2,1)} custom-call(s32[1]{0:T(128)} %bitcast.2.segment_ref, bf16[256,512]{1,0:T(8,128)(2,1)S(1)} %copy-done.3, bf16[256,512]{1,0:T(8,128)(2,1)S(1)} %copy-done.4, bf16[8,64,512]{2,1,0:T(8,128)(2,1)S(1)} %all-to-all-done.1.terms_ref, bf16[2,512,512]{2,1,0:T(8,128)(2,1)S(1)} %copy-done.2, ...), custom_call_target="tpu_custom_call" | custom-call | flops 14949999616 | bytes 4194304 | tf_op jit(solution)/shard_map/all_layers/pallas_call | solution.py:406
  76.6 4.5 %all-to-all-start.2 = ((bf16[32,2,2,32,256]{4,3,2,1,0:T(8,128)(2,1)}), bf16[32,2,2,32,256]{4,3,2,1,0:T(8,128)(2,1)S(1)}, u32[]{:S(2)}, u32[]{:S(2)}) async-start(bf16[32,2,2,32,256]{4,3,2,1,0:T(8,128)(2,1)} %all_layers.1), calls=%async_computation.2 | async-start | bytes 4194304 | tf_op jit(solution)/shard_map/all_to_all | solution.py:296
  81.2 27.2 %all-to-all-done.2 = bf16[32,2,2,32,256]{4,3,2,1,0:T(8,128)(2,1)S(1)} async-done(((bf16[32,2,2,32,256]{4,3,2,1,0:T(8,128)(2,1)}), bf16[32,2,2,32,256]{4,3,2,1,0:T(8,128)(2,1)S(1)}, u32[]{:S(2)}, u32[]{:S(2)}) %all-to-all-start.2) | async-done | bytes 2097184 | tf_op jit(solution)/shard_map/all_to_all | solution.py:296
  108.4 2.7 %weight_products.1 = (bf16[16,2,2,16,256]{4,3,2,1,0:T(8,128)(2,1)}, bf16[8,2,32,256]{3,2,1,0:T(8,128)(2,1)S(1)}, bf16[8,2,32,256]{3,2,1,0:T(8,128)(2,1)S(1)}) custom-call(s32[1]{0:T(128)} %bitcast.1.place_ref, bf16[8,4,2,2,32,256]{5,4,3,2,1,0:T(8,128)(2,1)S(1)} %bitcast.5, bf16[2,256,256]{2,1,0:T(8,128)(2,1)S(1)} %copy-done.5, ...), custom_call_target="tpu_custom_call" | custom-call | flops 3449999872 | bytes 4194304 | tf_op jit(solution)/shard_map/weight_products/pallas_call | solution.py:434
  111.1 4.6 %all-to-all-start.3 = ((bf16[16,2,2,16,256]{4,3,2,1,0:T(8,128)(2,1)}), bf16[16,2,2,16,256]{4,3,2,1,0:T(8,128)(2,1)S(1)}, u32[]{:S(2)}, u32[]{:S(2)}) async-start(bf16[16,2,2,16,256]{4,3,2,1,0:T(8,128)(2,1)} %get-tuple-element.39), calls=%async_computation.3 | async-start | bytes 1048576 | tf_op jit(solution)/shard_map/all_to_all | solution.py:296
  115.7 2.0 %collective-permute-start.10 = (bf16[8,2,32,256]{3,2,1,0:T(8,128)(2,1)S(1)}, bf16[8,2,32,256]{3,2,1,0:T(8,128)(2,1)S(1)}, u32[]{:S(2)}, u32[]{:S(2)}) collective-permute-start(bf16[8,2,32,256]{3,2,1,0:T(8,128)(2,1)S(1)} %get-tuple-element.41), channel_id=1, source_target_pairs={{0,16},{8,24},{16,0},{24,8},{1,17},{9,25},{17,1},{25,9},{2,18},{10... | collective-permute-start | bytes 786440 | tf_op jit(solution)/shard_map/ppermute | solution.py:292
  117.7 11.4 %collective-permute-done.10.missing_ref = bf16[8,2,32,256]{3,2,1,0:T(8,128)(2,1)S(1)} collective-permute-done((bf16[8,2,32,256]{3,2,1,0:T(8,128)(2,1)S(1)}, bf16[8,2,32,256]{3,2,1,0:T(8,128)(2,1)S(1)}, u32[]{:S(2)}, u32[]{:S(2)}) %collective-permute-start.10) | collective-permute-done | bytes 262176 | tf_op jit(solution)/shard_map/ppermute | solution.py:292
  129.1 1.8 %all-to-all-done.3 = bf16[16,2,2,16,256]{4,3,2,1,0:T(8,128)(2,1)S(1)} async-done(((bf16[16,2,2,16,256]{4,3,2,1,0:T(8,128)(2,1)}), bf16[16,2,2,16,256]{4,3,2,1,0:T(8,128)(2,1)S(1)}, u32[]{:S(2)}, u32[]{:S(2)}) %all-to-all-start.3) | async-done | bytes 524320 | tf_op jit(solution)/shard_map/all_to_all | solution.py:296
  130.9 0.9 finish.1
  (30 shorter events, 0.3 us)
Async XLA Ops:
  0.6 30.8 %copy-start = (s32[32,32]{1,0:T(8,128)S(1)}, s32[32,32]{1,0:T(8,128)}, u32[]{:S(2)}) copy-start(s32[32,32]{1,0:T(8,128)} %param.15) | copy-start | bytes 12292
  0.6 25.3 %collective-permute-start = (bf16[2,512,512]{2,1,0:T(8,128)(2,1)}, bf16[2,512,512]{2,1,0:T(8,128)(2,1)}, u32[]{:S(2)}, u32[]{:S(2)}) collective-permute-start(bf16[2,512,512]{2,1,0:T(8,128)(2,1)} %refs_0_.1), channel_id=1, source_target_pairs={{0,64},{32,96},{64,128},{96,160},{128,192},{160,224},{192,0},{224,... | collective-permute-start | bytes 3145736 | tf_op jit(solution)/shard_map/ppermute | solution.py:283
  2.3 24.9 %collective-permute-start.1 = (bf16[2,512,512]{2,1,0:T(8,128)(2,1)}, bf16[2,512,512]{2,1,0:T(8,128)(2,1)}, u32[]{:S(2)}, u32[]{:S(2)}) collective-permute-start(bf16[2,512,512]{2,1,0:T(8,128)(2,1)} %refs_0_.1), channel_id=1, source_target_pairs={{0,192},{32,224},{64,0},{96,32},{128,64},{160,96},{192,128},{224,1... | collective-permute-start | bytes 3145736 | tf_op jit(solution)/shard_map/ppermute | solution.py:283
  3.0 24.2 %collective-permute-start.2 = (bf16[2,512,512]{2,1,0:T(8,128)(2,1)}, bf16[2,512,512]{2,1,0:T(8,128)(2,1)S(1)}, u32[]{:S(2)}, u32[]{:S(2)}) collective-permute-start(bf16[2,512,512]{2,1,0:T(8,128)(2,1)} %refs_0_.1), channel_id=1, source_target_pairs={{0,32},{32,0},{64,96},{96,64},{128,160},{160,128},{192,224},{224,1... | collective-permute-start | bytes 3145736 | tf_op jit(solution)/shard_map/ppermute | solution.py:288
  3.9 1.0 copy-start.1
  6.4 40.3 %all-to-all-start = ((bf16[32,2,16,512]{3,2,1,0:T(8,128)(2,1)}), bf16[32,2,16,512]{3,2,1,0:T(8,128)(2,1)S(1)}, u32[]{:S(2)}, u32[]{:S(2)}) async-start(bf16[32,2,16,512]{3,2,1,0:T(8,128)(2,1)} %pick_rows.1), calls=%async_computation | async-start | bytes 2097152 | tf_op jit(solution)/shard_map/all_to_all | solution.py:296
  17.5 14.2 %copy-start.8 = (s32[256,16]{0,1:T(8,128)S(1)}, s32[256,16]{0,1:T(8,128)}, u32[]{:S(2)}) copy-start(s32[256,16]{0,1:T(8,128)} %param.16) | copy-start | bytes 49156
  29.6 21.7 %collective-permute-start.3 = (bf16[2,512,512]{2,1,0:T(8,128)(2,1)}, bf16[2,512,512]{2,1,0:T(8,128)(2,1)}, u32[]{:S(2)}, u32[]{:S(2)}) collective-permute-start(bf16[2,512,512]{2,1,0:T(8,128)(2,1)} %broadcast_select_fusion), channel_id=1, source_target_pairs={{0,64},{32,224},{64,128},{96,32},{128,192},{160,96},{192,0},{224,1... | collective-permute-start | bytes 3145736 | tf_op jit(solution)/shard_map/ppermute | solution.py:283
  30.9 20.5 %collective-permute-start.4 = (bf16[2,512,512]{2,1,0:T(8,128)(2,1)}, bf16[2,512,512]{2,1,0:T(8,128)(2,1)}, u32[]{:S(2)}, u32[]{:S(2)}) collective-permute-start(bf16[2,512,512]{2,1,0:T(8,128)(2,1)} %collective-permute-done.1.refs_2_), channel_id=1, source_target_pairs={{0,32},{32,0},{64,96},{96,64},{128,160},{160,128},{192,224},{224,1... | collective-permute-start | bytes 3145736 | tf_op jit(solution)/shard_map/ppermute | solution.py:288
  30.9 20.5 %collective-permute-start.5 = (bf16[2,512,512]{2,1,0:T(8,128)(2,1)}, bf16[2,512,512]{2,1,0:T(8,128)(2,1)}, u32[]{:S(2)}, u32[]{:S(2)}) collective-permute-start(bf16[2,512,512]{2,1,0:T(8,128)(2,1)} %collective-permute-done.refs_6_), channel_id=1, source_target_pairs={{0,32},{32,0},{64,96},{96,64},{128,160},{160,128},{192,224},{224,1... | collective-permute-start | bytes 3145736 | tf_op jit(solution)/shard_map/ppermute | solution.py:288
  34.4 0.8 copy-start.6
  46.7 1.0 copy-start.7
  47.7 17.8 %copy-start.2 = (bf16[2,512,512]{2,1,0:T(8,128)(2,1)S(1)}, bf16[2,512,512]{2,1,0:T(8,128)(2,1)}, u32[]{:S(2)}) copy-start(bf16[2,512,512]{2,1,0:T(8,128)(2,1)} %refs_0_.1) | copy-start | bytes 3145732
  47.7 17.8 %copy-start.3 = (bf16[256,512]{1,0:T(8,128)(2,1)S(1)}, bf16[256,512]{1,0:T(8,128)(2,1)}, u32[]{:S(2)}) copy-start(bf16[256,512]{1,0:T(8,128)(2,1)} %features_hbm.1) | copy-start | bytes 786436
  47.7 17.8 %copy-start.4 = (bf16[256,512]{1,0:T(8,128)(2,1)S(1)}, bf16[256,512]{1,0:T(8,128)(2,1)}, u32[]{:S(2)}) copy-start(bf16[256,512]{1,0:T(8,128)(2,1)} %cotangent_hbm.1) | copy-start | bytes 786436
  51.4 14.1 %collective-permute-start.6 = (bf16[2,512,512]{2,1,0:T(8,128)(2,1)}, bf16[2,512,512]{2,1,0:T(8,128)(2,1)}, u32[]{:S(2)}, u32[]{:S(2)}) collective-permute-start(bf16[2,512,512]{2,1,0:T(8,128)(2,1)} %collective-permute-done.3.refs_4_), channel_id=1, source_target_pairs={{0,32},{32,0},{64,96},{96,64},{128,160},{160,128},{192,224},{224,1... | collective-permute-start | bytes 3145736 | tf_op jit(solution)/shard_map/ppermute | solution.py:288
  51.5 14.0 %all-to-all-start.1 = ((bf16[8,64,512]{2,1,0:T(8,128)(2,1)}), bf16[8,64,512]{2,1,0:T(8,128)(2,1)S(1)}, u32[]{:S(2)}, u32[]{:S(2)}) async-start(bf16[8,64,512]{2,1,0:T(8,128)(2,1)} %get-tuple-element.24), calls=%async_computation.1 | async-start | bytes 1048576 | tf_op jit(solution)/shard_map/all_to_all | solution.py:296
  56.5 20.1 %collective-permute-start.7 = (bf16[2,256,256]{2,1,0:T(8,128)(2,1)}, bf16[2,256,256]{2,1,0:T(8,128)(2,1)S(1)}, u32[]{:S(2)}, u32[]{:S(2)}) collective-permute-start(bf16[2,256,256]{2,1,0:T(8,128)(2,1)} %get-tuple-element.29.mean0), channel_id=1, source_target_pairs={{0,8},{8,0},{16,24},{24,16},{1,9},{9,1},{17,25},{25,17},{2,10},{10... | collective-permute-start | bytes 786440 | tf_op jit(solution)/shard_map/ppermute | solution.py:292
  56.5 20.1 %collective-permute-start.8 = (bf16[2,256,256]{2,1,0:T(8,128)(2,1)}, bf16[2,256,256]{2,1,0:T(8,128)(2,1)}, u32[]{:S(2)}, u32[]{:S(2)}) collective-permute-start(bf16[2,256,256]{2,1,0:T(8,128)(2,1)} %get-tuple-element.34), channel_id=1, source_target_pairs={{0,16},{8,24},{16,0},{24,8},{1,17},{9,25},{17,1},{25,9},{2,18},{10... | collective-permute-start | bytes 786440 | tf_op jit(solution)/shard_map/ppermute | solution.py:292
  58.8 17.8 %collective-permute-start.9 = (bf16[2,256,256]{2,1,0:T(8,128)(2,1)}, bf16[2,256,256]{2,1,0:T(8,128)(2,1)}, u32[]{:S(2)}, u32[]{:S(2)}) collective-permute-start(bf16[2,256,256]{2,1,0:T(8,128)(2,1)} %get-tuple-element.34), channel_id=1, source_target_pairs={{0,24},{8,16},{16,8},{24,0},{1,25},{9,17},{17,9},{25,1},{2,26},{10... | collective-permute-start | bytes 786440 | tf_op jit(solution)/shard_map/ppermute | solution.py:292
  76.6 31.8 %copy-start.5 = (bf16[2,256,256]{2,1,0:T(8,128)(2,1)S(1)}, bf16[2,256,256]{2,1,0:T(8,128)(2,1)}, u32[]{:S(2)}) copy-start(bf16[2,256,256]{2,1,0:T(8,128)(2,1)} %get-tuple-element.29.mean0) | copy-start | bytes 786436
  76.6 31.8 %all-to-all-start.2 = ((bf16[32,2,2,32,256]{4,3,2,1,0:T(8,128)(2,1)}), bf16[32,2,2,32,256]{4,3,2,1,0:T(8,128)(2,1)S(1)}, u32[]{:S(2)}, u32[]{:S(2)}) async-start(bf16[32,2,2,32,256]{4,3,2,1,0:T(8,128)(2,1)} %all_layers.1), calls=%async_computation.2 | async-start | bytes 4194304 | tf_op jit(solution)/shard_map/all_to_all | solution.py:296
  111.1 19.8 %all-to-all-start.3 = ((bf16[16,2,2,16,256]{4,3,2,1,0:T(8,128)(2,1)}), bf16[16,2,2,16,256]{4,3,2,1,0:T(8,128)(2,1)S(1)}, u32[]{:S(2)}, u32[]{:S(2)}) async-start(bf16[16,2,2,16,256]{4,3,2,1,0:T(8,128)(2,1)} %get-tuple-element.39), calls=%async_computation.3 | async-start | bytes 1048576 | tf_op jit(solution)/shard_map/all_to_all | solution.py:296
  115.7 13.4 %collective-permute-start.10 = (bf16[8,2,32,256]{3,2,1,0:T(8,128)(2,1)S(1)}, bf16[8,2,32,256]{3,2,1,0:T(8,128)(2,1)S(1)}, u32[]{:S(2)}, u32[]{:S(2)}) collective-permute-start(bf16[8,2,32,256]{3,2,1,0:T(8,128)(2,1)S(1)} %get-tuple-element.41), channel_id=1, source_target_pairs={{0,16},{8,24},{16,0},{24,8},{1,17},{9,25},{17,1},{25,9},{2,18},{10... | collective-permute-start | bytes 786440 | tf_op jit(solution)/shard_map/ppermute | solution.py:292

commit v6 on v5

--- a/solution.py
+++ b/solution.py
@@ -418,7 +418,7 @@
             pltpu.SemaphoreType.DMA((segments,)),
             pltpu.SemaphoreType.DMA((segments,)),
         ],
-        compiler_params=params(50),
+        compiler_params=params(52),
         cost_estimate=lasting(13),
         name="all_layers",
     )(my_segment, features, cotangent, all_terms, *pieces)

time: 133 us -> 132 us (level)
    unnamed x20 -> x24, local copies, waits for them, and re-layouts: 3.64 us -> 3.4 us
  transfers between devices with their start and end apart: 15 -> 15, of which waited for: 7 -> 7; matrix products, arithmetic and copies ran while one was open for 3% -> 2% of each run, Pallas kernels for 14% -> 14%
where the time goes in v6:
time: 132 us; the launch traced here: 131 us
  waiting for transfers between devices  67 us (51%)
  starting transfers between devices  36.4 us (28%)
  Pallas kernels  20.5 us (16%)
  local copies, waits for them, and re-layouts  3.83 us (3%)
  between operations  1.52 us (1%)
  other arithmetic  1.39 us (1%)
    all_to_all x4, waiting for transfers between devices, exchange(): return lax.all_to_all(block, axes, split_axis=0, concat_axis=0, tiled=True)  46.1 us
    all_to_all x4, starting transfers between devices, exchange(): return lax.all_to_all(block, axes, split_axis=0, concat_axis=0, tiled=True)  25.4 us
    ppermute x4, waiting for transfers between devices, x_swap(): lax.ppermute(block, ('xa', 'xb'), [(i, i ^ step) for i in range(PAIR * PA...  11.4 us
    pallas_call x1, Pallas kernels, body(): pl.pallas_call(layers_kernel, in_specs=[smem, anywhere, anywhere, vmem] +...  11 us
    ppermute x3, waiting for transfers between devices, round_y(): return lax.ppermute(block, 'segment', route)  9.48 us
    ppermute x4, starting transfers between devices, x_swap(): lax.ppermute(block, ('xa', 'xb'), [(i, i ^ step) for i in range(PAIR * PA...  6.71 us
    ppermute x3, starting transfers between devices, round_y(): return lax.ppermute(block, 'segment', route)  3.64 us
    pallas_call x1, Pallas kernels, body(): pl.pallas_call(functools.partial(mean_kernel, fanout=fanout), in_specs=[s...  3.57 us
  transfers between devices with their start and end apart: 15, of which 7 were waited for; matrix products, arithmetic and copies ran while one was open for 2% of the time, Pallas kernels for 14%

profile of v6, /device:TPU:8, one launch (start us, length us, event | category | flops | bytes accessed | tf_op | source)
XLA Modules:
  0.0 130.6 jit_solution(12487396984844265616)
XLA Ops:
  0.6 1.7 %collective-permute-start = (bf16[2,512,512]{2,1,0:T(8,128)(2,1)}, bf16[2,512,512]{2,1,0:T(8,128)(2,1)S(1)}, u32[]{:S(2)}, u32[]{:S(2)}) collective-permute-start(bf16[2,512,512]{2,1,0:T(8,128)(2,1)} %refs_0_.1), channel_id=1, source_target_pairs={{0,64},{32,96},{64,128},{96,160},{128,192},{160,224},{192,0},{224,... | collective-permute-start | bytes 3145736 | tf_op jit(solution)/shard_map/ppermute | solution.py:283
  2.3 0.7 collective-permute-start.1
  3.0 0.8 copy.14
  3.8 0.2 reshape.59.index_ref
  4.0 1.0 copy-done.1
  5.0 1.4 %pick_rows.1 = bf16[32,2,16,512]{3,2,1,0:T(8,128)(2,1)} custom-call(s32[512,1]{1,0:T(8,128)S(1)} %reshape.59.index_ref, bf16[2,256,512]{2,1,0:T(8,128)(2,1)S(1)} %copy-done.1), custom_call_target="tpu_custom_call" | custom-call | tf_op jit(solution)/shard_map/pick_rows/pallas_call | solution.py:329
  6.4 11.2 %all-to-all-start = ((bf16[32,2,16,512]{3,2,1,0:T(8,128)(2,1)}), bf16[32,2,16,512]{3,2,1,0:T(8,128)(2,1)}, u32[]{:S(2)}, u32[]{:S(2)}) async-start(bf16[32,2,16,512]{3,2,1,0:T(8,128)(2,1)} %pick_rows.1), calls=%async_computation | async-start | bytes 2097152 | tf_op jit(solution)/shard_map/all_to_all | solution.py:296
  17.7 8.2 %collective-permute-done.refs_6_ = bf16[2,512,512]{2,1,0:T(8,128)(2,1)S(1)} collective-permute-done((bf16[2,512,512]{2,1,0:T(8,128)(2,1)}, bf16[2,512,512]{2,1,0:T(8,128)(2,1)S(1)}, u32[]{:S(2)}, u32[]{:S(2)}) %collective-permute-start) | collective-permute-done | bytes 1048608 | tf_op jit(solution)/shard_map/ppermute | solution.py:283
  25.8 1.3 collective-permute-done.1.refs_2_
  27.1 1.3 %broadcast_select_fusion = bf16[2,512,512]{2,1,0:T(8,128)(2,1)} fusion(bf16[2,512,512]{2,1,0:T(8,128)(2,1)S(1)} %collective-permute-done.refs_6_, bf16[2,512,512]{2,1,0:T(8,128)(2,1)S(1)} %collective-permute-done.1.refs_2_, pred[]{:T(512)S(6)} %eq.3), kind=kLoop, calls=%fused_computation | loop fusion | flops 524288 | bytes 3145729 | tf_op jit(solution)/shard_map/jit(_where)/select_n | solution.py:368
  28.4 1.3 collective-permute-start.3
  29.7 0.5 collective-permute-start.5
  30.2 0.2 dynamic-slice_reduce_fusion
  30.6 0.1 copy.16.neighbours_ref
  31.4 1.9 %count_rows.1.counts_hbm = bf16[256,768]{1,0:T(8,128)(2,1)S(1)} custom-call(s32[256,16]{1,0:T(8,128)S(1)} %copy.16.neighbours_ref, f32[1,768]{1,0:T(1,128)S(1)} %pad_convert_fusion.live_ref), custom_call_target="tpu_custom_call" | custom-call | flops 2300000000 | bytes 4194304 | tf_op jit(solution)/shard_map/count_rows/pallas_call | solution.py:357
  33.3 0.7 copy-done.6
  34.0 12.8 %all-to-all-done.received_hbm = bf16[32,2,16,512]{3,2,1,0:T(8,128)(2,1)} async-done(((bf16[32,2,16,512]{3,2,1,0:T(8,128)(2,1)}), bf16[32,2,16,512]{3,2,1,0:T(8,128)(2,1)}, u32[]{:S(2)}, u32[]{:S(2)}) %all-to-all-start) | async-done | bytes 1048608 | tf_op jit(solution)/shard_map/all_to_all | solution.py:296
  46.8 3.6 %neighbour_mean.1 = (bf16[2,256,256]{2,1,0:T(8,128)(2,1)}, bf16[2,256,256]{2,1,0:T(8,128)(2,1)}, bf16[8,64,512]{2,1,0:T(8,128)(2,1)}) custom-call(s32[1]{0:T(128)S(6)} %copy.17.depth_ref, s32[1]{0:T(128)} %bitcast.half_ref, bf16[32,2,16,512]{3,2,1,0:T(8,128)(2,1)} %all-to-all-done.received_hbm, bf16[256,768]{1,0:T(8,128)(2,1)} %copy-done.6, ...), custom_call_target="tpu_custom_call" | custom-call | flops 2300000000 | bytes 4194304 | tf_op jit(solution)/shard_map/neighbour_mean/pallas_call | solution.py:374
  50.5 5.1 %all-to-all-start.1 = ((bf16[8,64,512]{2,1,0:T(8,128)(2,1)}), bf16[8,64,512]{2,1,0:T(8,128)(2,1)S(1)}, u32[]{:S(2)}, u32[]{:S(2)}) async-start(bf16[8,64,512]{2,1,0:T(8,128)(2,1)} %get-tuple-element.24), calls=%async_computation.1 | async-start | bytes 1048576 | tf_op jit(solution)/shard_map/all_to_all | solution.py:296
  55.6 2.3 %collective-permute-start.8 = (bf16[2,256,256]{2,1,0:T(8,128)(2,1)}, bf16[2,256,256]{2,1,0:T(8,128)(2,1)S(1)}, u32[]{:S(2)}, u32[]{:S(2)}) collective-permute-start(bf16[2,256,256]{2,1,0:T(8,128)(2,1)} %get-tuple-element.34), channel_id=1, source_target_pairs={{0,16},{8,24},{16,0},{24,8},{1,17},{9,25},{17,1},{25,9},{2,18},{10... | collective-permute-start | bytes 786440 | tf_op jit(solution)/shard_map/ppermute | solution.py:292
  57.9 2.4 %collective-permute-start.9 = (bf16[2,256,256]{2,1,0:T(8,128)(2,1)}, bf16[2,256,256]{2,1,0:T(8,128)(2,1)S(1)}, u32[]{:S(2)}, u32[]{:S(2)}) collective-permute-start(bf16[2,256,256]{2,1,0:T(8,128)(2,1)} %get-tuple-element.34), channel_id=1, source_target_pairs={{0,24},{8,16},{16,8},{24,0},{1,25},{9,17},{17,9},{25,1},{2,26},{10... | collective-permute-start | bytes 786440 | tf_op jit(solution)/shard_map/ppermute | solution.py:292
  60.3 4.2 %all-to-all-done.1.terms_ref = bf16[8,64,512]{2,1,0:T(8,128)(2,1)S(1)} async-done(((bf16[8,64,512]{2,1,0:T(8,128)(2,1)}), bf16[8,64,512]{2,1,0:T(8,128)(2,1)S(1)}, u32[]{:S(2)}, u32[]{:S(2)}) %all-to-all-start.1) | async-done | bytes 524320 | tf_op jit(solution)/shard_map/all_to_all | solution.py:296
  64.5 11.0 %all_layers.1 = bf16[32,2,2,32,256]{4,3,2,1,0:T(8,128)(2,1)} custom-call(s32[1]{0:T(128)} %bitcast.2.segment_ref, bf16[256,512]{1,0:T(8,128)(2,1)S(1)} %copy-done.2, bf16[256,512]{1,0:T(8,128)(2,1)S(1)} %copy-done.3, bf16[8,64,512]{2,1,0:T(8,128)(2,1)S(1)} %all-to-all-done.1.terms_ref, bf16[2,512,512]{2,1,0:T(8,128)(2,1)} %refs_0_.1, ...), custom_call_target="tpu_custom_call" | custom-call | flops 14949999616 | bytes 4194304 | tf_op jit(solution)/shard_map/all_layers/pallas_call | solution.py:406
  75.6 5.3 %all-to-all-start.2 = ((bf16[32,2,2,32,256]{4,3,2,1,0:T(8,128)(2,1)}), bf16[32,2,2,32,256]{4,3,2,1,0:T(8,128)(2,1)S(1)}, u32[]{:S(2)}, u32[]{:S(2)}) async-start(bf16[32,2,2,32,256]{4,3,2,1,0:T(8,128)(2,1)} %all_layers.1), calls=%async_computation.2 | async-start | bytes 4194304 | tf_op jit(solution)/shard_map/all_to_all | solution.py:296
  80.9 27.3 %all-to-all-done.2 = bf16[32,2,2,32,256]{4,3,2,1,0:T(8,128)(2,1)S(1)} async-done(((bf16[32,2,2,32,256]{4,3,2,1,0:T(8,128)(2,1)}), bf16[32,2,2,32,256]{4,3,2,1,0:T(8,128)(2,1)S(1)}, u32[]{:S(2)}, u32[]{:S(2)}) %all-to-all-start.2) | async-done | bytes 2097184 | tf_op jit(solution)/shard_map/all_to_all | solution.py:296
  108.2 1.6 %weight_products.1 = (bf16[16,2,2,16,256]{4,3,2,1,0:T(8,128)(2,1)}, bf16[8,2,32,256]{3,2,1,0:T(8,128)(2,1)S(1)}, bf16[8,2,32,256]{3,2,1,0:T(8,128)(2,1)S(1)}) custom-call(s32[1]{0:T(128)} %bitcast.1.place_ref, bf16[8,4,2,2,32,256]{5,4,3,2,1,0:T(8,128)(2,1)S(1)} %bitcast.5, bf16[2,256,256]{2,1,0:T(8,128)(2,1)S(1)} %copy-done.4, ...), custom_call_target="tpu_custom_call" | custom-call | flops 3449999872 | bytes 4194304 | tf_op jit(solution)/shard_map/weight_products/pallas_call | solution.py:434
  109.9 0.7 copy-done.5
  110.6 3.9 %all-to-all-start.3 = ((bf16[16,2,2,16,256]{4,3,2,1,0:T(8,128)(2,1)}), bf16[16,2,2,16,256]{4,3,2,1,0:T(8,128)(2,1)S(1)}, u32[]{:S(2)}, u32[]{:S(2)}) async-start(bf16[16,2,2,16,256]{4,3,2,1,0:T(8,128)(2,1)} %get-tuple-element.39), calls=%async_computation.3 | async-start | bytes 1048576 | tf_op jit(solution)/shard_map/all_to_all | solution.py:296
  114.4 2.0 %collective-permute-start.10 = (bf16[8,2,32,256]{3,2,1,0:T(8,128)(2,1)}, bf16[8,2,32,256]{3,2,1,0:T(8,128)(2,1)S(1)}, u32[]{:S(2)}, u32[]{:S(2)}) collective-permute-start(bf16[8,2,32,256]{3,2,1,0:T(8,128)(2,1)} %copy-done.5), channel_id=1, source_target_pairs={{0,16},{8,24},{16,0},{24,8},{1,17},{9,25},{17,1},{25,9},{2,18},{10... | collective-permute-start | bytes 786440 | tf_op jit(solution)/shard_map/ppermute | solution.py:292
  116.4 11.4 %collective-permute-done.10.missing_ref = bf16[8,2,32,256]{3,2,1,0:T(8,128)(2,1)S(1)} collective-permute-done((bf16[8,2,32,256]{3,2,1,0:T(8,128)(2,1)}, bf16[8,2,32,256]{3,2,1,0:T(8,128)(2,1)S(1)}, u32[]{:S(2)}, u32[]{:S(2)}) %collective-permute-start.10) | collective-permute-done | bytes 262176 | tf_op jit(solution)/shard_map/ppermute | solution.py:292
  127.8 1.8 %all-to-all-done.3 = bf16[16,2,2,16,256]{4,3,2,1,0:T(8,128)(2,1)S(1)} async-done(((bf16[16,2,2,16,256]{4,3,2,1,0:T(8,128)(2,1)}), bf16[16,2,2,16,256]{4,3,2,1,0:T(8,128)(2,1)S(1)}, u32[]{:S(2)}, u32[]{:S(2)}) %all-to-all-start.3) | async-done | bytes 524320 | tf_op jit(solution)/shard_map/all_to_all | solution.py:296
  129.7 0.9 finish.1
  (34 shorter events, 0.3 us)
Async XLA Ops:
  0.6 29.6 %copy-start = (s32[32,32]{1,0:T(8,128)S(1)}, s32[32,32]{1,0:T(8,128)}, u32[]{:S(2)}) copy-start(s32[32,32]{1,0:T(8,128)} %param.15) | copy-start | bytes 12292
  0.6 25.2 %collective-permute-start = (bf16[2,512,512]{2,1,0:T(8,128)(2,1)}, bf16[2,512,512]{2,1,0:T(8,128)(2,1)S(1)}, u32[]{:S(2)}, u32[]{:S(2)}) collective-permute-start(bf16[2,512,512]{2,1,0:T(8,128)(2,1)} %refs_0_.1), channel_id=1, source_target_pairs={{0,64},{32,96},{64,128},{96,160},{128,192},{160,224},{192,0},{224,... | collective-permute-start | bytes 3145736 | tf_op jit(solution)/shard_map/ppermute | solution.py:283
  2.3 24.8 %collective-permute-start.1 = (bf16[2,512,512]{2,1,0:T(8,128)(2,1)}, bf16[2,512,512]{2,1,0:T(8,128)(2,1)S(1)}, u32[]{:S(2)}, u32[]{:S(2)}) collective-permute-start(bf16[2,512,512]{2,1,0:T(8,128)(2,1)} %refs_0_.1), channel_id=1, source_target_pairs={{0,192},{32,224},{64,0},{96,32},{128,64},{160,96},{192,128},{224,1... | collective-permute-start | bytes 3145736 | tf_op jit(solution)/shard_map/ppermute | solution.py:283
  3.0 24.1 %collective-permute-start.2 = (bf16[2,512,512]{2,1,0:T(8,128)(2,1)}, bf16[2,512,512]{2,1,0:T(8,128)(2,1)S(1)}, u32[]{:S(2)}, u32[]{:S(2)}) collective-permute-start(bf16[2,512,512]{2,1,0:T(8,128)(2,1)} %refs_0_.1), channel_id=1, source_target_pairs={{0,32},{32,0},{64,96},{96,64},{128,160},{160,128},{192,224},{224,1... | collective-permute-start | bytes 3145736 | tf_op jit(solution)/shard_map/ppermute | solution.py:288
  3.9 1.0 copy-start.1
  6.4 40.4 %all-to-all-start = ((bf16[32,2,16,512]{3,2,1,0:T(8,128)(2,1)}), bf16[32,2,16,512]{3,2,1,0:T(8,128)(2,1)}, u32[]{:S(2)}, u32[]{:S(2)}) async-start(bf16[32,2,16,512]{3,2,1,0:T(8,128)(2,1)} %pick_rows.1), calls=%async_computation | async-start | bytes 2097152 | tf_op jit(solution)/shard_map/all_to_all | solution.py:296
  17.6 13.0 %copy-start.9 = (s32[256,16]{0,1:T(8,128)S(1)}, s32[256,16]{0,1:T(8,128)}, u32[]{:S(2)}) copy-start(s32[256,16]{0,1:T(8,128)} %param.16) | copy-start | bytes 49156
  25.8 7.4 %copy-start.7 = (bf16[2,512,512]{2,1,0:T(8,128)(2,1)}, bf16[2,512,512]{2,1,0:T(8,128)(2,1)S(1)}, u32[]{:S(2)}) copy-start(bf16[2,512,512]{2,1,0:T(8,128)(2,1)S(1)} %collective-permute-done.refs_6_) | copy-start | bytes 3145732
  27.1 6.1 %copy-start.8 = (bf16[2,512,512]{2,1,0:T(8,128)(2,1)}, bf16[2,512,512]{2,1,0:T(8,128)(2,1)S(1)}, u32[]{:S(2)}) copy-start(bf16[2,512,512]{2,1,0:T(8,128)(2,1)S(1)} %collective-permute-done.1.refs_2_) | copy-start | bytes 3145732
  27.1 6.1 %copy-start.10 = (bf16[2,512,512]{2,1,0:T(8,128)(2,1)}, bf16[2,512,512]{2,1,0:T(8,128)(2,1)S(1)}, u32[]{:S(2)}) copy-start(bf16[2,512,512]{2,1,0:T(8,128)(2,1)S(1)} %collective-permute-done.2.refs_1_) | copy-start | bytes 3145732
  28.4 22.0 %collective-permute-start.3 = (bf16[2,512,512]{2,1,0:T(8,128)(2,1)}, bf16[2,512,512]{2,1,0:T(8,128)(2,1)}, u32[]{:S(2)}, u32[]{:S(2)}) collective-permute-start(bf16[2,512,512]{2,1,0:T(8,128)(2,1)} %broadcast_select_fusion), channel_id=1, source_target_pairs={{0,64},{32,224},{64,128},{96,32},{128,192},{160,96},{192,0},{224,1... | collective-permute-start | bytes 3145736 | tf_op jit(solution)/shard_map/ppermute | solution.py:283
  29.7 20.7 %collective-permute-start.4 = (bf16[2,512,512]{2,1,0:T(8,128)(2,1)S(1)}, bf16[2,512,512]{2,1,0:T(8,128)(2,1)}, u32[]{:S(2)}, u32[]{:S(2)}) collective-permute-start(bf16[2,512,512]{2,1,0:T(8,128)(2,1)S(1)} %collective-permute-done.1.refs_2_), channel_id=1, source_target_pairs={{0,32},{32,0},{64,96},{96,64},{128,160},{160,128},{192,224},{224,1... | collective-permute-start | bytes 3145736 | tf_op jit(solution)/shard_map/ppermute | solution.py:288
  29.7 20.7 %collective-permute-start.5 = (bf16[2,512,512]{2,1,0:T(8,128)(2,1)S(1)}, bf16[2,512,512]{2,1,0:T(8,128)(2,1)}, u32[]{:S(2)}, u32[]{:S(2)}) collective-permute-start(bf16[2,512,512]{2,1,0:T(8,128)(2,1)S(1)} %collective-permute-done.refs_6_), channel_id=1, source_target_pairs={{0,32},{32,0},{64,96},{96,64},{128,160},{160,128},{192,224},{224,1... | collective-permute-start | bytes 3145736 | tf_op jit(solution)/shard_map/ppermute | solution.py:288
  33.3 0.8 copy-start.6
  46.8 17.7 %copy-start.2 = (bf16[256,512]{1,0:T(8,128)(2,1)S(1)}, bf16[256,512]{1,0:T(8,128)(2,1)}, u32[]{:S(2)}) copy-start(bf16[256,512]{1,0:T(8,128)(2,1)} %features_hbm.1) | copy-start | bytes 786436
  46.8 17.7 %copy-start.3 = (bf16[256,512]{1,0:T(8,128)(2,1)S(1)}, bf16[256,512]{1,0:T(8,128)(2,1)}, u32[]{:S(2)}) copy-start(bf16[256,512]{1,0:T(8,128)(2,1)} %cotangent_hbm.1) | copy-start | bytes 786436
  50.4 14.1 %collective-permute-start.6 = (bf16[2,512,512]{2,1,0:T(8,128)(2,1)}, bf16[2,512,512]{2,1,0:T(8,128)(2,1)}, u32[]{:S(2)}, u32[]{:S(2)}) collective-permute-start(bf16[2,512,512]{2,1,0:T(8,128)(2,1)} %collective-permute-done.3.refs_4_), channel_id=1, source_target_pairs={{0,32},{32,0},{64,96},{96,64},{128,160},{160,128},{192,224},{224,1... | collective-permute-start | bytes 3145736 | tf_op jit(solution)/shard_map/ppermute | solution.py:288
  50.5 14.0 %all-to-all-start.1 = ((bf16[8,64,512]{2,1,0:T(8,128)(2,1)}), bf16[8,64,512]{2,1,0:T(8,128)(2,1)S(1)}, u32[]{:S(2)}, u32[]{:S(2)}) async-start(bf16[8,64,512]{2,1,0:T(8,128)(2,1)} %get-tuple-element.24), calls=%async_computation.1 | async-start | bytes 1048576 | tf_op jit(solution)/shard_map/all_to_all | solution.py:296
  55.6 19.9 %collective-permute-start.7 = (bf16[2,256,256]{2,1,0:T(8,128)(2,1)}, bf16[2,256,256]{2,1,0:T(8,128)(2,1)S(1)}, u32[]{:S(2)}, u32[]{:S(2)}) collective-permute-start(bf16[2,256,256]{2,1,0:T(8,128)(2,1)} %get-tuple-element.29.mean0), channel_id=1, source_target_pairs={{0,8},{8,0},{16,24},{24,16},{1,9},{9,1},{17,25},{25,17},{2,10},{10... | collective-permute-start | bytes 786440 | tf_op jit(solution)/shard_map/ppermute | solution.py:292
  55.6 20.0 %collective-permute-start.8 = (bf16[2,256,256]{2,1,0:T(8,128)(2,1)}, bf16[2,256,256]{2,1,0:T(8,128)(2,1)S(1)}, u32[]{:S(2)}, u32[]{:S(2)}) collective-permute-start(bf16[2,256,256]{2,1,0:T(8,128)(2,1)} %get-tuple-element.34), channel_id=1, source_target_pairs={{0,16},{8,24},{16,0},{24,8},{1,17},{9,25},{17,1},{25,9},{2,18},{10... | collective-permute-start | bytes 786440 | tf_op jit(solution)/shard_map/ppermute | solution.py:292
  57.9 17.7 %collective-permute-start.9 = (bf16[2,256,256]{2,1,0:T(8,128)(2,1)}, bf16[2,256,256]{2,1,0:T(8,128)(2,1)S(1)}, u32[]{:S(2)}, u32[]{:S(2)}) collective-permute-start(bf16[2,256,256]{2,1,0:T(8,128)(2,1)} %get-tuple-element.34), channel_id=1, source_target_pairs={{0,24},{8,16},{16,8},{24,0},{1,25},{9,17},{17,9},{25,1},{2,26},{10... | collective-permute-start | bytes 786440 | tf_op jit(solution)/shard_map/ppermute | solution.py:292
  75.6 32.7 %copy-start.4 = (bf16[2,256,256]{2,1,0:T(8,128)(2,1)S(1)}, bf16[2,256,256]{2,1,0:T(8,128)(2,1)}, u32[]{:S(2)}) copy-start(bf16[2,256,256]{2,1,0:T(8,128)(2,1)} %get-tuple-element.29.mean0) | copy-start | bytes 786436
  75.6 32.6 %all-to-all-start.2 = ((bf16[32,2,2,32,256]{4,3,2,1,0:T(8,128)(2,1)}), bf16[32,2,2,32,256]{4,3,2,1,0:T(8,128)(2,1)S(1)}, u32[]{:S(2)}, u32[]{:S(2)}) async-start(bf16[32,2,2,32,256]{4,3,2,1,0:T(8,128)(2,1)} %all_layers.1), calls=%async_computation.2 | async-start | bytes 4194304 | tf_op jit(solution)/shard_map/all_to_all | solution.py:296
  109.9 0.7 copy-start.5
  110.6 19.1 %all-to-all-start.3 = ((bf16[16,2,2,16,256]{4,3,2,1,0:T(8,128)(2,1)}), bf16[16,2,2,16,256]{4,3,2,1,0:T(8,128)(2,1)S(1)}, u32[]{:S(2)}, u32[]{:S(2)}) async-start(bf16[16,2,2,16,256]{4,3,2,1,0:T(8,128)(2,1)} %get-tuple-element.39), calls=%async_computation.3 | async-start | bytes 1048576 | tf_op jit(solution)/shard_map/all_to_all | solution.py:296
  114.4 13.4 %collective-permute-start.10 = (bf16[8,2,32,256]{3,2,1,0:T(8,128)(2,1)}, bf16[8,2,32,256]{3,2,1,0:T(8,128)(2,1)S(1)}, u32[]{:S(2)}, u32[]{:S(2)}) collective-permute-start(bf16[8,2,32,256]{3,2,1,0:T(8,128)(2,1)} %copy-done.5), channel_id=1, source_target_pairs={{0,16},{8,24},{16,0},{24,8},{1,17},{9,25},{17,1},{25,9},{2,18},{10... | collective-permute-start | bytes 786440 | tf_op jit(solution)/shard_map/ppermute | solution.py:292
